TPU v7x, 32 devices: a whole 2x2x4 slice. The times are simulated.
32 devices in a mesh: adapter: 8 (over z, core), tensor: 4 (over y, x).
Axes of the slice: x: 2, y: 2, z: 4, core: 2. Of those that a mesh axis runs over, the one named last changes fastest.
Arguments:
- attn_output: bfloat16 [2048, 8192], P('adapter', 'tensor'), may hold values from -6 to 6
- output_grad: bfloat16 [2048, 8192], P(('adapter', 'tensor')), may hold values from -6 to 6
- adapter_ids: int32 [2048], P('adapter'), may hold values from 0 to 255, as said below
- base_weight: bfloat16 [8192, 8192], P('tensor', 'adapter'), may hold values from -0.0625 to 0.0625
- adapter_down: bfloat16 [8192, 4096], P('tensor', 'adapter'), may hold values from -0.1796875 to 0.1796875
- adapter_up: bfloat16 [4096, 8192], P('adapter', 'tensor'), may hold values from -0.0625 to 0.0625
Outputs:
- attention_output_gradient: bfloat16 [2048, 8192], P('adapter', 'tensor')
- down_grad: float32 [8192, 4096], P('tensor', 'adapter')
- up_grad: float32 [4096, 8192], P('adapter', 'tensor')
Inputs may be any that keep to these rules, and one draw needn't show every extreme that they name: `adapter_ids`: the 256 tokens of each index of adapter form one block; the owner of adapter a is a // 32. At most 80 tokens of a block have adapters of one owner, and one owner, drawn from the seed, gets exactly 80 tokens of every block.
All inputs are finite; a program needn't handle non-finite values.
Results may differ from a plain program's by a relative error of at most 0.007.
Values may be sent and summed in bfloat16 or wider, within the bound.
No kernel may reach another device: no remote copies, remote signals or barrier semaphores. Data moves between devices by JAX's collectives and lax.ppermute only.
A program may use at most 128 MiB of HBM per device.

v0:
```python
import jax
import jax.numpy as jnp
from jax import lax
from jax.sharding import PartitionSpec as P

ADAPTER_RANK = 16


ADAPTER_SCALE = 2.0


def per_device(attn_output, output_grad, adapter_ids, base_weight, adapter_down, adapter_up):
    owners = lax.axis_size("adapter")
    tok_rows, width_part = attn_output.shape
    capacity = 5 * tok_rows // (2 * owners)
    adapter_slot_count = owners * capacity
    per_owner = adapter_down.shape[1] // ADAPTER_RANK
    full_grad = lax.all_gather(output_grad, "tensor", axis=0, tiled=True)
    start_col = lax.axis_index("tensor") * width_part
    grad_part = lax.dynamic_slice_in_dim(full_grad, start_col, width_part, 1)
    frozen_gradient = lax.dot_general(
        full_grad,
        lax.all_gather(base_weight, "adapter", axis=1, tiled=True),
        (((1,), (1,)), ((), ())),
        preferred_element_type=jnp.float32,
    )
    owner_of = adapter_ids // per_owner
    local_of = adapter_ids % per_owner
    onehot_own = (owner_of[:, None] == jnp.arange(owners, dtype=jnp.int32)[None, :]).astype(
        jnp.int32
    )
    before = jnp.cumsum(onehot_own, axis=0) - onehot_own
    rank_in = jnp.sum(before * onehot_own, axis=1)
    token_slot_index = owner_of * capacity + rank_in
    source_row = (
        jnp.full((adapter_slot_count,), tok_rows, jnp.int32)
        .at[token_slot_index]
        .set(jnp.arange(tok_rows, dtype=jnp.int32))
    )
    send_inputs = jnp.concatenate([attn_output, jnp.zeros((1, width_part), jnp.bfloat16)], axis=0)[
        source_row
    ]
    send_grads = jnp.concatenate([grad_part, jnp.zeros((1, width_part), jnp.bfloat16)], axis=0)[
        source_row
    ]
    send_labels = jnp.concatenate(
        [local_of.astype(jnp.bfloat16), jnp.full((1,), -1.0, jnp.bfloat16)]
    )[source_row]
    recv_inputs, recv_grads, recv_labels = (
        lax.all_to_all(send_inputs, "adapter", split_axis=0, concat_axis=0, tiled=True),
        lax.all_to_all(send_grads, "adapter", split_axis=0, concat_axis=0, tiled=True),
        lax.all_to_all(send_labels, "adapter", split_axis=0, concat_axis=0, tiled=True),
    )
    chosen = (
        recv_labels.astype(jnp.float32)[:, None]
        == jnp.arange(per_owner, dtype=jnp.float32)[None, :]
    ).astype(jnp.float32)
    spread = jnp.repeat(chosen, ADAPTER_RANK, axis=1)
    proj_inputs = jnp.dot(recv_inputs, adapter_down, preferred_element_type=jnp.float32)
    proj_grads = lax.dot_general(
        recv_grads, adapter_up, (((1,), (1,)), ((), ())), preferred_element_type=jnp.float32
    )
    rank_inputs = (
        (proj_inputs * spread)
        .reshape(adapter_slot_count, per_owner, ADAPTER_RANK)
        .sum(axis=1)
        .reshape(-1)
    )
    rank_gradients = (
        (proj_grads * spread)
        .reshape(adapter_slot_count, per_owner, ADAPTER_RANK)
        .sum(axis=1)
        .reshape(-1)
    )
    rank_inputs, rank_gradients = lax.psum((rank_inputs, rank_gradients), "tensor")
    scaled_up_weight = (
        ADAPTER_SCALE * rank_inputs.reshape(adapter_slot_count, ADAPTER_RANK)
    ).astype(jnp.bfloat16)
    rank_gradient = (
        ADAPTER_SCALE * rank_gradients.reshape(adapter_slot_count, ADAPTER_RANK)
    ).astype(jnp.bfloat16)
    spread_half = spread.astype(jnp.bfloat16)
    wide_gradient = jnp.tile(rank_gradient, (1, per_owner)) * spread_half
    up_wide = jnp.tile(scaled_up_weight, (1, per_owner)) * spread_half
    down_grad = lax.dot_general(
        recv_inputs, wide_gradient, (((0,), (0,)), ((), ())), preferred_element_type=jnp.float32
    )
    up_grad = lax.dot_general(
        up_wide, recv_grads, (((0,), (0,)), ((), ())), preferred_element_type=jnp.float32
    )
    adapter_block = lax.dot_general(
        wide_gradient, adapter_down, (((1,), (1,)), ((), ())), preferred_element_type=jnp.float32
    ).astype(jnp.bfloat16)
    returned_gradient = lax.all_to_all(
        adapter_block, "adapter", split_axis=0, concat_axis=0, tiled=True
    )
    adapter_contribution = returned_gradient[token_slot_index]
    attention_output_gradient = (frozen_gradient + adapter_contribution.astype(jnp.float32)).astype(
        jnp.bfloat16
    )
    return (attention_output_gradient, down_grad, up_grad)


def solution(mesh):
    placed = (
        P("adapter", "tensor"),
        P(("adapter", "tensor"), None),
        P("adapter"),
        P("tensor", "adapter"),
        P("tensor", "adapter"),
        P("adapter", "tensor"),
    )
    return jax.shard_map(
        per_device,
        mesh=mesh,
        in_specs=placed,
        out_specs=(P("adapter", "tensor"), P("tensor", "adapter"), P("adapter", "tensor")),
        check_vma=False,
    )
```

profile of v0, /device:TPU:0, one launch (start us, length us, event | category | flops | bytes accessed | tf_op | source)
XLA Modules:
  0.0 535.6 jit_solution(7233100301469261890)
XLA Ops:
  8.0 0.0 copy-start
  8.0 0.0 all-gather.3.cloned.1.call-start
  8.1 0.7 all-gather.3.cloned.1.call-update
  8.7 0.7 and_select_fusion.1
  9.4 0.6 reduce-window.6
  10.0 0.2 slice_reduce_fusion
  10.3 0.1 fusion.5
  10.4 1.4 scatter_custom_fusion
  11.9 4.3 gather_fusion.1
  16.2 0.7 all_to_all.41
  16.8 6.3 %all-to-all-start.1 = ((bf16[8,80,1]{1,2,0:T(2,128)(2,1)}), bf16[8,80,1]{1,2,0:T(2,128)(2,1)S(1)}, u32[]{:S(2)}, u32[]{:S(2)}) async-start(bf16[8,80,1]{1,2,0:T(2,128)(2,1)} %all_to_all.41), calls=%async_computation.1 | async-start | bytes 8192 | tf_op jit(solution)/shard_map/all_to_all | solution.py:52
  23.2 1.3 concatenate.11
  24.5 4.1 gather_fusion.3
  28.5 0.1 all-to-all-done.1
  28.7 5.0 all-to-all-start.3
  33.6 32.5 %all-gather.3.cloned.1.call-done = bf16[256,8192]{1,0:T(8,128)(2,1)} async-done(((bf16[64,8192]{1,0:T(8,128)(2,1)}), bf16[256,8192]{1,0:T(8,128)(2,1)}) %all-gather.3.cloned.1.call-update) | async-done | bytes 4194320 | tf_op jit(solution)/shard_map/all_gather | solution.py:18
  66.1 1.3 constant_dynamic-slice_fusion
  67.5 0.1 concatenate.9
  67.5 4.1 gather_fusion
  71.6 22.4 %all-to-all-done.3 = bf16[8,80,2048]{2,1,0:T(8,128)(2,1)} async-done(((bf16[8,80,2048]{2,1,0:T(8,128)(2,1)}), bf16[8,80,2048]{2,1,0:T(8,128)(2,1)}, u32[]{:S(2)}, u32[]{:S(2)}) %all-to-all-start.3) | async-done | bytes 2621472 | tf_op jit(solution)/shard_map/all_to_all | solution.py:50
  94.1 4.4 all-to-all-start
  98.5 0.0 all-reduce.5.cloned.1.call-start
  98.5 0.1 reshape.108
  98.6 0.0 copy-done
  98.6 3.6 bitcast_multiply_fusion
  102.2 0.7 reduce_sum.29
  102.9 0.9 copy.14
  103.9 0.8 reshape.107
  104.6 54.1 %all-to-all-done = bf16[8,80,2048]{2,1,0:T(8,128)(2,1)} async-done(((bf16[8,80,2048]{2,1,0:T(8,128)(2,1)}), bf16[8,80,2048]{2,1,0:T(8,128)(2,1)}, u32[]{:S(2)}, u32[]{:S(2)}) %all-to-all-start) | async-done | bytes 2621472 | tf_op jit(solution)/shard_map/all_to_all | solution.py:51
  158.8 4.2 bitcast_multiply_fusion.1
  163.0 0.7 reduce_sum.28
  163.7 0.9 copy.12
  164.6 0.8 reshape.105
  165.4 0.0 all-reduce.5.cloned.1.call-update
  165.4 0.0 all-gather.5.cloned.1.call-start
  165.5 0.5 all-gather.5.cloned.1.call-update
  166.0 39.7 %all-reduce.5.cloned.1.call-done = (f32[10240]{0:T(1024)}, f32[10240]{0:T(1024)}) async-done(((f32[10240]{0:T(1024)}, f32[10240]{0:T(1024)}), (f32[10240]{0:T(1024)}, f32[10240]{0:T(1024)})) %all-reduce.5.cloned.1.call-update) | async-done | bytes 81936 | tf_op jit(solution)/shard_map/psum | solution.py:75
  205.7 0.8 multiply_convert_fusion
  206.5 0.1 convert_element_type.68
  206.6 0.1 copy.13
  206.7 0.1 fusion.1
  206.9 3.0 convolution_convert_fusion
  209.9 4.6 all-to-all-start.2
  214.5 0.1 convert_element_type.75
  214.7 0.1 copy.15
  214.8 0.2 broadcast_multiply_fusion
  215.0 5.7 %fusion.11 = f32[512,2048]{1,0:T(8,128)} fusion(bf16[640,512]{0,1:T(8,128)(2,1)S(1)} %bitcast.46, bf16[640,2048]{1,0:T(8,128)(2,1)} %bitcast.4), kind=kOutput, calls=%fused_computation.44 | convolution fusion | flops 1342177280 | bytes 7471104 | tf_op jit(solution)/shard_map/dot_general | solution.py:88
  220.7 5.6 %fusion.10 = f32[2048,512]{1,0:T(8,128)} fusion(bf16[640,2048]{1,0:T(8,128)(2,1)} %bitcast.11, bf16[640,512]{0,1:T(8,128)(2,1)S(1)} %bitcast.45), kind=kOutput, calls=%fused_computation.43 | convolution fusion | flops 1342177280 | bytes 7471104 | tf_op jit(solution)/shard_map/dot_general | solution.py:85
  226.3 110.7 %all-to-all-done.2 = bf16[8,80,2048]{2,1,0:T(8,128)(2,1)S(1)} async-done(((bf16[8,80,2048]{2,1,0:T(8,128)(2,1)}), bf16[8,80,2048]{2,1,0:T(8,128)(2,1)S(1)}, u32[]{:S(2)}, u32[]{:S(2)}) %all-to-all-start.2) | async-done | bytes 2621472 | tf_op jit(solution)/shard_map/all_to_all | solution.py:94
  337.0 2.3 gather_fusion.2
  339.4 171.6 %all-gather.5.cloned.1.call-done = bf16[2048,8192]{1,0:T(8,128)(2,1)} async-done(((bf16[2048,1024]{1,0:T(8,128)(2,1)}), bf16[2048,8192]{1,0:T(8,128)(2,1)}) %all-gather.5.cloned.1.call-update) | async-done | bytes 33554448 | tf_op jit(solution)/shard_map/all_gather | solution.py:23
  510.9 0.0 copy-start.1
  510.9 17.2 %fusion = bf16[256,2048]{1,0:T(8,128)(2,1)} fusion(bf16[256,8192]{1,0:T(8,128)(2,1)} %all-gather.3.cloned.1.call-done, bf16[2048,8192]{1,0:T(8,128)(2,1)} %all-gather.5.cloned.1.call-done, bf16[256,2048]{1,0:T(8,128)(2,1)} %gather_fusion.2), kind=kOutput, calls=%fused_computation.10 | convolution fusion | flops 8591507456 | bytes 39845888 | tf_op jit(solution)/shard_map/dot_general | solution.py:21
  528.1 0.0 copy-done.1
  (11 shorter events, 0.1 us)
Async XLA Ops:
  8.0 90.6 %copy-start = (bf16[2048,512]{1,0:T(8,128)(2,1)S(1)}, bf16[2048,512]{1,0:T(8,128)(2,1)}, u32[]{:S(2)}) copy-start(bf16[2048,512]{1,0:T(8,128)(2,1)} %param.10) | copy-start | bytes 6291460
  8.0 58.1 %all-gather.3.cloned.1.call-start = ((), (), s32[]{:S(2)}) async-start(), calls=%async_computation.4 | async-start | bytes 5242880 | tf_op jit(solution)/shard_map/all_gather | solution.py:18
  16.8 11.8 %all-to-all-start.1 = ((bf16[8,80,1]{1,2,0:T(2,128)(2,1)}), bf16[8,80,1]{1,2,0:T(2,128)(2,1)S(1)}, u32[]{:S(2)}, u32[]{:S(2)}) async-start(bf16[8,80,1]{1,2,0:T(2,128)(2,1)} %all_to_all.41), calls=%async_computation.1 | async-start | bytes 8192 | tf_op jit(solution)/shard_map/all_to_all | solution.py:52
  28.7 65.4 %all-to-all-start.3 = ((bf16[8,80,2048]{2,1,0:T(8,128)(2,1)}), bf16[8,80,2048]{2,1,0:T(8,128)(2,1)}, u32[]{:S(2)}, u32[]{:S(2)}) async-start(bf16[8,80,2048]{2,1,0:T(8,128)(2,1)} %bitcast.40), calls=%async_computation.3 | async-start | bytes 5242880 | tf_op jit(solution)/shard_map/all_to_all | solution.py:50
  94.1 64.7 %all-to-all-start = ((bf16[8,80,2048]{2,1,0:T(8,128)(2,1)}), bf16[8,80,2048]{2,1,0:T(8,128)(2,1)}, u32[]{:S(2)}, u32[]{:S(2)}) async-start(bf16[8,80,2048]{2,1,0:T(8,128)(2,1)} %bitcast.41), calls=%async_computation | async-start | bytes 5242880 | tf_op jit(solution)/shard_map/all_to_all | solution.py:51
  98.5 107.2 %all-reduce.5.cloned.1.call-start = ((), (), s32[]{:S(2)}) async-start(), calls=%async_computation.6 | async-start | bytes 163840 | tf_op jit(solution)/shard_map/psum | solution.py:75
  165.4 345.5 %all-gather.5.cloned.1.call-start = ((), (), s32[]{:S(2)}) async-start(), calls=%async_computation.5 | async-start | bytes 37748736 | tf_op jit(solution)/shard_map/all_gather | solution.py:23
  209.9 127.1 %all-to-all-start.2 = ((bf16[8,80,2048]{2,1,0:T(8,128)(2,1)}), bf16[8,80,2048]{2,1,0:T(8,128)(2,1)S(1)}, u32[]{:S(2)}, u32[]{:S(2)}) async-start(bf16[8,80,2048]{2,1,0:T(8,128)(2,1)} %bitcast.44), calls=%async_computation.2 | async-start | bytes 5242880 | tf_op jit(solution)/shard_map/all_to_all | solution.py:94
  510.9 17.2 %copy-start.1 = (bf16[2048,512]{1,0:T(8,128)(2,1)S(1)}, bf16[2048,512]{1,0:T(8,128)(2,1)}, u32[]{:S(2)}) copy-start(bf16[2048,512]{1,0:T(8,128)(2,1)} %param.10) | copy-start | bytes 6291460
Sparse Core Ops, SparseCore 0:
  10.7 55.3 all-gather.2
  165.5 40.1 all-reduce.4
Sparse Core Ops, SparseCore 1:
  167.5 343.4 all-gather.4
where the time goes:
time: 536 us
  waiting for transfers between devices  432 us (81%)
  matrix products  39.4 us (7%)
  local copies, waits for them, and re-layouts  23.8 us (4%)
  starting transfers between devices  20.4 us (4%)
  between operations  15.7 us (3%)
    all_gather x1, waiting for transfers between devices, per_device(): lax.all_gather(base_weight, 'adapter', axis=1, tiled=True)  172 us
    all_to_all x1, waiting for transfers between devices, per_device(): lax.all_to_all(adapter_block, 'adapter', split_axis=0, concat_axis=0, til...  111 us
    all_to_all x1, waiting for transfers between devices, per_device(): lax.all_to_all(send_grads, 'adapter', split_axis=0, concat_axis=0, tiled=...  54.1 us
    psum x1, waiting for transfers between devices, per_device(): lax.psum((rank_inputs, rank_gradients), 'tensor')  39.7 us
    all_gather x1, waiting for transfers between devices, per_device(): full_grad = lax.all_gather(output_grad, 'tensor', axis=0, tiled=True)  32.5 us
    all_to_all x1, waiting for transfers between devices, per_device(): lax.all_to_all(send_inputs, 'adapter', split_axis=0, concat_axis=0, tiled...  22.4 us
    dot_general x1, matrix products, per_device(): lax.dot_general(full_grad, lax.all_gather(base_weight, 'adapter', axis=1,...  17.2 us
  transfers between devices with their start and end apart: 7, of which 7 were waited for; matrix products, arithmetic and copies ran while one was open for 8% of the time, Pallas kernels for 0%

commit v1 on v0

v1 whole, which is shorter than its diff:
```python
import jax
import jax.numpy as jnp
from jax import lax
from jax.sharding import PartitionSpec as P

ADAPTER_RANK = 16
ADAPTER_SCALE = 2.0
F32 = jnp.float32
BF16 = jnp.bfloat16


def per_device(attn, grad, ids, weight, down, up):
    owners = lax.axis_size("adapter")
    tensors = lax.axis_size("tensor")
    planes = owners // 2
    half_ring = planes // 2
    me = lax.axis_index("adapter")
    plane, core = me // 2, me % 2
    tensor = lax.axis_index("tensor")
    tokens, width = attn.shape
    sub = grad.shape[0]
    out_cols = weight.shape[1]
    rank_cols = down.shape[1]
    per_owner = rank_cols // ADAPTER_RANK

    up_pairs = [(2 * z + c, 2 * ((z + 1) % planes) + c) for z in range(planes) for c in range(2)]
    down_pairs = [(dst, src) for src, dst in up_pairs]
    core_pairs = [(a, a ^ 1) for a in range(owners)]

    def send_up(x):
        return lax.ppermute(x, "adapter", up_pairs)

    def send_down(x):
        return lax.ppermute(x, "adapter", down_pairs)

    def swap(x):
        return lax.ppermute(x, "adapter", core_pairs)

    def flip(x, bit):
        return lax.ppermute(x, "tensor", [(t, t ^ bit) for t in range(tensors)])

    bits = [1 << i for i in range(tensors.bit_length() - 1)]

    def after(x, *others):
        return lax.optimization_barrier((x, *others))[0]

    def plane_cols(offset, which):
        p = (plane + offset) % planes
        start = (2 * p + (core if which == 0 else 1 - core)) * out_cols
        return lax.dynamic_slice_in_dim(grad, start, out_cols, 1)

    going_up = [plane_cols(s, w) for s in range(1, half_ring) for w in range(2)] + [plane_cols(half_ring, 0)]
    going_down = [plane_cols(-s, w) for s in range(1, half_ring) for w in range(2)] + [plane_cols(half_ring, 1)]
    going_up = jnp.concatenate(going_up, axis=1)
    going_down = jnp.concatenate(going_down, axis=1)
    part = [None] * planes
    part[0] = jnp.concatenate([plane_cols(0, 0), plane_cols(0, 1)], axis=1)
    for s in range(1, half_ring + 1):
        going_up = send_up(going_up)
        going_down = send_down(going_down)
        if s < half_ring:
            part[s] = going_up[:, : 2 * out_cols]
            part[planes - s] = going_down[:, : 2 * out_cols]
            going_up = going_up[:, 2 * out_cols :]
            going_down = going_down[:, 2 * out_cols :]
        else:
            part[s] = jnp.concatenate([going_up, going_down], axis=1)

    grad_cols = lax.all_to_all(grad, "tensor", split_axis=1, concat_axis=0, tiled=True)
    other_weight = swap(weight)
    other_down = swap(down)
    all_ids = lax.all_gather(ids, "adapter", axis=0, tiled=False)

    stacked = jnp.stack(part, axis=0)
    first, second = stacked[:, : sub // 2], stacked[:, sub // 2 :]
    first, second = first[None], second[None]
    first_order, second_order = [0], [0]
    for low, high in zip(bits, reversed(bits)):
        first = jnp.concatenate([first, flip(first, low)], axis=0)
        first_order = first_order + [k ^ low for k in first_order]
        second = jnp.concatenate([second, flip(second, high)], axis=0)
        second_order = second_order + [k ^ high for k in second_order]

    def ring_gather(x, gate):
        if gate is not None:
            x = after(x, gate)
        blocks = [None] * planes
        blocks[0] = x
        above, below = x, x
        for s in range(1, half_ring):
            above, below = send_up(above), send_down(below)
            blocks[s], blocks[planes - s] = above, below
        above = send_up(above[: tokens // 2])
        below = send_down(below[tokens // 2 :])
        blocks[half_ring] = jnp.concatenate([above, below], axis=0)
        return blocks + [swap(b) for b in blocks]

    grad_blocks = ring_gather(grad_cols, part[half_ring])
    attn_blocks = ring_gather(attn, grad_blocks[half_ring])

    block_ids = [all_ids[2 * ((plane - d) % planes) + core] for d in range(planes)]
    block_ids += [all_ids[2 * ((plane - d) % planes) + 1 - core] for d in range(planes)]
    block_ids = jnp.concatenate(block_ids)
    own_mask = block_ids[None, :] == (me * per_owner + jnp.arange(per_owner, dtype=jnp.int32))[:, None]
    other_mask = block_ids[None, :] == ((me ^ 1) * per_owner + jnp.arange(per_owner, dtype=jnp.int32))[:, None]

    def ranks_of(projected):
        chosen = projected.reshape(per_owner, ADAPTER_RANK, -1)
        return jnp.sum(jnp.where(own_mask[:, None, :], chosen, 0.0), axis=0)

    def widen(ranks, mask):
        wide = jnp.where(mask[:, None, :], ranks[None], jnp.zeros((), BF16))
        return wide.reshape(rank_cols, -1)

    grads_all = jnp.concatenate(grad_blocks, axis=0)
    low_grads = ranks_of(
        lax.dot_general(up, grads_all, (((1,), (1,)), ((), ())), preferred_element_type=F32)
    )
    low_grads = low_grads + jnp.roll(swap(low_grads), planes * tokens, axis=1)
    for bit in bits:
        low_grads = low_grads + flip(low_grads, bit)
    grad_low = (ADAPTER_SCALE * low_grads).astype(BF16)
    wide_gradient = widen(grad_low, own_mask)
    other_gradient = widen(grad_low, other_mask)

    def partial_sum(d):
        gathered = jnp.zeros((tensors, sub, 2 * out_cols), BF16)
        gathered = jnp.concatenate(
            [
                jnp.stack([first[first_order.index(k), d] for k in range(tensors)]),
                jnp.stack([second[second_order.index(k), d] for k in range(tensors)]),
            ],
            axis=1,
        )
        natural = [
            lax.dynamic_index_in_dim(gathered, tensor ^ k, 0, keepdims=False) for k in range(tensors)
        ]
        rows = jnp.concatenate(natural, axis=0)
        here = slice(d * tokens, (d + 1) * tokens)
        return (
            lax.dot_general(rows[:, :out_cols], weight, (((1,), (1,)), ((), ())), preferred_element_type=F32)
            + lax.dot_general(rows[:, out_cols:], other_weight, (((1,), (1,)), ((), ())), preferred_element_type=F32)
            + lax.dot_general(wide_gradient[:, here], down, (((0,), (1,)), ((), ())), preferred_element_type=F32)
            + lax.dot_general(other_gradient[:, here], other_down, (((0,), (1,)), ((), ())), preferred_element_type=F32)
        )

    far = partial_sum(half_ring).astype(BF16)
    back_down, back_up = far[: tokens // 2], far[tokens // 2 :]
    back_down, back_up = send_down(back_down), send_up(back_up)
    for s in range(half_ring - 1, 0, -1):
        mine_down, mine_up = partial_sum(s), partial_sum(planes - s)
        if s == half_ring - 1:
            mine_down = jnp.concatenate(
                [mine_down[: tokens // 2] + back_down.astype(F32), mine_down[tokens // 2 :]], axis=0
            )
            mine_up = jnp.concatenate(
                [mine_up[: tokens // 2], mine_up[tokens // 2 :] + back_up.astype(F32)], axis=0
            )
        else:
            mine_down = mine_down + back_down.astype(F32)
            mine_up = mine_up + back_up.astype(F32)
        back_down, back_up = send_down(mine_down.astype(BF16)), send_up(mine_up.astype(BF16))
    own = partial_sum(0)
    if half_ring > 1:
        total = own + back_down.astype(F32) + back_up.astype(F32)
    else:
        total = own + jnp.concatenate([back_down, back_up], axis=0).astype(F32)
    attention_output_gradient = total.astype(BF16)

    attn_all = jnp.concatenate(attn_blocks, axis=0)
    low_inputs = ranks_of(
        lax.dot_general(down, attn_all, (((0,), (1,)), ((), ())), preferred_element_type=F32)
    )
    for bit in bits:
        low_inputs = low_inputs + flip(low_inputs, bit)
    up_wide = widen((ADAPTER_SCALE * low_inputs).astype(BF16), own_mask)
    down_grad = lax.dot_general(
        attn_all, wide_gradient, (((0,), (1,)), ((), ())), preferred_element_type=F32
    )
    up_grad = jnp.dot(up_wide, grads_all, preferred_element_type=F32)
    return attention_output_gradient, down_grad, up_grad


def solution(mesh):
    placed = (
        P("adapter", "tensor"),
        P(("adapter", "tensor"), None),
        P("adapter"),
        P("tensor", "adapter"),
        P("tensor", "adapter"),
        P("adapter", "tensor"),
    )
    return jax.shard_map(
        per_device,
        mesh=mesh,
        in_specs=placed,
        out_specs=(P("adapter", "tensor"), P("tensor", "adapter"), P("adapter", "tensor")),
        check_vma=False,
    )
```

time: 536 us -> 312 us (0.58)
  waiting for transfers between devices: 432 us -> 129 us
  starting transfers between devices: 20.4 us -> 62.2 us
  matrix products: 39.4 us -> 60.3 us
  blocking collectives: 0 us -> 15.8 us
  between operations: 15.7 us -> 1.68 us
  local copies, waits for them, and re-layouts: 23.8 us -> 33.7 us
    all_gather x2 -> x0, waiting for transfers between devices: 204 us -> none  [the longest x1 172 us: per_device(): lax.all_gather(base_weight, 'adapter', axis=1, tiled=True)]
    all_to_all x4 -> x1, waiting for transfers between devices: 187 us -> 0.01 us  [per_device(): lax.all_to_all(grad, 'tensor', split_axis=1, concat_axis=0, tiled=True)]
    ppermute x0 -> x35, waiting for transfers between devices: none -> 129 us  [the longest x8 60.5 us: send_up(): return lax.ppermute(x, 'adapter', up_pairs)]
    ppermute x0 -> x35, starting transfers between devices: none -> 57.9 us  [the longest x8 23.6 us: send_up(): return lax.ppermute(x, 'adapter', up_pairs)]
    psum x1 -> x0, waiting for transfers between devices: 39.7 us -> none  [per_device(): lax.psum((rank_inputs, rank_gradients), 'tensor')]
    dot_general x6 -> x20, matrix products: 39.4 us -> 60.3 us  [the longest x4 17.2 us: partial_sum(): lax.dot_general(rows[:, :out_cols], weight, (((1,), (1,)), ((), ())), pre...]
    unnamed x4 -> x66, local copies, waits for them, and re-layouts: 0.02 us -> 20.9 us
    all_to_all x4 -> x1, starting transfers between devices: 20.3 us -> 4.25 us  [per_device(): lax.all_to_all(grad, 'tensor', split_axis=1, concat_axis=0, tiled=True)]
  transfers between devices with their start and end apart: 7 -> 36, of which waited for: 7 -> 18; matrix products, arithmetic and copies ran while one was open for 8% -> 30% of each run, Pallas kernels for 0% -> 0%
where the time goes in v1:
time: 312 us; the launch traced here: 311 us
  waiting for transfers between devices  129 us (41%)
  starting transfers between devices  62.2 us (20%)
  matrix products  60.3 us (19%)
  local copies, waits for them, and re-layouts  33.7 us (11%)
  blocking collectives  15.8 us (5%)
  other arithmetic  8.69 us (3%)
    ppermute x8, waiting for transfers between devices, send_up(): return lax.ppermute(x, 'adapter', up_pairs)  60.5 us
    ppermute x8, waiting for transfers between devices, send_down(): return lax.ppermute(x, 'adapter', down_pairs)  55.9 us
    ppermute x8, starting transfers between devices, send_up(): return lax.ppermute(x, 'adapter', up_pairs)  23.6 us
    ppermute x8, starting transfers between devices, send_down(): return lax.ppermute(x, 'adapter', down_pairs)  23.1 us
    unnamed x66, local copies, waits for them, and re-layouts  20.9 us
    dot_general x4, matrix products, partial_sum(): lax.dot_general(rows[:, :out_cols], weight, (((1,), (1,)), ((), ())), pre...  17.2 us
    all_gather x1, blocking collectives, per_device(): all_ids = lax.all_gather(ids, 'adapter', axis=0, tiled=False)  15.8 us
    ppermute x8, waiting for transfers between devices, flip(): return lax.ppermute(x, 'tensor', [(t, t ^ bit) for t in range(tensors)])  12.1 us
  transfers between devices with their start and end apart: 36, of which 18 were waited for; matrix products, arithmetic and copies ran while one was open for 30% of the time, Pallas kernels for 0%

profile of v1, /device:TPU:0, one launch (start us, length us, event | category | flops | bytes accessed | tf_op | source)
XLA Modules:
  0.0 311.0 jit_solution(13033687538901646635)
XLA Ops:
  0.8 1.6 constant_dynamic-slice_fusion.15
  3.2 3.0 collective-permute-start
  7.0 2.0 collective-permute-start.2
  10.1 4.3 %all-to-all-start = ((bf16[64,4,2048]{2,0,1:T(8,128)(2,1)}), bf16[64,4,2048]{2,0,1:T(8,128)(2,1)}, u32[]{:S(2)}, u32[]{:S(2)}) async-start(bf16[64,4,2048]{2,0,1:T(8,128)(2,1)} %bitcast.168), calls=%async_computation | async-start | bytes 2097152 | tf_op jit(solution)/shard_map/all_to_all | solution.py:69
  14.4 15.8 %all-gather.1 = s32[8,1,256]{2,1,0:T(1,128)S(1)} all-gather(s32[1,1,256]{2,1,0:T(1,128)S(1)} %bitcast.181), channel_id=2, replica_groups=mesh['adapter'=8,'tensor'=4] {'adapter'}, dimensions={0}, use_global_device_ids=true | all-gather | bytes 9216 | tf_op jit(solution)/shard_map/all_gather | solution.py:72
  33.4 3.6 %collective-permute-start.3 = (bf16[64,1024]{1,0:T(8,128)(2,1)S(1)}, bf16[64,1024]{1,0:T(8,128)(2,1)S(1)}, u32[]{:S(2)}, u32[]{:S(2)}) collective-permute-start(bf16[64,1024]{1,0:T(8,128)(2,1)S(1)} %slice.270), channel_id=1, source_target_pairs={{8,0},{12,4},{16,8},{20,12},{24,16},{28,20},{0,24},{4,28},{9,1},{1... | collective-permute-start | bytes 393224 | tf_op jit(solution)/shard_map/ppermute | solution.py:34
  38.9 1.4 collective-permute-done.1
  40.4 1.3 collective-permute-done.3
  42.0 1.6 collective-permute-start.4
  43.5 1.5 collective-permute-start.6
  46.4 3.3 %collective-permute-start.11 = (bf16[256,2048]{1,0:T(8,128)(2,1)}, bf16[256,2048]{1,0:T(8,128)(2,1)S(1)}, u32[]{:S(2)}, u32[]{:S(2)}) collective-permute-start(bf16[256,2048]{1,0:T(8,128)(2,1)} %bitcast.28), channel_id=1, source_target_pairs={{8,0},{12,4},{16,8},{20,12},{24,16},{28,20},{0,24},{4,28},{9,1},{1... | collective-permute-start | bytes 3145736 | tf_op jit(solution)/shard_map/ppermute | solution.py:34
  49.7 2.3 constant_dynamic-update-slice_fusion.13
  52.0 3.2 %collective-permute-done.4 = bf16[1,4,32,2048]{3,2,1,0:T(8,128)(2,1)} collective-permute-done((bf16[1,4,32,2048]{3,2,1,0:T(8,128)(2,1)S(1)}, bf16[1,4,32,2048]{3,2,1,0:T(8,128)(2,1)}, u32[]{:S(2)}, u32[]{:S(2)}) %collective-permute-start.4) | collective-permute-done | bytes 524320 | tf_op jit(solution)/shard_map/ppermute | solution.py:40
  55.2 1.1 pad_maximum_fusion.1
  56.4 1.6 collective-permute-start.5
  57.9 1.1 pad_maximum_fusion.2
  59.1 1.6 collective-permute-start.7
  60.6 1.1 slice_bitcast_fusion.26
  61.8 1.1 slice_bitcast_fusion.21
  62.9 11.1 %collective-permute-done.9 = bf16[256,2048]{1,0:T(8,128)(2,1)S(1)} collective-permute-done((bf16[256,2048]{1,0:T(8,128)(2,1)}, bf16[256,2048]{1,0:T(8,128)(2,1)S(1)}, u32[]{:S(2)}, u32[]{:S(2)}) %collective-permute-start.9) | collective-permute-done | bytes 1048608 | tf_op jit(solution)/shard_map/ppermute | solution.py:31
  74.0 16.8 %collective-permute-start.10 = (bf16[128,2048]{1,0:T(8,128)(2,1)S(1)}, bf16[128,2048]{1,0:T(8,128)(2,1)S(1)}, u32[]{:S(2)}, u32[]{:S(2)}) collective-permute-start(bf16[128,2048]{1,0:T(8,128)(2,1)S(1)} %slice.284), channel_id=1, source_target_pairs={{0,8},{4,12},{8,16},{12,20},{16,24},{20,28},{24,0},{28,4},{1,9},{5... | collective-permute-start | bytes 1572872 | tf_op jit(solution)/shard_map/ppermute | solution.py:31
  90.9 2.4 collective-permute-done.11
  93.3 3.8 %collective-permute-start.12 = (bf16[128,2048]{1,0:T(8,128)(2,1)S(1)}, bf16[128,2048]{1,0:T(8,128)(2,1)S(1)}, u32[]{:S(2)}, u32[]{:S(2)}) collective-permute-start(bf16[128,2048]{1,0:T(8,128)(2,1)S(1)} %slice.285), channel_id=1, source_target_pairs={{8,0},{12,4},{16,8},{20,12},{24,16},{28,20},{0,24},{4,28},{9,1},{1... | collective-permute-start | bytes 1572872 | tf_op jit(solution)/shard_map/ppermute | solution.py:34
  97.1 1.1 constant_dynamic-update-slice_fusion.12
  100.4 3.5 %fusion.13 = f32[256,2048]{1,0:T(8,128)S(1)} fusion(bf16[2048,1024]{1,0:T(8,128)(2,1)} %param.9, bf16[256,2048]{1,0:T(8,128)(2,1)S(1)} %pad_maximum_fusion.4), kind=kOutput, calls=%fused_computation.49 | convolution fusion | flops 1073741824 | bytes 6815744 | tf_op jit(solution)/shard_map/dot_general | solution.py:141
  104.1 3.6 %fusion.10 = f32[256,2048]{1,0:T(8,128)S(1)} fusion(bf16[2048,1024]{1,0:T(8,128)(2,1)} %param.9, bf16[256,2048]{1,0:T(8,128)(2,1)S(1)} %pad_maximum_fusion.5), kind=kOutput, calls=%fused_computation.46 | convolution fusion | flops 1073741824 | bytes 6815744 | tf_op jit(solution)/shard_map/dot_general | solution.py:141
  107.9 5.2 %fusion.7 = f32[256,2048]{1,0:T(8,128)} fusion(bf16[2048,1024]{1,0:T(8,128)(2,1)} %param.9, bf16[256,2048]{1,0:T(8,128)(2,1)S(1)} %pad_maximum_fusion.7), kind=kOutput, calls=%fused_computation.43 | convolution fusion | flops 1073741824 | bytes 6815744 | tf_op jit(solution)/shard_map/dot_general | solution.py:141
  114.3 2.1 collective-permute-done.12
  118.1 3.1 collective-permute-start.27
  121.2 4.8 %fusion.16 = f32[256,2048]{1,0:T(8,128)} fusion(bf16[2048,1024]{1,0:T(8,128)(2,1)} %param.9, bf16[256,2048]{1,0:T(8,128)(2,1)S(1)} %pad_maximum_fusion.3), kind=kOutput, calls=%fused_computation.52 | convolution fusion | flops 1073741824 | bytes 6815744 | tf_op jit(solution)/shard_map/dot_general | solution.py:141
  126.0 1.1 constant_dynamic-update-slice_fusion.22
  127.2 1.2 constant_dynamic-update-slice_fusion.9
  131.0 14.1 %collective-permute-done.25 = bf16[256,2048]{1,0:T(8,128)(2,1)S(1)} collective-permute-done((bf16[256,2048]{1,0:T(8,128)(2,1)S(1)}, bf16[256,2048]{1,0:T(8,128)(2,1)S(1)}, u32[]{:S(2)}, u32[]{:S(2)}) %collective-permute-start.25) | collective-permute-done | bytes 1048608 | tf_op jit(solution)/shard_map/ppermute | solution.py:31
  145.2 20.6 %collective-permute-done.27 = bf16[256,2048]{1,0:T(8,128)(2,1)S(1)} collective-permute-done((bf16[256,2048]{1,0:T(8,128)(2,1)S(1)}, bf16[256,2048]{1,0:T(8,128)(2,1)S(1)}, u32[]{:S(2)}, u32[]{:S(2)}) %collective-permute-start.27) | collective-permute-done | bytes 1048608 | tf_op jit(solution)/shard_map/ppermute | solution.py:34
  167.8 3.1 %collective-permute-start.28 = (bf16[128,2048]{1,0:T(8,128)(2,1)S(1)}, bf16[128,2048]{1,0:T(8,128)(2,1)S(1)}, u32[]{:S(2)}, u32[]{:S(2)}) collective-permute-start(bf16[128,2048]{1,0:T(8,128)(2,1)S(1)} %slice.333), channel_id=1, source_target_pairs={{8,0},{12,4},{16,8},{20,12},{24,16},{28,20},{0,24},{4,28},{9,1},{1... | collective-permute-start | bytes 1572872 | tf_op jit(solution)/shard_map/ppermute | solution.py:34
  170.9 1.1 constant_dynamic-update-slice_fusion.5
  172.0 6.9 %fusion.28 = f32[2048,512]{0,1:T(8,128)S(1)} fusion(bf16[2048,2048]{1,0:T(8,128)(2,1)} %constant_dynamic-update-slice_fusion.5, bf16[512,2048]{1,0:T(8,128)(2,1)S(1)} %copy-done), kind=kOutput, calls=%fused_computation.172 | convolution fusion | flops 4294967296 | bytes 14680064 | tf_op jit(solution)/shard_map/dot_general | solution.py:117
  178.9 1.1 constant_dynamic-update-slice_fusion.21
  180.0 2.6 collective-permute-done.26
  183.4 9.7 %collective-permute-done.28 = bf16[128,2048]{1,0:T(8,128)(2,1)S(1)} collective-permute-done((bf16[128,2048]{1,0:T(8,128)(2,1)S(1)}, bf16[128,2048]{1,0:T(8,128)(2,1)S(1)}, u32[]{:S(2)}, u32[]{:S(2)}) %collective-permute-start.28) | collective-permute-done | bytes 524320 | tf_op jit(solution)/shard_map/ppermute | solution.py:34
  196.7 1.3 convolution_add_fusion.10
  198.0 1.3 convolution_add_fusion.9
  199.4 1.1 constant_dynamic-update-slice_fusion.16
  200.5 1.1 constant_dynamic-update-slice_fusion.15
  201.6 1.2 constant_dynamic-update-slice_fusion.14
  202.8 7.2 %fusion.30 = f32[2048,512]{0,1:T(8,128)S(1)} fusion(bf16[2048,2048]{1,0:T(8,128)(2,1)} %constant_dynamic-update-slice_fusion.14, bf16[2048,512]{1,0:T(8,128)(2,1)S(1)} %copy-done.2), kind=kOutput, calls=%fused_computation.174 | convolution fusion | flops 4294967296 | bytes 14680064 | tf_op jit(solution)/shard_map/dot_general | solution.py:172
  210.0 2.0 select_reduce_fusion
  212.1 1.4 convolution_add_fusion.8
  214.2 1.6 collective-permute-start.18
  215.7 4.2 %collective-permute-done.33 = f32[16,2048]{1,0:T(8,128)S(1)} collective-permute-done((f32[16,2048]{1,0:T(8,128)S(1)}, f32[16,2048]{1,0:T(8,128)S(1)}, u32[]{:S(2)}, u32[]{:S(2)}) %collective-permute-start.33) | collective-permute-done | bytes 131104 | tf_op jit(solution)/shard_map/ppermute | solution.py:40
  220.5 1.3 convolution_add_fusion.11
  222.3 1.1 collective-permute-start.19
  223.4 1.8 collective-permute-done.34
  225.2 2.5 collective-permute-done.19
  230.1 1.3 slice-done.1
  231.5 6.7 %fusion.29 = f32[2048,512]{1,0:T(8,128)} fusion(bf16[2048,2048]{1,0:T(8,128)(2,1)S(1)} %bitcast.172, bf16[512,2048]{1,0:T(8,128)(2,1)S(1)} %bitcast.158), kind=kOutput, calls=%fused_computation.173 | convolution fusion | flops 4294967296 | bytes 14680064 | tf_op jit(solution)/shard_map/dot_general | solution.py:177
  241.0 1.3 collective-permute-start.23
  244.8 9.0 %collective-permute-done.21 = bf16[128,2048]{1,0:T(8,128)(2,1)S(1)} collective-permute-done((bf16[128,2048]{1,0:T(8,128)(2,1)S(1)}, bf16[128,2048]{1,0:T(8,128)(2,1)S(1)}, u32[]{:S(2)}, u32[]{:S(2)}) %collective-permute-start.21) | collective-permute-done | bytes 524320 | tf_op jit(solution)/shard_map/ppermute | solution.py:34
  254.0 3.1 %collective-permute-start.22 = (bf16[256,2048]{1,0:T(8,128)(2,1)S(1)}, bf16[256,2048]{1,0:T(8,128)(2,1)S(1)}, u32[]{:S(2)}, u32[]{:S(2)}) collective-permute-start(bf16[256,2048]{1,0:T(8,128)(2,1)S(1)} %pad_maximum_fusion.6), channel_id=1, source_target_pairs={{8,0},{12,4},{16,8},{20,12},{24,16},{28,20},{0,24},{4,28},{9,1},{1... | collective-permute-start | bytes 3145736 | tf_op jit(solution)/shard_map/ppermute | solution.py:34
  257.1 9.4 %collective-permute-done.23 = bf16[128,2048]{1,0:T(8,128)(2,1)S(1)} collective-permute-done((bf16[128,2048]{1,0:T(8,128)(2,1)S(1)}, bf16[128,2048]{1,0:T(8,128)(2,1)S(1)}, u32[]{:S(2)}, u32[]{:S(2)}) %collective-permute-start.23) | collective-permute-done | bytes 524320 | tf_op jit(solution)/shard_map/ppermute | solution.py:31
  266.8 9.6 %fusion.31 = f32[512,2048]{1,0:T(8,128)} fusion(bf16[512,2048]{1,0:T(8,128)(2,1)S(1)} %bitcast.169, bf16[2048,2048]{1,0:T(8,128)(2,1)} %constant_dynamic-update-slice_fusion.5), kind=kOutput, calls=%fused_computation.175 | convolution fusion | flops 4294967296 | bytes 14680064 | tf_op jit(solution)/shard_map/dot_general | solution.py:180
  276.4 10.8 %collective-permute-done.22 = bf16[256,2048]{1,0:T(8,128)(2,1)S(1)} collective-permute-done((bf16[256,2048]{1,0:T(8,128)(2,1)S(1)}, bf16[256,2048]{1,0:T(8,128)(2,1)S(1)}, u32[]{:S(2)}, u32[]{:S(2)}) %collective-permute-start.22) | collective-permute-done | bytes 1048608 | tf_op jit(solution)/shard_map/ppermute | solution.py:34
  287.1 22.0 %collective-permute-done.24 = bf16[256,2048]{1,0:T(8,128)(2,1)S(1)} collective-permute-done((bf16[256,2048]{1,0:T(8,128)(2,1)S(1)}, bf16[256,2048]{1,0:T(8,128)(2,1)S(1)}, u32[]{:S(2)}, u32[]{:S(2)}) %collective-permute-start.24) | collective-permute-done | bytes 1048608 | tf_op jit(solution)/shard_map/ppermute | solution.py:31
  309.1 1.9 fusion.3
  (154 shorter events, 33.4 us)
Async XLA Ops:
  0.6 171.3 %copy-start = (bf16[512,2048]{1,0:T(8,128)(2,1)S(1)}, bf16[512,2048]{1,0:T(8,128)(2,1)}, u32[]{:S(2)}) copy-start(bf16[512,2048]{1,0:T(8,128)(2,1)} %param.11) | copy-start | bytes 6291460
  0.6 8.4 %copy-start.3 = (bf16[64,8192]{1,0:T(8,128)(2,1)S(1)}, bf16[64,8192]{1,0:T(8,128)(2,1)}, u32[]{:S(2)}) copy-start(bf16[64,8192]{1,0:T(8,128)(2,1)} %param.7) | copy-start | bytes 3145732
  3.2 28.0 %collective-permute-start = (bf16[64,3072]{1,0:T(8,128)(2,1)}, bf16[64,3072]{1,0:T(8,128)(2,1)}, u32[]{:S(2)}, u32[]{:S(2)}) collective-permute-start(bf16[64,3072]{1,0:T(8,128)(2,1)} %pad_maximum_fusion.10), channel_id=1, source_target_pairs={{0,8},{4,12},{8,16},{12,20},{16,24},{20,28},{24,0},{28,4},{1,9},{5... | collective-permute-start | bytes 1179656 | tf_op jit(solution)/shard_map/ppermute | solution.py:31
  7.0 25.5 %collective-permute-start.2 = (bf16[64,3072]{1,0:T(8,128)(2,1)}, bf16[64,3072]{1,0:T(8,128)(2,1)}, u32[]{:S(2)}, u32[]{:S(2)}) collective-permute-start(bf16[64,3072]{1,0:T(8,128)(2,1)} %pad_maximum_fusion.11), channel_id=1, source_target_pairs={{8,0},{12,4},{16,8},{20,12},{24,16},{28,20},{0,24},{4,28},{9,1},{1... | collective-permute-start | bytes 1179656 | tf_op jit(solution)/shard_map/ppermute | solution.py:34
  9.0 5.4 %copy-start.18 = (s32[256]{0:T(256)S(1)}, s32[256]{0:T(256)}, u32[]{:S(2)}) copy-start(s32[256]{0:T(256)} %param.8) | copy-start | bytes 3076
  10.1 35.8 %all-to-all-start = ((bf16[64,4,2048]{2,0,1:T(8,128)(2,1)}), bf16[64,4,2048]{2,0,1:T(8,128)(2,1)}, u32[]{:S(2)}, u32[]{:S(2)}) async-start(bf16[64,4,2048]{2,0,1:T(8,128)(2,1)} %bitcast.168), calls=%async_computation | async-start | bytes 2097152 | tf_op jit(solution)/shard_map/all_to_all | solution.py:69
  32.1 8.2 %collective-permute-start.1 = (bf16[64,1024]{1,0:T(8,128)(2,1)S(1)}, bf16[64,1024]{1,0:T(8,128)(2,1)S(1)}, u32[]{:S(2)}, u32[]{:S(2)}) collective-permute-start(bf16[64,1024]{1,0:T(8,128)(2,1)S(1)} %slice.269), channel_id=1, source_target_pairs={{0,8},{4,12},{8,16},{12,20},{16,24},{20,28},{24,0},{28,4},{1,9},{5... | collective-permute-start | bytes 393224 | tf_op jit(solution)/shard_map/ppermute | solution.py:31
  33.4 8.3 %collective-permute-start.3 = (bf16[64,1024]{1,0:T(8,128)(2,1)S(1)}, bf16[64,1024]{1,0:T(8,128)(2,1)S(1)}, u32[]{:S(2)}, u32[]{:S(2)}) collective-permute-start(bf16[64,1024]{1,0:T(8,128)(2,1)S(1)} %slice.270), channel_id=1, source_target_pairs={{8,0},{12,4},{16,8},{20,12},{24,16},{28,20},{0,24},{4,28},{9,1},{1... | collective-permute-start | bytes 393224 | tf_op jit(solution)/shard_map/ppermute | solution.py:34
  42.0 13.2 %collective-permute-start.4 = (bf16[1,4,32,2048]{3,2,1,0:T(8,128)(2,1)S(1)}, bf16[1,4,32,2048]{3,2,1,0:T(8,128)(2,1)}, u32[]{:S(2)}, u32[]{:S(2)}) collective-permute-start(bf16[1,4,32,2048]{3,2,1,0:T(8,128)(2,1)S(1)} %get-tuple-element.43), channel_id=1, source_target_pairs={{0,1},{1,0},{2,3},{3,2},{4,5},{5,4},{6,7},{7,6},{8,9},{9,8},{10,11... | collective-permute-start | bytes 1572872 | tf_op jit(solution)/shard_map/ppermute | solution.py:40
  43.5 14.4 %collective-permute-start.6 = (bf16[1,4,32,2048]{3,2,1,0:T(8,128)(2,1)S(1)}, bf16[1,4,32,2048]{3,2,1,0:T(8,128)(2,1)}, u32[]{:S(2)}, u32[]{:S(2)}) collective-permute-start(bf16[1,4,32,2048]{3,2,1,0:T(8,128)(2,1)S(1)} %get-tuple-element.44), channel_id=1, source_target_pairs={{0,2},{1,3},{2,0},{3,1},{4,6},{5,7},{6,4},{7,5},{8,10},{9,11},{10,... | collective-permute-start | bytes 1572872 | tf_op jit(solution)/shard_map/ppermute | solution.py:40
  45.9 28.1 %collective-permute-start.9 = (bf16[256,2048]{1,0:T(8,128)(2,1)}, bf16[256,2048]{1,0:T(8,128)(2,1)S(1)}, u32[]{:S(2)}, u32[]{:S(2)}) collective-permute-start(bf16[256,2048]{1,0:T(8,128)(2,1)} %bitcast.28), channel_id=1, source_target_pairs={{0,8},{4,12},{8,16},{12,20},{16,24},{20,28},{24,0},{28,4},{1,9},{5... | collective-permute-start | bytes 3145736 | tf_op jit(solution)/shard_map/ppermute | solution.py:31
  46.4 46.9 %collective-permute-start.11 = (bf16[256,2048]{1,0:T(8,128)(2,1)}, bf16[256,2048]{1,0:T(8,128)(2,1)S(1)}, u32[]{:S(2)}, u32[]{:S(2)}) collective-permute-start(bf16[256,2048]{1,0:T(8,128)(2,1)} %bitcast.28), channel_id=1, source_target_pairs={{8,0},{12,4},{16,8},{20,12},{24,16},{28,20},{0,24},{4,28},{9,1},{1... | collective-permute-start | bytes 3145736 | tf_op jit(solution)/shard_map/ppermute | solution.py:34
  49.7 76.3 %collective-permute-start.13 = (bf16[256,2048]{1,0:T(8,128)(2,1)}, bf16[256,2048]{1,0:T(8,128)(2,1)S(1)}, u32[]{:S(2)}, u32[]{:S(2)}) collective-permute-start(bf16[256,2048]{1,0:T(8,128)(2,1)} %bitcast.28), channel_id=1, source_target_pairs={{0,4},{4,0},{8,12},{12,8},{16,20},{20,16},{24,28},{28,24},{1,5},{5... | collective-permute-start | bytes 3145736 | tf_op jit(solution)/shard_map/ppermute | solution.py:37
  56.4 41.9 %collective-permute-start.5 = (bf16[2,4,32,2048]{3,2,1,0:T(8,128)(2,1)S(1)}, bf16[2,4,32,2048]{3,2,1,0:T(8,128)(2,1)S(1)}, u32[]{:S(2)}, u32[]{:S(2)}) collective-permute-start(bf16[2,4,32,2048]{3,2,1,0:T(8,128)(2,1)S(1)} %pad_maximum_fusion.1), channel_id=1, source_target_pairs={{0,2},{1,3},{2,0},{3,1},{4,6},{5,7},{6,4},{7,5},{8,10},{9,11},{10,... | collective-permute-start | bytes 3145736 | tf_op jit(solution)/shard_map/ppermute | solution.py:40
  59.1 39.3 %collective-permute-start.7 = (bf16[2,4,32,2048]{3,2,1,0:T(8,128)(2,1)S(1)}, bf16[2,4,32,2048]{3,2,1,0:T(8,128)(2,1)S(1)}, u32[]{:S(2)}, u32[]{:S(2)}) collective-permute-start(bf16[2,4,32,2048]{3,2,1,0:T(8,128)(2,1)S(1)} %pad_maximum_fusion.2), channel_id=1, source_target_pairs={{0,1},{1,0},{2,3},{3,2},{4,5},{5,4},{6,7},{7,6},{8,9},{9,8},{10,11... | collective-permute-start | bytes 3145736 | tf_op jit(solution)/shard_map/ppermute | solution.py:40
  74.0 39.4 %collective-permute-start.10 = (bf16[128,2048]{1,0:T(8,128)(2,1)S(1)}, bf16[128,2048]{1,0:T(8,128)(2,1)S(1)}, u32[]{:S(2)}, u32[]{:S(2)}) collective-permute-start(bf16[128,2048]{1,0:T(8,128)(2,1)S(1)} %slice.284), channel_id=1, source_target_pairs={{0,8},{4,12},{8,16},{12,20},{16,24},{20,28},{24,0},{28,4},{1,9},{5... | collective-permute-start | bytes 1572872 | tf_op jit(solution)/shard_map/ppermute | solution.py:31
  93.3 23.1 %collective-permute-start.12 = (bf16[128,2048]{1,0:T(8,128)(2,1)S(1)}, bf16[128,2048]{1,0:T(8,128)(2,1)S(1)}, u32[]{:S(2)}, u32[]{:S(2)}) collective-permute-start(bf16[128,2048]{1,0:T(8,128)(2,1)S(1)} %slice.285), channel_id=1, source_target_pairs={{8,0},{12,4},{16,8},{20,12},{24,16},{28,20},{0,24},{4,28},{9,1},{1... | collective-permute-start | bytes 1572872 | tf_op jit(solution)/shard_map/ppermute | solution.py:34
  98.2 0.9 copy-start.15
  98.2 1.0 copy-start.16
  98.2 30.1 %collective-permute-start.14 = (bf16[256,2048]{1,0:T(8,128)(2,1)S(1)}, bf16[256,2048]{1,0:T(8,128)(2,1)S(1)}, u32[]{:S(2)}, u32[]{:S(2)}) collective-permute-start(bf16[256,2048]{1,0:T(8,128)(2,1)S(1)} %collective-permute-done.9), channel_id=1, source_target_pairs={{0,4},{4,0},{8,12},{12,8},{16,20},{20,16},{24,28},{28,24},{1,5},{5... | collective-permute-start | bytes 3145736 | tf_op jit(solution)/shard_map/ppermute | solution.py:37
  99.2 0.9 copy-start.13
  99.2 1.0 copy-start.14
  104.1 3.6 %copy-start.12 = (bf16[1,32,2048]{2,1,0:T(8,128)(2,1)S(1)}, bf16[1,32,2048]{2,1,0:T(8,128)(2,1)}, u32[]{:S(2)}) copy-start(bf16[1,32,2048]{2,1,0:T(8,128)(2,1)} %get-tuple-element.90) | copy-start | bytes 393220
  107.9 5.2 %copy-start.6 = (bf16[256,2048]{1,0:T(8,128)(2,1)}, bf16[256,2048]{1,0:T(8,128)(2,1)S(1)}, u32[]{:S(2)}) copy-start(bf16[256,2048]{1,0:T(8,128)(2,1)S(1)} %pad_maximum_fusion.7) | copy-start | bytes 3145732
  113.4 12.6 %copy-start.4 = (bf16[256,2048]{1,0:T(8,128)(2,1)}, bf16[256,2048]{1,0:T(8,128)(2,1)S(1)}, u32[]{:S(2)}) copy-start(bf16[256,2048]{1,0:T(8,128)(2,1)S(1)} %pad_maximum_fusion.3) | copy-start | bytes 3145732
  113.4 3.9 %copy-start.10 = (bf16[256,2048]{1,0:T(8,128)(2,1)S(1)}, bf16[256,2048]{1,0:T(8,128)(2,1)}, u32[]{:S(2)}) copy-start(bf16[256,2048]{1,0:T(8,128)(2,1)} %param.6) | copy-start | bytes 3145732
  117.3 48.6 %collective-permute-start.15 = (bf16[256,2048]{1,0:T(8,128)(2,1)S(1)}, bf16[256,2048]{1,0:T(8,128)(2,1)S(1)}, u32[]{:S(2)}, u32[]{:S(2)}) collective-permute-start(bf16[256,2048]{1,0:T(8,128)(2,1)S(1)} %get-tuple-element.70), channel_id=1, source_target_pairs={{0,4},{4,0},{8,12},{12,8},{16,20},{20,16},{24,28},{28,24},{1,5},{5... | collective-permute-start | bytes 3145736 | tf_op jit(solution)/shard_map/ppermute | solution.py:37
  117.3 27.8 %collective-permute-start.25 = (bf16[256,2048]{1,0:T(8,128)(2,1)S(1)}, bf16[256,2048]{1,0:T(8,128)(2,1)S(1)}, u32[]{:S(2)}, u32[]{:S(2)}) collective-permute-start(bf16[256,2048]{1,0:T(8,128)(2,1)S(1)} %copy-done.10), channel_id=1, source_target_pairs={{0,8},{4,12},{8,16},{12,20},{16,24},{20,28},{24,0},{28,4},{1,9},{5... | collective-permute-start | bytes 3145736 | tf_op jit(solution)/shard_map/ppermute | solution.py:31
  118.1 47.7 %collective-permute-start.27 = (bf16[256,2048]{1,0:T(8,128)(2,1)S(1)}, bf16[256,2048]{1,0:T(8,128)(2,1)S(1)}, u32[]{:S(2)}, u32[]{:S(2)}) collective-permute-start(bf16[256,2048]{1,0:T(8,128)(2,1)S(1)} %copy-done.10), channel_id=1, source_target_pairs={{8,0},{12,4},{16,8},{20,12},{24,16},{28,20},{0,24},{4,28},{9,1},{1... | collective-permute-start | bytes 3145736 | tf_op jit(solution)/shard_map/ppermute | solution.py:34
  126.0 41.7 %collective-permute-start.16 = (bf16[256,2048]{1,0:T(8,128)(2,1)S(1)}, bf16[256,2048]{1,0:T(8,128)(2,1)S(1)}, u32[]{:S(2)}, u32[]{:S(2)}) collective-permute-start(bf16[256,2048]{1,0:T(8,128)(2,1)S(1)} %collective-permute-done.11), channel_id=1, source_target_pairs={{0,4},{4,0},{8,12},{12,8},{16,20},{20,16},{24,28},{28,24},{1,5},{5... | collective-permute-start | bytes 3145736 | tf_op jit(solution)/shard_map/ppermute | solution.py:37
  128.3 16.8 %copy-start.2 = (bf16[2048,512]{1,0:T(8,128)(2,1)S(1)}, bf16[2048,512]{1,0:T(8,128)(2,1)}, u32[]{:S(2)}) copy-start(bf16[2048,512]{1,0:T(8,128)(2,1)} %param.10) | copy-start | bytes 6291460
  128.3 68.3 %collective-permute-start.8 = (bf16[2048,1024]{1,0:T(8,128)(2,1)}, bf16[2048,1024]{1,0:T(8,128)(2,1)S(1)}, u32[]{:S(2)}, u32[]{:S(2)}) collective-permute-start(bf16[2048,1024]{1,0:T(8,128)(2,1)} %param.9), channel_id=1, source_target_pairs={{0,4},{4,0},{8,12},{12,8},{16,20},{20,16},{24,28},{28,24},{1,5},{5... | collective-permute-start | bytes 12582920 | tf_op jit(solution)/shard_map/ppermute | solution.py:37
  145.2 93.0 %collective-permute-start.20 = (bf16[2048,512]{1,0:T(8,128)(2,1)S(1)}, bf16[2048,512]{1,0:T(8,128)(2,1)S(1)}, u32[]{:S(2)}, u32[]{:S(2)}) collective-permute-start(bf16[2048,512]{1,0:T(8,128)(2,1)S(1)} %copy-done.2), channel_id=1, source_target_pairs={{0,4},{4,0},{8,12},{12,8},{16,20},{20,16},{24,28},{28,24},{1,5},{5... | collective-permute-start | bytes 6291464 | tf_op jit(solution)/shard_map/ppermute | solution.py:37
  165.9 29.2 %collective-permute-start.29 = (bf16[256,2048]{1,0:T(8,128)(2,1)S(1)}, bf16[256,2048]{1,0:T(8,128)(2,1)S(1)}, u32[]{:S(2)}, u32[]{:S(2)}) collective-permute-start(bf16[256,2048]{1,0:T(8,128)(2,1)S(1)} %copy-done.10), channel_id=1, source_target_pairs={{0,4},{4,0},{8,12},{12,8},{16,20},{20,16},{24,28},{28,24},{1,5},{5... | collective-permute-start | bytes 3145736 | tf_op jit(solution)/shard_map/ppermute | solution.py:37
  165.9 16.7 %collective-permute-start.26 = (bf16[128,2048]{1,0:T(8,128)(2,1)S(1)}, bf16[128,2048]{1,0:T(8,128)(2,1)S(1)}, u32[]{:S(2)}, u32[]{:S(2)}) collective-permute-start(bf16[128,2048]{1,0:T(8,128)(2,1)S(1)} %slice.332), channel_id=1, source_target_pairs={{0,8},{4,12},{8,16},{12,20},{16,24},{20,28},{24,0},{28,4},{1,9},{5... | collective-permute-start | bytes 1572872 | tf_op jit(solution)/shard_map/ppermute | solution.py:31
  167.8 25.4 %collective-permute-start.28 = (bf16[128,2048]{1,0:T(8,128)(2,1)S(1)}, bf16[128,2048]{1,0:T(8,128)(2,1)S(1)}, u32[]{:S(2)}, u32[]{:S(2)}) collective-permute-start(bf16[128,2048]{1,0:T(8,128)(2,1)S(1)} %slice.333), channel_id=1, source_target_pairs={{8,0},{12,4},{16,8},{20,12},{24,16},{28,20},{0,24},{4,28},{9,1},{1... | collective-permute-start | bytes 1572872 | tf_op jit(solution)/shard_map/ppermute | solution.py:34
  182.6 16.8 %collective-permute-start.30 = (bf16[256,2048]{1,0:T(8,128)(2,1)S(1)}, bf16[256,2048]{1,0:T(8,128)(2,1)S(1)}, u32[]{:S(2)}, u32[]{:S(2)}) collective-permute-start(bf16[256,2048]{1,0:T(8,128)(2,1)S(1)} %collective-permute-done.25), channel_id=1, source_target_pairs={{0,4},{4,0},{8,12},{12,8},{16,20},{20,16},{24,28},{28,24},{1,5},{5... | collective-permute-start | bytes 3145736 | tf_op jit(solution)/shard_map/ppermute | solution.py:37
  193.1 8.5 %collective-permute-start.32 = (bf16[256,2048]{1,0:T(8,128)(2,1)S(1)}, bf16[256,2048]{1,0:T(8,128)(2,1)S(1)}, u32[]{:S(2)}, u32[]{:S(2)}) collective-permute-start(bf16[256,2048]{1,0:T(8,128)(2,1)S(1)} %collective-permute-done.27), channel_id=1, source_target_pairs={{0,4},{4,0},{8,12},{12,8},{16,20},{20,16},{24,28},{28,24},{1,5},{5... | collective-permute-start | bytes 3145736 | tf_op jit(solution)/shard_map/ppermute | solution.py:37
  195.1 5.4 %collective-permute-start.31 = (bf16[256,2048]{1,0:T(8,128)(2,1)S(1)}, bf16[256,2048]{1,0:T(8,128)(2,1)S(1)}, u32[]{:S(2)}, u32[]{:S(2)}) collective-permute-start(bf16[256,2048]{1,0:T(8,128)(2,1)S(1)} %pad_maximum_fusion.9), channel_id=1, source_target_pairs={{0,4},{4,0},{8,12},{12,8},{16,20},{20,16},{24,28},{28,24},{1,5},{5... | collective-permute-start | bytes 3145736 | tf_op jit(solution)/shard_map/ppermute | solution.py:37
  210.0 2.1 copy-start.7
  210.0 2.1 copy-start.8
  212.0 8.5 %copy-start.5 = (bf16[256,2048]{1,0:T(8,128)(2,1)S(1)}, bf16[256,2048]{1,0:T(8,128)(2,1)}, u32[]{:S(2)}) copy-start(bf16[256,2048]{1,0:T(8,128)(2,1)} %copy-done.4) | copy-start | bytes 3145732
  212.0 8.5 %copy-start.9 = (f32[256,2048]{1,0:T(8,128)S(1)}, f32[256,2048]{1,0:T(8,128)}, u32[]{:S(2)}) copy-start(f32[256,2048]{1,0:T(8,128)} %fusion.16) | copy-start | bytes 6291460
  212.0 2.1 collective-permute-start.17
  213.5 6.4 %collective-permute-start.33 = (f32[16,2048]{1,0:T(8,128)S(1)}, f32[16,2048]{1,0:T(8,128)S(1)}, u32[]{:S(2)}, u32[]{:S(2)}) collective-permute-start(f32[16,2048]{1,0:T(8,128)S(1)} %get-tuple-element.7), channel_id=1, source_target_pairs={{0,1},{1,0},{2,3},{3,2},{4,5},{5,4},{6,7},{7,6},{8,9},{9,8},{10,11... | collective-permute-start | bytes 393224 | tf_op jit(solution)/shard_map/ppermute | solution.py:40
  214.2 8.1 %collective-permute-start.18 = (f32[16,2048]{1,0:T(8,128)S(1)}, f32[16,2048]{1,0:T(8,128)S(1)}, u32[]{:S(2)}, u32[]{:S(2)}) collective-permute-start(f32[16,2048]{1,0:T(8,128)S(1)} %maximum_add_fusion), channel_id=1, source_target_pairs={{0,1},{1,0},{2,3},{3,2},{4,5},{5,4},{6,7},{7,6},{8,9},{9,8},{10,11... | collective-permute-start | bytes 393224 | tf_op jit(solution)/shard_map/ppermute | solution.py:40
  219.9 7.9 %copy-start.11 = (pred[32,2048]{1,0:T(8,128)(4,1)S(1)}, pred[32,2048]{1,0:T(8,128)(4,1)}, u32[]{:S(2)}) copy-start(pred[32,2048]{1,0:T(8,128)(4,1)} %get-tuple-element.79) | copy-start | bytes 196612
  219.9 7.9 %copy-start.17 = (pred[32,2048]{1,0:T(8,128)(4,1)S(1)}, pred[32,2048]{1,0:T(8,128)(4,1)}, u32[]{:S(2)}) copy-start(pred[32,2048]{1,0:T(8,128)(4,1)} %get-tuple-element.78) | copy-start | bytes 196612
  219.9 5.3 %collective-permute-start.34 = (f32[16,2048]{1,0:T(8,128)S(1)}, f32[16,2048]{1,0:T(8,128)S(1)}, u32[]{:S(2)}, u32[]{:S(2)}) collective-permute-start(f32[16,2048]{1,0:T(8,128)S(1)} %add.315), channel_id=1, source_target_pairs={{0,2},{1,3},{2,0},{3,1},{4,6},{5,7},{6,4},{7,5},{8,10},{9,11},{10,... | collective-permute-start | bytes 393224 | tf_op jit(solution)/shard_map/ppermute | solution.py:40
  222.3 5.5 %collective-permute-start.19 = (f32[16,2048]{1,0:T(8,128)S(1)}, f32[16,2048]{1,0:T(8,128)S(1)}, u32[]{:S(2)}, u32[]{:S(2)}) collective-permute-start(f32[16,2048]{1,0:T(8,128)S(1)} %add.296), channel_id=1, source_target_pairs={{0,2},{1,3},{2,0},{3,1},{4,6},{5,7},{6,4},{7,5},{8,10},{9,11},{10,... | collective-permute-start | bytes 393224 | tf_op jit(solution)/shard_map/ppermute | solution.py:40
  227.8 2.3 slice-start
  228.5 2.9 slice-start.1
  239.0 14.7 %collective-permute-start.21 = (bf16[128,2048]{1,0:T(8,128)(2,1)S(1)}, bf16[128,2048]{1,0:T(8,128)(2,1)S(1)}, u32[]{:S(2)}, u32[]{:S(2)}) collective-permute-start(bf16[128,2048]{1,0:T(8,128)(2,1)S(1)} %get-tuple-element.9), channel_id=1, source_target_pairs={{8,0},{12,4},{16,8},{20,12},{24,16},{28,20},{0,24},{4,28},{9,1},{1... | collective-permute-start | bytes 1572872 | tf_op jit(solution)/shard_map/ppermute | solution.py:34
  241.0 25.5 %collective-permute-start.23 = (bf16[128,2048]{1,0:T(8,128)(2,1)S(1)}, bf16[128,2048]{1,0:T(8,128)(2,1)S(1)}, u32[]{:S(2)}, u32[]{:S(2)}) collective-permute-start(bf16[128,2048]{1,0:T(8,128)(2,1)S(1)} %get-tuple-element.10), channel_id=1, source_target_pairs={{0,8},{4,12},{8,16},{12,20},{16,24},{20,28},{24,0},{28,4},{1,9},{5... | collective-permute-start | bytes 1572872 | tf_op jit(solution)/shard_map/ppermute | solution.py:31
  254.0 33.2 %collective-permute-start.22 = (bf16[256,2048]{1,0:T(8,128)(2,1)S(1)}, bf16[256,2048]{1,0:T(8,128)(2,1)S(1)}, u32[]{:S(2)}, u32[]{:S(2)}) collective-permute-start(bf16[256,2048]{1,0:T(8,128)(2,1)S(1)} %pad_maximum_fusion.6), channel_id=1, source_target_pairs={{8,0},{12,4},{16,8},{20,12},{24,16},{28,20},{0,24},{4,28},{9,1},{1... | collective-permute-start | bytes 3145736 | tf_op jit(solution)/shard_map/ppermute | solution.py:34
  266.7 42.4 %collective-permute-start.24 = (bf16[256,2048]{1,0:T(8,128)(2,1)S(1)}, bf16[256,2048]{1,0:T(8,128)(2,1)S(1)}, u32[]{:S(2)}, u32[]{:S(2)}) collective-permute-start(bf16[256,2048]{1,0:T(8,128)(2,1)S(1)} %pad_maximum_fusion.8), channel_id=1, source_target_pairs={{0,8},{4,12},{8,16},{12,20},{16,24},{20,28},{24,0},{28,4},{1,9},{5... | collective-permute-start | bytes 3145736 | tf_op jit(solution)/shard_map/ppermute | solution.py:31
  266.8 44.2 %copy-start.1 = (bf16[512,2048]{1,0:T(8,128)(2,1)S(1)}, bf16[512,2048]{1,0:T(8,128)(2,1)}, u32[]{:S(2)}) copy-start(bf16[512,2048]{1,0:T(8,128)(2,1)} %param.11) | copy-start | bytes 6291460

commit v2 on v0

v2 whole, which is shorter than its diff:
```python
import functools

import jax
import jax.numpy as jnp
from jax import lax
from jax.experimental import pallas as pl
from jax.experimental.pallas import tpu as pltpu
from jax.sharding import PartitionSpec as P

ADAPTER_RANK = 16
ADAPTER_SCALE = 2.0
ROWS = 16
F32 = jnp.float32
BF16 = jnp.bfloat16
I32 = jnp.int32
NT = (((1,), (1,)), ((), ()))
VMEM_BYTES = 56 * 1024 * 1024
IN_VMEM = pl.BlockSpec(memory_space=pltpu.VMEM)
IN_SMEM = pl.BlockSpec(memory_space=pltpu.SMEM)
ANYWHERE = pl.BlockSpec(memory_space=pl.ANY)


def cost(flops, nbytes):
    return pl.CostEstimate(flops=int(flops) // 64, bytes_accessed=int(nbytes) // 64, transcendentals=0)


def params():
    return pltpu.CompilerParams(vmem_limit_bytes=VMEM_BYTES)


def pack_kernel(slot_ref, *refs):
    pieces, out_ref = refs[:-1], refs[-1]
    shape = (out_ref.shape[0], slot_ref.shape[1])
    pick = (lax.broadcasted_iota(I32, shape, 0) == slot_ref[...]).astype(F32).astype(BF16)
    rows = jnp.concatenate([piece[...] for piece in pieces], axis=0)
    out_ref[...] = jnp.dot(pick, rows, preferred_element_type=F32).astype(BF16)


def pack_rows(slot, pieces, slots):
    tokens, width = slot.shape[1], pieces[0].shape[1]
    tile = min(1024, width)
    column = lambda n: (0, n)
    return pl.pallas_call(
        pack_kernel,
        grid=(width // tile,),
        out_shape=jax.ShapeDtypeStruct((slots, width), BF16),
        in_specs=[pl.BlockSpec((1, tokens), lambda n: (0, 0))]
        + [pl.BlockSpec((piece.shape[0], tile), column) for piece in pieces],
        out_specs=pl.BlockSpec((slots, tile), column),
        compiler_params=params(),
        cost_estimate=cost(2 * tokens * slots * width, 2 * (tokens + slots) * width),
        name="pack_rows",
    )(slot, *pieces)


def masked_sum(projected, local, per_owner):
    total = jnp.zeros((ADAPTER_RANK, projected.shape[1]), F32)
    for j in range(per_owner):
        total = total + jnp.where(local == j, projected[j * ADAPTER_RANK : (j + 1) * ADAPTER_RANK], 0.0)
    return total


def repack_kernel(planes, per_owner, plane_ref, places_ref, local_ref, own_d_ref, other_d_ref, *refs):
    pieces = refs[: 2 * planes - 1]
    own_ref, other_ref, ranks_ref, rows, downs, sems, down_sems = refs[2 * planes - 1 :]
    here, below, above = pieces[0], pieces[1:planes], pieces[planes:]
    plane = plane_ref[0]

    def copy(source, d):
        return pltpu.make_async_copy(source, rows.at[d], sems.at[d])

    copy(here, 0).start()
    for d in range(1, planes):
        @pl.when(plane + d < planes)
        def _():
            copy(below[d - 1], d).start()

        @pl.when(plane + d >= planes)
        def _():
            copy(above[planes - d - 1], d).start()

    weights = [
        pltpu.make_async_copy(source, downs.at[i], down_sems.at[i]) for i, source in enumerate((own_d_ref, other_d_ref))
    ]
    for weight in weights:
        weight.start()
    tokens = here.shape[0]
    capacity = own_ref.shape[0] // planes
    row = lax.broadcasted_iota(I32, (2 * capacity, tokens), 0)
    for d in range(planes):
        copy(here, d).wait()
        pick = (row == places_ref[:, d * tokens : (d + 1) * tokens]).astype(F32).astype(BF16)
        packed = jnp.dot(pick, rows[d], preferred_element_type=F32).astype(BF16)
        own_ref[pl.ds(d * capacity, capacity), :] = packed[:capacity]
        other_ref[pl.ds(d * capacity, capacity), :] = packed[capacity:]
    for i, out_ref in enumerate((own_ref, other_ref)):
        weights[i].wait()
        projected = lax.dot_general(downs[i], out_ref[...], NT, preferred_element_type=F32)
        ranks_ref[i] = masked_sum(projected, local_ref[i : i + 1, :], per_owner)


def repack(plane, places, local, down_ts, here, below, above, capacity, per_owner):
    tokens, width = here.shape
    planes = len(below) + 1
    slots = planes * capacity
    rank_cols = down_ts[0].shape[0]
    return pl.pallas_call(
        functools.partial(repack_kernel, planes, per_owner),
        out_shape=[jax.ShapeDtypeStruct((slots, width), BF16)] * 2
        + [jax.ShapeDtypeStruct((2, ADAPTER_RANK, slots), F32)],
        in_specs=[IN_SMEM, IN_VMEM, IN_VMEM] + [ANYWHERE] * (2 * planes + 1),
        out_specs=[IN_VMEM] * 3,
        scratch_shapes=[
            pltpu.VMEM((planes, tokens, width), BF16),
            pltpu.VMEM((2, rank_cols, width), BF16),
            pltpu.SemaphoreType.DMA((planes,)),
            pltpu.SemaphoreType.DMA((2,)),
        ],
        compiler_params=params(),
        cost_estimate=cost(4 * slots * (tokens + rank_cols) * width, 2 * planes * (tokens + 2 * capacity) * width),
        name="repack",
    )(plane.reshape(1), places, local, *down_ts, here, *below, *above)


def ranks_kernel(per_owner, blocks, order_ref, local_ref, weight_ref, *refs):
    pieces, (out_ref, projected) = refs[:blocks], refs[blocks:]
    k = pl.program_id(0)
    rows = jnp.concatenate([piece[...] for piece in pieces], axis=0)
    part = lax.dot_general(weight_ref[...], rows, NT, preferred_element_type=F32)

    @pl.when(k == 0)
    def _():
        projected[...] = part

    @pl.when(k > 0)
    def _():
        projected[...] += part

    @pl.when(k == pl.num_programs(0) - 1)
    def _():
        out_ref[...] = masked_sum(projected, local_ref[...], per_owner)


def block_specs(blocks, capacity, tile):
    return [pl.BlockSpec((capacity, tile), lambda n, order, i=i: (order[i], n)) for i in range(blocks)]


def token_ranks(order, local, weight, slots, per_owner):
    blocks, width = order.shape[0], weight.shape[1]
    total = local.shape[1]
    rank_cols = weight.shape[0]
    tile = min(512, width)
    return pl.pallas_call(
        functools.partial(ranks_kernel, per_owner, blocks),
        out_shape=jax.ShapeDtypeStruct((ADAPTER_RANK, total), F32),
        grid_spec=pltpu.PrefetchScalarGridSpec(
            num_scalar_prefetch=1,
            grid=(width // tile,),
            in_specs=[
                pl.BlockSpec((1, total), lambda n, order: (0, 0)),
                pl.BlockSpec((rank_cols, tile), lambda n, order: (0, n)),
            ]
            + block_specs(blocks, total // blocks, tile),
            out_specs=pl.BlockSpec((ADAPTER_RANK, total), lambda n, order: (0, 0)),
            scratch_shapes=[pltpu.VMEM((rank_cols, total), F32)],
        ),
        compiler_params=params(),
        cost_estimate=cost(2 * total * width * rank_cols, 2 * width * (total + rank_cols)),
        name="token_ranks",
    )(order, local, weight, *[slots] * blocks)


def load_rows(place_ref, pieces, rows, sems):
    me = place_ref[0]
    copies = []
    tensors = rows.shape[1]
    for i, piece in enumerate(pieces):
        blocks = pl.ds(i // tensors * piece.shape[0], piece.shape[0])
        copies.append(pltpu.make_async_copy(piece, rows.at[blocks, me ^ (i % tensors)], sems.at[i]))
        copies[-1].start()
    for copy in copies:
        copy.wait()


def frozen_kernel(place_ref, own_w_ref, other_w_ref, *refs):
    pieces, (out_ref, rows, sems) = refs[:-3], refs[-3:]
    blocks, tensors, sub, _ = rows.shape
    tokens = tensors * sub
    depth = own_w_ref.shape[1]

    @pl.when(pl.program_id(0) == 0)
    def _():
        load_rows(place_ref, pieces, rows, sems)

    for b in range(blocks):
        x = rows[b].reshape(tokens, 2 * depth)
        product = lax.dot_general(x[:, :depth], own_w_ref[...], NT, preferred_element_type=F32)
        product += lax.dot_general(x[:, depth:], other_w_ref[...], NT, preferred_element_type=F32)
        out_ref[pl.ds(b * tokens, tokens), :] = product


def frozen_part(tensor, weights, pieces):
    blocks, sub, cols = pieces[0].shape
    blocks, tensors = 2 * blocks, len(pieces) // 2
    rows = blocks * sub * tensors
    width, depth = weights[0].shape
    tile = min(512, width)
    return pl.pallas_call(
        frozen_kernel,
        grid=(width // tile,),
        out_shape=jax.ShapeDtypeStruct((rows, width), F32),
        in_specs=[IN_SMEM] + [pl.BlockSpec((tile, depth), lambda n: (n, 0))] * 2 + [ANYWHERE] * len(pieces),
        out_specs=pl.BlockSpec((rows, tile), lambda n: (0, n)),
        scratch_shapes=[pltpu.VMEM((blocks, tensors, sub, cols), BF16), pltpu.SemaphoreType.DMA((len(pieces),))],
        compiler_params=params(),
        cost_estimate=cost(2 * rows * width * cols, 4 * rows * width + 4 * width * depth),
        name="frozen_part",
    )(tensor.reshape(1), *weights, *pieces)


def spread_rows(wide, first, local, ranks, per_owner):
    for j in range(per_owner):
        wide[pl.ds(first + j * ADAPTER_RANK, ADAPTER_RANK), :] = jnp.where(local == j, ranks, 0.0).astype(BF16)


def term_kernel(per_owner, frozen_ref, places_ref, *refs):
    ranks, downs, out_refs, (wide, flat) = refs[:2], refs[2:4], refs[4:-2], refs[-2:]
    rank_cols = downs[0].shape[0]

    @pl.when(pl.program_id(0) == 0)
    def _():
        for i in range(2):
            slot, local = places_ref[i : i + 1, :], places_ref[i + 2 : i + 3, :]
            pick = lax.broadcasted_iota(I32, (ranks[i].shape[1], slot.shape[1]), 0) == slot
            in_order = jnp.dot(ranks[i][...], pick.astype(F32).astype(BF16), preferred_element_type=F32)
            spread_rows(wide, i * rank_cols, local, in_order, per_owner)
        flat[...] = wide[...].T

    total = frozen_ref[...]
    total += jnp.dot(flat[:, :rank_cols], downs[0][...], preferred_element_type=F32)
    total += jnp.dot(flat[:, rank_cols:], downs[1][...], preferred_element_type=F32)
    rows = total.shape[0] // len(out_refs)
    for i, out_ref in enumerate(out_refs):
        out_ref[...] = total[i * rows : (i + 1) * rows].astype(out_ref.dtype)


def add_term(frozen, first, rows, places, ranks, downs, per_owner, types):
    width = frozen.shape[1]
    rank_cols = downs[0].shape[0]
    tile = min(512, width)
    column = lambda n: (0, n)
    each = rows // len(types)
    return pl.pallas_call(
        functools.partial(term_kernel, per_owner),
        grid=(width // tile,),
        out_shape=[jax.ShapeDtypeStruct((each, width), kind) for kind in types],
        in_specs=[
            pl.BlockSpec((rows, tile), lambda n: (first, n)),
            pl.BlockSpec((places.shape[0], rows), lambda n: (0, first)),
        ]
        + [pl.BlockSpec(x.shape, lambda n: (0, 0)) for x in ranks]
        + [pl.BlockSpec((rank_cols, tile), column)] * 2,
        out_specs=[pl.BlockSpec((each, tile), column)] * len(types),
        scratch_shapes=[pltpu.VMEM((2 * rank_cols, rows), BF16), pltpu.VMEM((rows, 2 * rank_cols), BF16)],
        compiler_params=params(),
        cost_estimate=cost(4 * rows * width * rank_cols, 6 * rows * width + 4 * rank_cols * width),
        name="add_term",
    )(frozen, places, *ranks, *downs)


def gradients_kernel(per_owner, blocks, order_ref, local_ref, grad_ranks_ref, up_ranks_ref, own_ref, other_ref, *refs):
    grad, (down_ref, up_ref, wide_grad, wide_up) = refs[:blocks], refs[blocks:]

    @pl.when(pl.program_id(0) == 0)
    def _():
        local = local_ref[...]
        spread_rows(wide_grad, 0, local, grad_ranks_ref[...].astype(F32), per_owner)
        spread_rows(wide_up, 0, local, up_ranks_ref[...].astype(F32), per_owner)

    rows = jnp.concatenate([own_ref[...], other_ref[...]], axis=0)
    down_ref[...] = jnp.dot(wide_grad[...], rows, preferred_element_type=F32).T
    rows = jnp.concatenate([piece[...] for piece in grad], axis=0)
    up_ref[...] = jnp.dot(wide_up[...], rows, preferred_element_type=F32)


def adapter_gradients(order, local, grad_ranks, up_ranks, attn, grad, per_owner):
    total, width = grad.shape
    blocks = order.shape[0]
    rank_cols = per_owner * ADAPTER_RANK
    tile = min(256, width)
    whole = lambda n, order: (0, 0)
    column = lambda n, order: (0, n)
    return pl.pallas_call(
        functools.partial(gradients_kernel, per_owner, blocks),
        out_shape=(
            jax.ShapeDtypeStruct((width, rank_cols), F32),
            jax.ShapeDtypeStruct((rank_cols, width), F32),
        ),
        grid_spec=pltpu.PrefetchScalarGridSpec(
            num_scalar_prefetch=1,
            grid=(width // tile,),
            in_specs=[pl.BlockSpec((1, total), whole)]
            + [pl.BlockSpec((ADAPTER_RANK, total), whole)] * 2
            + [pl.BlockSpec((total // 2, tile), column)] * 2
            + block_specs(blocks, total // blocks, tile),
            out_specs=(
                pl.BlockSpec((tile, rank_cols), lambda n, order: (n, 0)),
                pl.BlockSpec((rank_cols, tile), column),
            ),
            scratch_shapes=[pltpu.VMEM((rank_cols, total), BF16)] * 2,
        ),
        compiler_params=params(),
        cost_estimate=cost(4 * total * width * rank_cols, 4 * total * width + 8 * rank_cols * width),
        name="adapter_gradients",
    )(order, local, grad_ranks, up_ranks, *attn, *[grad] * blocks)


def per_device(attn, grad, ids, weight, down, up):
    owners = lax.axis_size("adapter")
    tensors = lax.axis_size("tensor")
    planes = owners // 2
    me = lax.axis_index("adapter")
    plane, core = me // 2, me % 2
    tensor = lax.axis_index("tensor")
    tokens, width = attn.shape
    sub = grad.shape[0]
    out_cols = weight.shape[1]
    rank_cols = down.shape[1]
    per_owner = rank_cols // ADAPTER_RANK
    capacity = -(-5 * tokens // (2 * owners) // ROWS) * ROWS
    slot_count = owners * capacity

    def shift(x, by):
        pairs = [(2 * z + c, 2 * ((z + by) % planes) + c) for z in range(planes) for c in range(2)]
        return lax.ppermute(x, "adapter", pairs)

    def up_line(x, distance):
        pairs = [(2 * z + c, 2 * z + 2 + c) for z in range(planes - distance) for c in range(2)]
        return lax.ppermute(x, "adapter", pairs)

    def down_line(x, distance):
        pairs = [(2 * z + c, 2 * z - 2 + c) for z in range(distance, planes) for c in range(2)]
        return lax.ppermute(x, "adapter", pairs)

    def attn_line(x, d, way):
        planes_on = range(d - 1, planes - 1) if way == 1 else range(1, planes - d + 1)
        return lax.ppermute(x, "adapter", [(2 * z + c, 2 * (z + way) + c) for z in planes_on for c in range(2)])

    def swap(x):
        return lax.ppermute(x, "adapter", [(a, a ^ 1) for a in range(owners)])

    def flip(x, k):
        return lax.ppermute(x, "tensor", [(t, t ^ k) for t in range(tensors)])

    def after(x, *others):
        return lax.optimization_barrier((x, *others))[0]

    def tensor_cols(k):
        return lax.dynamic_slice_in_dim(grad, (tensor ^ k) * width, width, 1)

    tensor_parts = [tensor_cols(k) for k in range(tensors)]
    grad_rows = tensor_parts[:1] + [flip(tensor_parts[k], k) for k in range(1, tensors)]
    grad_again, ids_again = after((grad, ids), *tensor_parts)

    def plane_cols(offset):
        p = (plane + offset) % planes
        parts = [
            lax.dynamic_slice_in_dim(grad_again, (2 * p + c) * out_cols, out_cols, 1) for c in (core, 1 - core)
        ]
        return jnp.concatenate(parts, axis=1)

    half = planes // 2
    order = [d for s in range(1, half) for d in (s, planes - s)] + [half, 0]
    plane_parts = [plane_cols(d) for d in range(planes)]
    part = {0: plane_parts[0]}
    for d in range(1, planes):
        part[planes - d] = shift(plane_parts[d], d)
    ids_again = after(ids_again, *plane_parts)

    all_ids = lax.all_to_all(jnp.broadcast_to(ids_again, (owners, tokens)), "adapter", 0, 0, tiled=True)

    def placing(block_ids):
        owner = block_ids // per_owner
        earlier = jnp.arange(tokens)[:, None] > jnp.arange(tokens)[None, :]
        same = owner[..., :, None] == owner[..., None, :]
        place = jnp.sum((same & earlier).astype(I32), axis=-1)
        return owner, place

    owner, place = placing(ids)
    slot = owner * capacity + place
    slot_here = jnp.concatenate(
        [lax.dynamic_slice_in_dim(slot, (tensor ^ k) * sub, sub, 0) for k in range(tensors)]
    )
    down_t = down.T
    grad_packed = pack_rows(slot_here.reshape(1, -1), after(grad_rows, down_t), slot_count)

    def to_owners(x):
        x = x.reshape(owners, capacity, width)
        return lax.all_to_all(x, "adapter", 0, 0, tiled=True).reshape(slot_count, width)

    grad_packed = after(grad_packed, *(part[d] for d in range(1, planes)))
    grad_slots = to_owners(grad_packed)

    halves = [jnp.stack([part[d] for d in order[i * half : (i + 1) * half]], axis=0) for i in range(2)]
    bits = [1 << i for i in range(tensors.bit_length() - 1)]
    plane_rows = [{0: halves[0]}, {0: halves[1]}]
    for step in zip(bits, reversed(bits)):
        for rows, bit in zip(plane_rows, step):
            rows.update({k ^ bit: flip(x, bit) for k, x in list(rows.items())})
    plane_rows = [rows[k] for rows in plane_rows for k in range(tensors)]
    other_weight = swap(weight)
    other_down_t = swap(down_t)

    all_owner, all_place = placing(all_ids)
    ahead = [2 * ((plane + jnp.arange(planes)) % planes) + c for c in (core, 1 - core)]
    slot_order = jnp.concatenate(ahead)

    def labels(owner, blocks):
        mine = (all_owner[blocks] == owner)[:, None, :]
        mine &= all_place[blocks][:, None, :] == jnp.arange(capacity, dtype=I32)[:, None]
        from_first = all_ids[blocks][:, None, :] - owner * per_owner
        return (jnp.sum(jnp.where(mine, from_first + 1, 0), axis=-1) - 1).reshape(1, -1)

    here, there = (labels(me, blocks) for blocks in ahead)
    local = jnp.concatenate([here, there], axis=1)
    parity_local = jnp.concatenate([here, labels(me ^ 1, ahead[0])], axis=0)

    parity_ids, parity_owner, parity_place = (x[ahead[0]] for x in (all_ids, all_owner, all_place))
    attn_places = jnp.where(parity_owner == me, parity_place, -1)
    attn_places = jnp.where(parity_owner == (me ^ 1), parity_place + capacity, attn_places).reshape(1, -1)
    base = capacity * jnp.arange(planes, dtype=I32)[:, None]
    places = jnp.stack(
        [
            jnp.where(parity_owner == me, parity_place + base, -1),
            jnp.where(parity_owner == (me ^ 1), parity_place + base + planes * capacity, -1),
            parity_ids - me * per_owner,
            parity_ids - (me ^ 1) * per_owner,
        ]
    )
    places = jnp.concatenate([places[:, d : d + 1] for d in order], axis=1).reshape(4, -1)

    first_weight = after(weight, places, local, parity_local, attn_places, slot_order, other_down_t)
    attn_start = after(attn, *plane_rows)
    going_down, going_up = attn_line(attn_start, 1, -1), attn_line(attn_start, 1, 1)
    frozen = frozen_part(tensor, (first_weight, other_weight), plane_rows)
    grad_slots = after(grad_slots, frozen)
    low_grads = token_ranks(slot_order, local, up, grad_slots, per_owner)
    low_grads = sum([flip(low_grads, k) for k in range(1, tensors)], low_grads)
    grad_low = (ADAPTER_SCALE * low_grads).astype(BF16)
    ranks = (grad_low, swap(grad_low))
    downs = (down_t, other_down_t)

    def with_term(i, types):
        return add_term(frozen, i, half * tokens, places, ranks, downs, per_owner, types)

    pairs = with_term(0, [BF16] * planes)
    below, above = [going_down], [going_up]
    for d in range(2, planes):
        if d == 2:
            going_down, going_up = after((going_down, going_up), *pairs)
        going_down, going_up = attn_line(going_down, d, -1), attn_line(going_up, d, 1)
        below.append(going_down)
        above.append(going_up)
    pairs += with_term(1, [BF16] * (planes - 2) + [F32] * 2)
    sums = {d: pairs[2 * i : 2 * i + 2] for i, d in enumerate(order)}
    attn_own, attn_other, parity_inputs = repack(
        plane, attn_places, parity_local, downs, attn, below, above, capacity, per_owner
    )
    attn_slots = [attn_own, swap(attn_other)]
    going_up, going_down = [None, None], [None, None]
    for d in range(planes - 1, 0, -1):
        for i in range(2):
            up_sum, down_sum = sums[d][i], sums[planes - d][i]
            if d == 1 and i == 1:
                up_sum, down_sum = after((up_sum, down_sum), parity_inputs)
            if going_up[i] is not None:
                up_sum = (up_sum.astype(F32) + going_up[i].astype(F32)).astype(BF16)
                down_sum = (down_sum.astype(F32) + going_down[i].astype(F32)).astype(BF16)
            going_up[i], going_down[i] = up_line(up_sum, d), down_line(down_sum, d)
    total = [x + up_sum.astype(F32) + down_sum.astype(F32) for x, up_sum, down_sum in zip(sums[0], going_up, going_down)]
    attention_output_gradient = jnp.concatenate(total, axis=0).astype(BF16)

    low_inputs = sum([flip(parity_inputs, k) for k in range(1, tensors)], parity_inputs)
    up_scaled = (ADAPTER_SCALE * low_inputs).astype(BF16)
    up_scaled = jnp.concatenate([up_scaled[0], swap(up_scaled[1])], axis=1)
    down_grad, up_grad = adapter_gradients(slot_order, local, grad_low, up_scaled, attn_slots, grad_slots, per_owner)
    return attention_output_gradient, down_grad, up_grad


def solution(mesh):
    placed = (
        P("adapter", "tensor"),
        P(("adapter", "tensor"), None),
        P("adapter"),
        P("tensor", "adapter"),
        P("tensor", "adapter"),
        P("adapter", "tensor"),
    )
    return jax.shard_map(
        per_device,
        mesh=mesh,
        in_specs=placed,
        out_specs=(P("adapter", "tensor"), P("tensor", "adapter"), P("adapter", "tensor")),
        check_vma=False,
    )
```

time: 536 us -> 237 us (0.44)
  waiting for transfers between devices: 432 us -> 77.7 us
  Pallas kernels: 0 us -> 56 us
  starting transfers between devices: 20.4 us -> 69.8 us
  matrix products: 39.4 us -> 0 us
  between operations: 15.7 us -> 1.56 us
  other arithmetic: 3.94 us -> 15.3 us
  local copies, waits for them, and re-layouts: 23.8 us -> 15.8 us
    all_gather x2 -> x0, waiting for transfers between devices: 204 us -> none  [the longest x1 172 us: per_device(): lax.all_gather(base_weight, 'adapter', axis=1, tiled=True)]
    all_to_all x4 -> x2, waiting for transfers between devices: 187 us -> 0.01 us  [the longest x1 0.01 us: per_device(): lax.all_to_all(jnp.broadcast_to(ids_again, (owners, tokens)), 'adapter',...]
    ppermute x0 -> x41, waiting for transfers between devices: none -> 77.7 us  [the longest x15 40.2 us: flip(): return lax.ppermute(x, 'tensor', [(t, t ^ k) for t in range(tensors)])]
    ppermute x0 -> x41, starting transfers between devices: none -> 62.6 us  [the longest x6 22.6 us: up_line(): return lax.ppermute(x, 'adapter', pairs)]
    pallas_call x0 -> x7, Pallas kernels: none -> 56 us  [the longest x1 14.9 us: frozen_part(): pl.pallas_call(frozen_kernel, grid=(width // tile,), out_shape=jax.ShapeD...]
    psum x1 -> x0, waiting for transfers between devices: 39.7 us -> none  [per_device(): lax.psum((rank_inputs, rank_gradients), 'tensor')]
    dot_general x6 -> x0, matrix products: 39.4 us -> none  [the longest x1 17.2 us: per_device(): lax.dot_general(full_grad, lax.all_gather(base_weight, 'adapter', axis=1,...]
    all_to_all x4 -> x2, starting transfers between devices: 20.3 us -> 7.18 us  [the longest x1 3.77 us: to_owners(): lax.all_to_all(x, 'adapter', 0, 0, tiled=True).reshape(slot_count, width)]
  transfers between devices with their start and end apart: 7 -> 43, of which waited for: 7 -> 19; matrix products, arithmetic and copies ran while one was open for 8% -> 10% of each run, Pallas kernels for 0% -> 19%
where the time goes in v2:
time: 237 us; the launch traced here: 236 us
  waiting for transfers between devices  77.7 us (33%)
  starting transfers between devices  69.8 us (29%)
  Pallas kernels  56 us (24%)
  local copies, waits for them, and re-layouts  15.8 us (7%)
  other arithmetic  15.3 us (6%)
    ppermute x15, waiting for transfers between devices, flip(): return lax.ppermute(x, 'tensor', [(t, t ^ k) for t in range(tensors)])  40.2 us
    ppermute x6, starting transfers between devices, up_line(): return lax.ppermute(x, 'adapter', pairs)  22.6 us
    ppermute x15, starting transfers between devices, flip(): return lax.ppermute(x, 'tensor', [(t, t ^ k) for t in range(tensors)])  17.2 us
    pallas_call x1, Pallas kernels, frozen_part(): pl.pallas_call(frozen_kernel, grid=(width // tile,), out_shape=jax.ShapeD...  14.9 us
    ppermute x6, waiting for transfers between devices, up_line(): return lax.ppermute(x, 'adapter', pairs)  14.7 us
    ppermute x6, waiting for transfers between devices, attn_line(): lax.ppermute(x, 'adapter', [(2 * z + c, 2 * (z + way) + c) for z in plane...  14.3 us
    pallas_call x2, Pallas kernels, add_term(): pl.pallas_call(functools.partial(term_kernel, per_owner), grid=(width //...  14.2 us
    ppermute x6, starting transfers between devices, attn_line(): lax.ppermute(x, 'adapter', [(2 * z + c, 2 * (z + way) + c) for z in plane...  11 us
  transfers between devices with their start and end apart: 43, of which 19 were waited for; matrix products, arithmetic and copies ran while one was open for 10% of the time, Pallas kernels for 19%

profile of v2, /device:TPU:0, one launch (start us, length us, event | category | flops | bytes accessed | tf_op | source)
XLA Modules:
  0.0 236.2 jit_solution(18273403279327484882)
XLA Ops:
  0.7 2.2 constant_dynamic-slice_fusion.8
  2.8 2.9 %collective-permute-start.11 = (bf16[64,2048]{1,0:T(8,128)(2,1)}, bf16[64,2048]{1,0:T(8,128)(2,1)}, u32[]{:S(2)}, u32[]{:S(2)}) collective-permute-start(bf16[64,2048]{1,0:T(8,128)(2,1)} %get-tuple-element.74), channel_id=1, source_target_pairs={{0,1},{1,0},{2,3},{3,2},{4,5},{5,4},{6,7},{7,6},{8,9},{9,8},{10,11... | collective-permute-start | bytes 786440 | tf_op jit(solution)/shard_map/ppermute | solution.py:353
  5.8 1.5 collective-permute-start.12
  7.3 0.7 constant_dynamic-slice_fusion.7
  8.1 1.6 collective-permute-start.3
  9.7 2.3 collective-permute-start.2
  12.0 0.9 collective-permute-start.7
  13.5 3.4 %all-to-all-start = ((s32[8,1,256]{2,1,0:T(1,128)}), s32[8,1,256]{2,1,0:T(1,128)S(1)}, u32[]{:S(2)}, u32[]{:S(2)}) async-start(s32[8,1,256]{2,1,0:T(1,128)} %broadcast_in_dim.33), calls=%async_computation | async-start | bytes 16384 | tf_op jit(solution)/shard_map/all_to_all | solution.py:380
  19.5 2.4 %copy.11 = bf16[2048,512]{0,1:T(8,128)(2,1)} copy(bf16[2048,512]{1,0:T(8,128)(2,1)S(1)} %copy-done.3) | data formatting | bytes 4194304 | tf_op args[4]
  22.0 5.5 %collective-permute-done.13.refs_3_ = bf16[64,2048]{1,0:T(8,128)(2,1)} collective-permute-done((bf16[64,2048]{1,0:T(8,128)(2,1)S(1)}, bf16[64,2048]{1,0:T(8,128)(2,1)}, u32[]{:S(2)}, u32[]{:S(2)}) %collective-permute-start.13) | collective-permute-done | bytes 262176 | tf_op jit(solution)/shard_map/ppermute | solution.py:353
  27.5 3.2 %pack_rows.1 = bf16[640,2048]{1,0:T(8,128)(2,1)} custom-call(s32[1,256]{1,0:T(1,128)} %bitcast.72, bf16[64,2048]{1,0:T(8,128)(2,1)} %get-tuple-element.35.refs_0_, bf16[64,2048]{1,0:T(8,128)(2,1)} %collective-permute-done.11.refs_1_, bf16[64,2048]{1,0:T(8,128)(2,1)} %collective-permute-done.12.refs_2_, bf16[64,2048]{1,0:T(8,128)(2,1)} %collective-permute-done.13.refs_3_), custom_call_target="tpu_custom_call" | custom-call | flops 10485760 | bytes 57344 | tf_op jit(solution)/shard_map/pack_rows/pallas_call | solution.py:43
  30.7 3.8 %collective-permute-done.7 = bf16[64,2048]{1,0:T(8,128)(2,1)} collective-permute-done((bf16[64,2048]{1,0:T(8,128)(2,1)S(1)}, bf16[64,2048]{1,0:T(8,128)(2,1)}, u32[]{:S(2)}, u32[]{:S(2)}) %collective-permute-start.7) | collective-permute-done | bytes 262176 | tf_op jit(solution)/shard_map/ppermute | solution.py:335
  34.6 3.8 %all-to-all-start.1 = ((bf16[8,80,2048]{2,1,0:T(8,128)(2,1)}), bf16[8,80,2048]{2,1,0:T(8,128)(2,1)S(1)}, u32[]{:S(2)}, u32[]{:S(2)}) async-start(bf16[8,80,2048]{2,1,0:T(8,128)(2,1)} %bitcast.64), calls=%async_computation.1 | async-start | bytes 5242880 | tf_op jit(solution)/shard_map/all_to_all | solution.py:399
  40.4 0.8 convert_reduce_fusion
  43.5 1.1 pad_maximum_fusion.1.refs_0_
  45.7 1.8 pad_maximum_fusion.2.refs_4_
  47.5 1.5 collective-permute-start.9
  49.7 9.3 %collective-permute-done.4.refs_1_ = bf16[2,64,2048]{2,1,0:T(8,128)(2,1)} collective-permute-done((bf16[2,64,2048]{2,1,0:T(8,128)(2,1)S(1)}, bf16[2,64,2048]{2,1,0:T(8,128)(2,1)}, u32[]{:S(2)}, u32[]{:S(2)}) %collective-permute-start.4) | collective-permute-done | bytes 524320 | tf_op jit(solution)/shard_map/ppermute | solution.py:353
  60.0 0.8 copy-done.14
  61.3 10.0 %collective-permute-done.9.refs_6_ = bf16[2,64,2048]{2,1,0:T(8,128)(2,1)} collective-permute-done((bf16[2,64,2048]{2,1,0:T(8,128)(2,1)}, bf16[2,64,2048]{2,1,0:T(8,128)(2,1)}, u32[]{:S(2)}, u32[]{:S(2)}) %collective-permute-start.9) | collective-permute-done | bytes 524320 | tf_op jit(solution)/shard_map/ppermute | solution.py:353
  71.4 1.5 collective-permute-start.10
  73.1 8.6 %collective-permute-done.6.refs_3_ = bf16[2,64,2048]{2,1,0:T(8,128)(2,1)} collective-permute-done((bf16[2,64,2048]{2,1,0:T(8,128)(2,1)}, bf16[2,64,2048]{2,1,0:T(8,128)(2,1)}, u32[]{:S(2)}, u32[]{:S(2)}) %collective-permute-start.6) | collective-permute-done | bytes 524320 | tf_op jit(solution)/shard_map/ppermute | solution.py:353
  81.7 2.2 collective-permute-done.10.refs_7_
  83.9 1.3 collective-permute-start.24
  85.2 5.5 %collective-permute-start.25 = (bf16[256,2048]{1,0:T(8,128)(2,1)}, bf16[256,2048]{1,0:T(8,128)(2,1)}, u32[]{:S(2)}, u32[]{:S(2)}) collective-permute-start(bf16[256,2048]{1,0:T(8,128)(2,1)} %refs_0_.1), channel_id=1, source_target_pairs={{0,8},{4,12},{8,16},{12,20},{16,24},{20,28},{1,9},{5,13},{9,17},{1... | collective-permute-start | bytes 3145736 | tf_op jit(solution)/shard_map/ppermute | solution.py:347
  93.1 14.9 %frozen_part.1.frozen_ref = f32[1024,2048]{1,0:T(8,128)} custom-call(s32[1]{0:T(128)} %bitcast.place_ref, bf16[2048,1024]{1,0:T(8,128)(2,1)} %own_w_ref, bf16[2048,1024]{1,0:T(8,128)(2,1)} %collective-permute-done.1.other_w_ref, bf16[2,64,2048]{2,1,0:T(8,128)(2,1)} %copy-done.2, bf16[2,64,2048]{2,1,0:T(8,128)(2,1)} %collective-permute-done.4.refs_1_, ...), custom_call_target="tpu_custom_call" | custom-call | flops 134217728 | bytes 262144 | tf_op jit(solution)/shard_map/frozen_part/pallas_call | solution.py:208
  108.0 1.5 copy-done
  109.5 6.4 %token_ranks.1 = f32[16,640]{1,0:T(8,128)} custom-call(s32[8]{0:T(128)} %pad_add_fusion.4.order_ref, s32[1,640]{1,0:T(1,128)} %pad_add_fusion.2.local_ref, bf16[512,2048]{1,0:T(8,128)(2,1)} %weight_ref.1, bf16[640,2048]{1,0:T(8,128)(2,1)} %bitcast.48, bf16[640,2048]{1,0:T(8,128)(2,1)} %bitcast.49, bf16[640,2048]{1,0:T(8,128)(2,1)} %bitcast.50, ...), custom_call_target="tpu_custom_call" | custom-call | flops 20971520 | bytes 73728 | tf_op jit(solution)/shard_map/token_ranks/pallas_call | solution.py:153
  115.9 1.4 collective-permute-start.16
  117.2 1.5 collective-permute-start.15
  119.4 1.6 collective-permute-done.16
  121.5 1.5 collective-permute-done.14
  123.0 0.8 multiply_convert_fusion.1.refs_0_.grad_ranks_ref
  123.9 1.2 collective-permute-done.17.refs_1_
  125.6 6.9 %add_term.3 = (bf16[128,2048]{1,0:T(8,128)(2,1)}, bf16[128,2048]{1,0:T(8,128)(2,1)}, bf16[128,2048]{1,0:T(8,128)(2,1)}, bf16[128,2048]{1,0:T(8,128)(2,1)}) custom-call(f32[1024,2048]{1,0:T(8,128)} %frozen_part.1.frozen_ref, s32[4,1024]{1,0:T(4,128)} %bitcast.68, bf16[16,640]{1,0:T(8,128)(2,1)} %copy-done.18, bf16[16,640]{1,0:T(8,128)(2,1)} %copy-done.20, ...), custom_call_target="tpu_custom_call" | custom-call | flops 33554432 | bytes 163840 | tf_op jit(solution)/shard_map/add_term/pallas_call | solution.py:253
  132.6 1.4 collective-permute-start.26
  134.7 6.3 %collective-permute-start.18 = (bf16[128,2048]{1,0:T(8,128)(2,1)}, bf16[128,2048]{1,0:T(8,128)(2,1)S(1)}, u32[]{:S(2)}, u32[]{:S(2)}) collective-permute-start(bf16[128,2048]{1,0:T(8,128)(2,1)} %get-tuple-element.44), channel_id=1, source_target_pairs={{0,8},{4,12},{1,9},{5,13},{2,10},{6,14},{3,11},{7,15}} | collective-permute-start | bytes 1572872 | tf_op jit(solution)/shard_map/ppermute | solution.py:339
  141.8 1.3 collective-permute-start.30
  143.1 7.3 %add_term.2 = (bf16[128,2048]{1,0:T(8,128)(2,1)}, bf16[128,2048]{1,0:T(8,128)(2,1)}, f32[128,2048]{1,0:T(8,128)}, f32[128,2048]{1,0:T(8,128)}) custom-call(f32[1024,2048]{1,0:T(8,128)} %frozen_part.1.frozen_ref, s32[4,1024]{1,0:T(4,128)} %bitcast.69, bf16[16,640]{1,0:T(8,128)(2,1)} %copy-done.18, bf16[16,640]{1,0:T(8,128)(2,1)} %copy-done.20, ...), custom_call_target="tpu_custom_call" | custom-call | flops 33554432 | bytes 163840 | tf_op jit(solution)/shard_map/add_term/pallas_call | solution.py:253
  150.4 3.3 %collective-permute-done.18 = bf16[128,2048]{1,0:T(8,128)(2,1)S(1)} collective-permute-done((bf16[128,2048]{1,0:T(8,128)(2,1)}, bf16[128,2048]{1,0:T(8,128)(2,1)S(1)}, u32[]{:S(2)}, u32[]{:S(2)}) %collective-permute-start.18) | collective-permute-done | bytes 524320 | tf_op jit(solution)/shard_map/ppermute | solution.py:339
  154.4 1.4 fusion
  156.5 7.1 %collective-permute-done.30 = bf16[128,2048]{1,0:T(8,128)(2,1)S(1)} collective-permute-done((bf16[128,2048]{1,0:T(8,128)(2,1)}, bf16[128,2048]{1,0:T(8,128)(2,1)S(1)}, u32[]{:S(2)}, u32[]{:S(2)}) %collective-permute-start.30) | collective-permute-done | bytes 524320 | tf_op jit(solution)/shard_map/ppermute | solution.py:339
  163.6 4.3 %collective-permute-start.19 = (bf16[128,2048]{1,0:T(8,128)(2,1)S(1)}, bf16[128,2048]{1,0:T(8,128)(2,1)S(1)}, u32[]{:S(2)}, u32[]{:S(2)}) collective-permute-start(bf16[128,2048]{1,0:T(8,128)(2,1)S(1)} %get-tuple-element.76), channel_id=1, source_target_pairs={{0,8},{4,12},{8,16},{12,20},{1,9},{5,13},{9,17},{13,21},{2,10},{6,... | collective-permute-start | bytes 1572872 | tf_op jit(solution)/shard_map/ppermute | solution.py:339
  167.9 1.3 collective-permute-start.27
  170.0 1.1 fusion.2
  171.1 1.5 collective-permute-start.34
  172.6 4.6 %collective-permute-start.31 = (bf16[128,2048]{1,0:T(8,128)(2,1)S(1)}, bf16[128,2048]{1,0:T(8,128)(2,1)S(1)}, u32[]{:S(2)}, u32[]{:S(2)}) collective-permute-start(bf16[128,2048]{1,0:T(8,128)(2,1)S(1)} %get-tuple-element.78), channel_id=1, source_target_pairs={{0,8},{4,12},{8,16},{12,20},{1,9},{5,13},{9,17},{13,21},{2,10},{6,... | collective-permute-start | bytes 1572872 | tf_op jit(solution)/shard_map/ppermute | solution.py:339
  177.4 2.8 %collective-permute-done.19 = bf16[128,2048]{1,0:T(8,128)(2,1)S(1)} collective-permute-done((bf16[128,2048]{1,0:T(8,128)(2,1)S(1)}, bf16[128,2048]{1,0:T(8,128)(2,1)S(1)}, u32[]{:S(2)}, u32[]{:S(2)}) %collective-permute-start.19) | collective-permute-done | bytes 524320 | tf_op jit(solution)/shard_map/ppermute | solution.py:339
  180.3 1.3 collective-permute-start.23
  181.7 14.2 %collective-permute-done.27.refs_3_ = bf16[256,2048]{1,0:T(8,128)(2,1)S(1)} collective-permute-done((bf16[256,2048]{1,0:T(8,128)(2,1)S(1)}, bf16[256,2048]{1,0:T(8,128)(2,1)S(1)}, u32[]{:S(2)}, u32[]{:S(2)}) %collective-permute-start.27) | collective-permute-done | bytes 1048608 | tf_op jit(solution)/shard_map/ppermute | solution.py:347
  195.9 1.5 collective-permute-start.20
  197.4 0.9 copy-done.8
  198.4 6.8 %repack.1 = (bf16[320,2048]{1,0:T(8,128)(2,1)}, bf16[320,2048]{1,0:T(8,128)(2,1)}, f32[2,16,320]{2,1,0:T(8,128)}) custom-call(s32[1]{0:T(128)} %bitcast.16.plane_ref, s32[1,1024]{1,0:T(1,128)} %bitcast.71, s32[2,320]{1,0:T(2,128)} %pad_add_fusion.1.local_ref, bf16[512,2048]{1,0:T(8,128)(2,1)} %bitcast.8.refs_2_.own_d_ref, ...), custom_call_target="tpu_custom_call" | custom-call | flops 31457280 | bytes 106496 | tf_op jit(solution)/shard_map/repack/pallas_call | solution.py:107
  205.9 1.5 collective-permute-start.37
  207.4 1.2 add_convert_fusion.1
  208.6 1.5 collective-permute-start.36
  210.6 1.3 collective-permute-start.35
  211.9 4.6 %collective-permute-start.32 = (bf16[128,2048]{1,0:T(8,128)(2,1)S(1)}, bf16[128,2048]{1,0:T(8,128)(2,1)S(1)}, u32[]{:S(2)}, u32[]{:S(2)}) collective-permute-start(bf16[128,2048]{1,0:T(8,128)(2,1)S(1)} %add_convert_fusion.2), channel_id=1, source_target_pairs={{0,8},{4,12},{8,16},{12,20},{16,24},{20,28},{1,9},{5,13},{9,17},{1... | collective-permute-start | bytes 1572872 | tf_op jit(solution)/shard_map/ppermute | solution.py:339
  217.4 2.2 collective-permute-done.39
  220.4 1.3 collective-permute-done.35
  221.7 1.5 collective-permute-done.32
  223.4 1.1 pad_maximum_fusion
  224.5 1.1 copy-done.4
  225.5 10.5 %adapter_gradients.1 = (f32[2048,512]{1,0:T(8,128)}, f32[512,2048]{1,0:T(8,128)}) custom-call(s32[8]{0:T(128)} %pad_add_fusion.4.order_ref, s32[1,640]{1,0:T(1,128)} %pad_add_fusion.2.local_ref, bf16[16,640]{1,0:T(8,128)(2,1)} %copy-done.18, bf16[16,640]{1,0:T(8,128)(2,1)} %pad_maximum_fusion.7.up_ranks_ref, bf16[320,2048]{1,0:T(8,128)(2,1)} %get-tuple-element.55.own_ref, ...), custom_call_target="tpu_custom_call" | custom-call | flops 41943040 | bytes 212992 | tf_op jit(solution)/shard_map/adapter_gradients/pallas_call | solution.py:293
  (149 shorter events, 22.0 us)
Async XLA Ops:
  0.6 6.7 %copy-start.1 = (bf16[64,8192]{1,0:T(8,128)(2,1)S(1)}, bf16[64,8192]{1,0:T(8,128)(2,1)}, u32[]{:S(2)}) copy-start(bf16[64,8192]{1,0:T(8,128)(2,1)} %param.7) | copy-start | bytes 3145732
  2.8 10.1 %copy-start.22 = (s32[256]{0:T(256)S(1)}, s32[256]{0:T(256)}, u32[]{:S(2)}) copy-start(s32[256]{0:T(256)} %param.8) | copy-start | bytes 3076
  2.8 16.7 %copy-start.3 = (bf16[2048,512]{1,0:T(8,128)(2,1)S(1)}, bf16[2048,512]{1,0:T(8,128)(2,1)}, u32[]{:S(2)}) copy-start(bf16[2048,512]{1,0:T(8,128)(2,1)} %param.10) | copy-start | bytes 6291460
  2.8 14.9 %collective-permute-start.11 = (bf16[64,2048]{1,0:T(8,128)(2,1)}, bf16[64,2048]{1,0:T(8,128)(2,1)}, u32[]{:S(2)}, u32[]{:S(2)}) collective-permute-start(bf16[64,2048]{1,0:T(8,128)(2,1)} %get-tuple-element.74), channel_id=1, source_target_pairs={{0,1},{1,0},{2,3},{3,2},{4,5},{5,4},{6,7},{7,6},{8,9},{9,8},{10,11... | collective-permute-start | bytes 786440 | tf_op jit(solution)/shard_map/ppermute | solution.py:353
  5.8 16.1 %collective-permute-start.12 = (bf16[64,2048]{1,0:T(8,128)(2,1)}, bf16[64,2048]{1,0:T(8,128)(2,1)}, u32[]{:S(2)}, u32[]{:S(2)}) collective-permute-start(bf16[64,2048]{1,0:T(8,128)(2,1)} %get-tuple-element.73), channel_id=1, source_target_pairs={{0,2},{1,3},{2,0},{3,1},{4,6},{5,7},{6,4},{7,5},{8,10},{9,11},{10,... | collective-permute-start | bytes 786440 | tf_op jit(solution)/shard_map/ppermute | solution.py:353
  8.1 22.6 %collective-permute-start.3 = (bf16[64,2048]{1,0:T(8,128)(2,1)S(1)}, bf16[64,2048]{1,0:T(8,128)(2,1)S(1)}, u32[]{:S(2)}, u32[]{:S(2)}) collective-permute-start(bf16[64,2048]{1,0:T(8,128)(2,1)S(1)} %pad_maximum_fusion.4), channel_id=1, source_target_pairs={{0,8},{4,12},{8,16},{12,20},{16,24},{20,28},{24,0},{28,4},{1,9},{5... | collective-permute-start | bytes 786440 | tf_op jit(solution)/shard_map/ppermute | solution.py:335
  9.7 21.0 %collective-permute-start.2 = (bf16[64,2048]{1,0:T(8,128)(2,1)S(1)}, bf16[64,2048]{1,0:T(8,128)(2,1)}, u32[]{:S(2)}, u32[]{:S(2)}) collective-permute-start(bf16[64,2048]{1,0:T(8,128)(2,1)S(1)} %pad_maximum_fusion.6), channel_id=1, source_target_pairs={{0,24},{4,28},{8,0},{12,4},{16,8},{20,12},{24,16},{28,20},{1,25},{... | collective-permute-start | bytes 786440 | tf_op jit(solution)/shard_map/ppermute | solution.py:335
  12.0 22.5 %collective-permute-start.7 = (bf16[64,2048]{1,0:T(8,128)(2,1)S(1)}, bf16[64,2048]{1,0:T(8,128)(2,1)}, u32[]{:S(2)}, u32[]{:S(2)}) collective-permute-start(bf16[64,2048]{1,0:T(8,128)(2,1)S(1)} %pad_maximum_fusion.5), channel_id=1, source_target_pairs={{0,16},{4,20},{8,24},{12,28},{16,0},{20,4},{24,8},{28,12},{1,17},{... | collective-permute-start | bytes 786440 | tf_op jit(solution)/shard_map/ppermute | solution.py:335
  13.5 21.1 %all-to-all-start = ((s32[8,1,256]{2,1,0:T(1,128)}), s32[8,1,256]{2,1,0:T(1,128)S(1)}, u32[]{:S(2)}, u32[]{:S(2)}) async-start(s32[8,1,256]{2,1,0:T(1,128)} %broadcast_in_dim.33), calls=%async_computation | async-start | bytes 16384 | tf_op jit(solution)/shard_map/all_to_all | solution.py:380
  17.7 9.8 %collective-permute-start.13 = (bf16[64,2048]{1,0:T(8,128)(2,1)S(1)}, bf16[64,2048]{1,0:T(8,128)(2,1)}, u32[]{:S(2)}, u32[]{:S(2)}) collective-permute-start(bf16[64,2048]{1,0:T(8,128)(2,1)S(1)} %get-tuple-element.72), channel_id=1, source_target_pairs={{0,3},{1,2},{2,1},{3,0},{4,7},{5,6},{6,5},{7,4},{8,11},{9,10},{10,... | collective-permute-start | bytes 786440 | tf_op jit(solution)/shard_map/ppermute | solution.py:353
  21.9 71.2 %collective-permute-start = (bf16[512,2048]{1,0:T(8,128)(2,1)}, bf16[512,2048]{1,0:T(8,128)(2,1)}, u32[]{:S(2)}, u32[]{:S(2)}) collective-permute-start(bf16[512,2048]{1,0:T(8,128)(2,1)} %bitcast.8.refs_2_.own_d_ref), channel_id=1, source_target_pairs={{0,4},{4,0},{8,12},{12,8},{16,20},{20,16},{24,28},{28,24},{1,5},{5... | collective-permute-start | bytes 6291464 | tf_op jit(solution)/shard_map/ppermute | solution.py:350
  27.5 65.6 %collective-permute-start.1 = (bf16[2048,1024]{1,0:T(8,128)(2,1)}, bf16[2048,1024]{1,0:T(8,128)(2,1)}, u32[]{:S(2)}, u32[]{:S(2)}) collective-permute-start(bf16[2048,1024]{1,0:T(8,128)(2,1)} %own_w_ref), channel_id=1, source_target_pairs={{0,4},{4,0},{8,12},{12,8},{16,20},{20,16},{24,28},{28,24},{1,5},{5... | collective-permute-start | bytes 12582920 | tf_op jit(solution)/shard_map/ppermute | solution.py:350
  30.7 3.9 %copy-start.19 = (bf16[64,2048]{1,0:T(8,128)(2,1)}, bf16[64,2048]{1,0:T(8,128)(2,1)S(1)}, u32[]{:S(2)}) copy-start(bf16[64,2048]{1,0:T(8,128)(2,1)S(1)} %collective-permute-done.3) | copy-start | bytes 786436
  34.6 3.8 %copy-start.24 = (s32[4]{0:T(128)S(1)}, s32[4]{0:T(128)}, u32[]{:S(2)}) copy-start(s32[4]{0:T(128)} %get-tuple-element.96) | copy-start | bytes 52
  34.6 3.8 %copy-start.23 = (s32[4]{0:T(128)S(1)}, s32[4]{0:T(128)}, u32[]{:S(2)}) copy-start(s32[4]{0:T(128)} %get-tuple-element.97) | copy-start | bytes 52
  34.6 3.9 %copy-start.25 = (s32[4]{0:T(128)S(1)}, s32[4]{0:T(128)}, u32[]{:S(2)}) copy-start(s32[4]{0:T(128)} %get-tuple-element.99) | copy-start | bytes 52
  34.6 4.5 %copy-start.17 = (bf16[64,1024]{1,0:T(8,128)(2,1)S(1)}, bf16[64,1024]{1,0:T(8,128)(2,1)}, u32[]{:S(2)}) copy-start(bf16[64,1024]{1,0:T(8,128)(2,1)} %get-tuple-element.71) | copy-start | bytes 393220
  34.6 73.4 %all-to-all-start.1 = ((bf16[8,80,2048]{2,1,0:T(8,128)(2,1)}), bf16[8,80,2048]{2,1,0:T(8,128)(2,1)S(1)}, u32[]{:S(2)}, u32[]{:S(2)}) async-start(bf16[8,80,2048]{2,1,0:T(8,128)(2,1)} %bitcast.64), calls=%async_computation.1 | async-start | bytes 5242880 | tf_op jit(solution)/shard_map/all_to_all | solution.py:399
  44.6 48.5 %copy-start.2 = (bf16[2,64,2048]{2,1,0:T(8,128)(2,1)}, bf16[2,64,2048]{2,1,0:T(8,128)(2,1)S(1)}, u32[]{:S(2)}) copy-start(bf16[2,64,2048]{2,1,0:T(8,128)(2,1)S(1)} %pad_maximum_fusion.1.refs_0_) | copy-start | bytes 1572868
  44.6 14.4 %collective-permute-start.4 = (bf16[2,64,2048]{2,1,0:T(8,128)(2,1)S(1)}, bf16[2,64,2048]{2,1,0:T(8,128)(2,1)}, u32[]{:S(2)}, u32[]{:S(2)}) collective-permute-start(bf16[2,64,2048]{2,1,0:T(8,128)(2,1)S(1)} %pad_maximum_fusion.1.refs_0_), channel_id=1, source_target_pairs={{0,1},{1,0},{2,3},{3,2},{4,5},{5,4},{6,7},{7,6},{8,9},{9,8},{10,11... | collective-permute-start | bytes 1572872 | tf_op jit(solution)/shard_map/ppermute | solution.py:353
  45.2 14.8 %collective-permute-start.5 = (bf16[2,64,2048]{2,1,0:T(8,128)(2,1)S(1)}, bf16[2,64,2048]{2,1,0:T(8,128)(2,1)S(1)}, u32[]{:S(2)}, u32[]{:S(2)}) collective-permute-start(bf16[2,64,2048]{2,1,0:T(8,128)(2,1)S(1)} %pad_maximum_fusion.1.refs_0_), channel_id=1, source_target_pairs={{0,2},{1,3},{2,0},{3,1},{4,6},{5,7},{6,4},{7,5},{8,10},{9,11},{10,... | collective-permute-start | bytes 1572872 | tf_op jit(solution)/shard_map/ppermute | solution.py:353
  47.5 23.8 %collective-permute-start.9 = (bf16[2,64,2048]{2,1,0:T(8,128)(2,1)}, bf16[2,64,2048]{2,1,0:T(8,128)(2,1)}, u32[]{:S(2)}, u32[]{:S(2)}) collective-permute-start(bf16[2,64,2048]{2,1,0:T(8,128)(2,1)} %pad_maximum_fusion.2.refs_4_), channel_id=1, source_target_pairs={{0,2},{1,3},{2,0},{3,1},{4,6},{5,7},{6,4},{7,5},{8,10},{9,11},{10,... | collective-permute-start | bytes 1572872 | tf_op jit(solution)/shard_map/ppermute | solution.py:353
  59.0 14.1 %collective-permute-start.8 = (bf16[2,64,2048]{2,1,0:T(8,128)(2,1)}, bf16[2,64,2048]{2,1,0:T(8,128)(2,1)}, u32[]{:S(2)}, u32[]{:S(2)}) collective-permute-start(bf16[2,64,2048]{2,1,0:T(8,128)(2,1)} %pad_maximum_fusion.2.refs_4_), channel_id=1, source_target_pairs={{0,1},{1,0},{2,3},{3,2},{4,5},{5,4},{6,7},{7,6},{8,9},{9,8},{10,11... | collective-permute-start | bytes 1572872 | tf_op jit(solution)/shard_map/ppermute | solution.py:353
  60.8 20.9 %collective-permute-start.6 = (bf16[2,64,2048]{2,1,0:T(8,128)(2,1)}, bf16[2,64,2048]{2,1,0:T(8,128)(2,1)}, u32[]{:S(2)}, u32[]{:S(2)}) collective-permute-start(bf16[2,64,2048]{2,1,0:T(8,128)(2,1)} %collective-permute-done.4.refs_1_), channel_id=1, source_target_pairs={{0,2},{1,3},{2,0},{3,1},{4,6},{5,7},{6,4},{7,5},{8,10},{9,11},{10,... | collective-permute-start | bytes 1572872 | tf_op jit(solution)/shard_map/ppermute | solution.py:353
  71.4 12.6 %collective-permute-start.10 = (bf16[2,64,2048]{2,1,0:T(8,128)(2,1)}, bf16[2,64,2048]{2,1,0:T(8,128)(2,1)}, u32[]{:S(2)}, u32[]{:S(2)}) collective-permute-start(bf16[2,64,2048]{2,1,0:T(8,128)(2,1)} %collective-permute-done.9.refs_6_), channel_id=1, source_target_pairs={{0,1},{1,0},{2,3},{3,2},{4,5},{5,4},{6,7},{7,6},{8,9},{9,8},{10,11... | collective-permute-start | bytes 1572872 | tf_op jit(solution)/shard_map/ppermute | solution.py:353
  83.9 48.6 %collective-permute-start.24 = (bf16[256,2048]{1,0:T(8,128)(2,1)}, bf16[256,2048]{1,0:T(8,128)(2,1)}, u32[]{:S(2)}, u32[]{:S(2)}) collective-permute-start(bf16[256,2048]{1,0:T(8,128)(2,1)} %refs_0_.1), channel_id=1, source_target_pairs={{8,0},{12,4},{16,8},{20,12},{24,16},{28,20},{9,1},{13,5},{17,9},{2... | collective-permute-start | bytes 3145736 | tf_op jit(solution)/shard_map/ppermute | solution.py:347
  85.2 47.3 %collective-permute-start.25 = (bf16[256,2048]{1,0:T(8,128)(2,1)}, bf16[256,2048]{1,0:T(8,128)(2,1)}, u32[]{:S(2)}, u32[]{:S(2)}) collective-permute-start(bf16[256,2048]{1,0:T(8,128)(2,1)} %refs_0_.1), channel_id=1, source_target_pairs={{0,8},{4,12},{8,16},{12,20},{16,24},{20,28},{1,9},{5,13},{9,17},{1... | collective-permute-start | bytes 3145736 | tf_op jit(solution)/shard_map/ppermute | solution.py:347
  115.9 5.1 %collective-permute-start.16 = (f32[16,640]{1,0:T(8,128)}, f32[16,640]{1,0:T(8,128)S(1)}, u32[]{:S(2)}, u32[]{:S(2)}) collective-permute-start(f32[16,640]{1,0:T(8,128)} %token_ranks.1), channel_id=1, source_target_pairs={{0,3},{1,2},{2,1},{3,0},{4,7},{5,6},{6,5},{7,4},{8,11},{9,10},{10,... | collective-permute-start | bytes 122888 | tf_op jit(solution)/shard_map/ppermute | solution.py:353
  117.2 4.2 %collective-permute-start.15 = (f32[16,640]{1,0:T(8,128)}, f32[16,640]{1,0:T(8,128)S(1)}, u32[]{:S(2)}, u32[]{:S(2)}) collective-permute-start(f32[16,640]{1,0:T(8,128)} %token_ranks.1), channel_id=1, source_target_pairs={{0,2},{1,3},{2,0},{3,1},{4,6},{5,7},{6,4},{7,5},{8,10},{9,11},{10,... | collective-permute-start | bytes 122888 | tf_op jit(solution)/shard_map/ppermute | solution.py:353
  118.8 4.2 %collective-permute-start.14 = (f32[16,640]{1,0:T(8,128)}, f32[16,640]{1,0:T(8,128)S(1)}, u32[]{:S(2)}, u32[]{:S(2)}) collective-permute-start(f32[16,640]{1,0:T(8,128)} %token_ranks.1), channel_id=1, source_target_pairs={{0,1},{1,0},{2,3},{3,2},{4,5},{5,4},{6,7},{7,6},{8,9},{9,8},{10,11... | collective-permute-start | bytes 122888 | tf_op jit(solution)/shard_map/ppermute | solution.py:353
  123.8 1.3 collective-permute-start.17
  132.6 21.1 %copy-start.11 = (bf16[128,2048]{1,0:T(8,128)(2,1)S(1)}, bf16[128,2048]{1,0:T(8,128)(2,1)}, u32[]{:S(2)}) copy-start(bf16[128,2048]{1,0:T(8,128)(2,1)} %get-tuple-element.52) | copy-start | bytes 1572868
  132.6 35.4 %collective-permute-start.26 = (bf16[256,2048]{1,0:T(8,128)(2,1)}, bf16[256,2048]{1,0:T(8,128)(2,1)S(1)}, u32[]{:S(2)}, u32[]{:S(2)}) collective-permute-start(bf16[256,2048]{1,0:T(8,128)(2,1)} %collective-permute-done.24.refs_1_), channel_id=1, source_target_pairs={{8,0},{12,4},{16,8},{20,12},{9,1},{13,5},{17,9},{21,13},{10,2},{14... | collective-permute-start | bytes 3145736 | tf_op jit(solution)/shard_map/ppermute | solution.py:347
  134.0 35.2 %collective-permute-start.28 = (bf16[256,2048]{1,0:T(8,128)(2,1)}, bf16[256,2048]{1,0:T(8,128)(2,1)S(1)}, u32[]{:S(2)}, u32[]{:S(2)}) collective-permute-start(bf16[256,2048]{1,0:T(8,128)(2,1)} %collective-permute-done.25.refs_4_), channel_id=1, source_target_pairs={{8,16},{12,20},{16,24},{20,28},{9,17},{13,21},{17,25},{21,29},{10,... | collective-permute-start | bytes 3145736 | tf_op jit(solution)/shard_map/ppermute | solution.py:347
  134.7 19.0 %collective-permute-start.18 = (bf16[128,2048]{1,0:T(8,128)(2,1)}, bf16[128,2048]{1,0:T(8,128)(2,1)S(1)}, u32[]{:S(2)}, u32[]{:S(2)}) collective-permute-start(bf16[128,2048]{1,0:T(8,128)(2,1)} %get-tuple-element.44), channel_id=1, source_target_pairs={{0,8},{4,12},{1,9},{5,13},{2,10},{6,14},{3,11},{7,15}} | collective-permute-start | bytes 1572872 | tf_op jit(solution)/shard_map/ppermute | solution.py:339
  141.1 13.3 %collective-permute-start.21 = (bf16[128,2048]{1,0:T(8,128)(2,1)}, bf16[128,2048]{1,0:T(8,128)(2,1)S(1)}, u32[]{:S(2)}, u32[]{:S(2)}) collective-permute-start(bf16[128,2048]{1,0:T(8,128)(2,1)} %get-tuple-element.42), channel_id=1, source_target_pairs={{24,16},{28,20},{25,17},{29,21},{26,18},{30,22},{27,19},{31,23}} | collective-permute-start | bytes 1572872 | tf_op jit(solution)/shard_map/ppermute | solution.py:343
  141.8 21.8 %collective-permute-start.30 = (bf16[128,2048]{1,0:T(8,128)(2,1)}, bf16[128,2048]{1,0:T(8,128)(2,1)S(1)}, u32[]{:S(2)}, u32[]{:S(2)}) collective-permute-start(bf16[128,2048]{1,0:T(8,128)(2,1)} %get-tuple-element.54), channel_id=1, source_target_pairs={{0,8},{4,12},{1,9},{5,13},{2,10},{6,14},{3,11},{7,15}} | collective-permute-start | bytes 1572872 | tf_op jit(solution)/shard_map/ppermute | solution.py:339
  150.4 19.6 %copy-start.16 = (bf16[128,2048]{1,0:T(8,128)(2,1)S(1)}, bf16[128,2048]{1,0:T(8,128)(2,1)}, u32[]{:S(2)}) copy-start(bf16[128,2048]{1,0:T(8,128)(2,1)} %get-tuple-element.53) | copy-start | bytes 1572868
  153.7 16.3 %collective-permute-start.33 = (bf16[128,2048]{1,0:T(8,128)(2,1)S(1)}, bf16[128,2048]{1,0:T(8,128)(2,1)S(1)}, u32[]{:S(2)}, u32[]{:S(2)}) collective-permute-start(bf16[128,2048]{1,0:T(8,128)(2,1)S(1)} %copy-done.11), channel_id=1, source_target_pairs={{24,16},{28,20},{25,17},{29,21},{26,18},{30,22},{27,19},{31,23}} | collective-permute-start | bytes 1572872 | tf_op jit(solution)/shard_map/ppermute | solution.py:343
  154.4 22.9 %copy-start.15 = (bf16[128,2048]{1,0:T(8,128)(2,1)S(1)}, bf16[128,2048]{1,0:T(8,128)(2,1)}, u32[]{:S(2)}) copy-start(bf16[128,2048]{1,0:T(8,128)(2,1)} %get-tuple-element.44) | copy-start | bytes 1572868
  155.8 16.8 %collective-permute-start.22 = (bf16[128,2048]{1,0:T(8,128)(2,1)S(1)}, bf16[128,2048]{1,0:T(8,128)(2,1)S(1)}, u32[]{:S(2)}, u32[]{:S(2)}) collective-permute-start(bf16[128,2048]{1,0:T(8,128)(2,1)S(1)} %get-tuple-element.77), channel_id=1, source_target_pairs={{16,8},{20,12},{24,16},{28,20},{17,9},{21,13},{25,17},{29,21},{18,... | collective-permute-start | bytes 1572872 | tf_op jit(solution)/shard_map/ppermute | solution.py:343
  163.6 16.6 %collective-permute-start.19 = (bf16[128,2048]{1,0:T(8,128)(2,1)S(1)}, bf16[128,2048]{1,0:T(8,128)(2,1)S(1)}, u32[]{:S(2)}, u32[]{:S(2)}) collective-permute-start(bf16[128,2048]{1,0:T(8,128)(2,1)S(1)} %get-tuple-element.76), channel_id=1, source_target_pairs={{0,8},{4,12},{8,16},{12,20},{1,9},{5,13},{9,17},{13,21},{2,10},{6,... | collective-permute-start | bytes 1572872 | tf_op jit(solution)/shard_map/ppermute | solution.py:339
  167.9 9.5 %copy-start.5 = (bf16[256,2048]{1,0:T(8,128)(2,1)}, bf16[256,2048]{1,0:T(8,128)(2,1)S(1)}, u32[]{:S(2)}) copy-start(bf16[256,2048]{1,0:T(8,128)(2,1)S(1)} %collective-permute-done.26.refs_2_) | copy-start | bytes 3145732
  167.9 28.0 %collective-permute-start.27 = (bf16[256,2048]{1,0:T(8,128)(2,1)S(1)}, bf16[256,2048]{1,0:T(8,128)(2,1)S(1)}, u32[]{:S(2)}, u32[]{:S(2)}) collective-permute-start(bf16[256,2048]{1,0:T(8,128)(2,1)S(1)} %collective-permute-done.26.refs_2_), channel_id=1, source_target_pairs={{8,0},{12,4},{9,1},{13,5},{10,2},{14,6},{11,3},{15,7}} | collective-permute-start | bytes 3145736 | tf_op jit(solution)/shard_map/ppermute | solution.py:347
  169.3 8.2 %copy-start.6 = (bf16[256,2048]{1,0:T(8,128)(2,1)}, bf16[256,2048]{1,0:T(8,128)(2,1)S(1)}, u32[]{:S(2)}) copy-start(bf16[256,2048]{1,0:T(8,128)(2,1)S(1)} %collective-permute-done.28.refs_5_) | copy-start | bytes 3145732
  169.3 28.2 %collective-permute-start.29 = (bf16[256,2048]{1,0:T(8,128)(2,1)S(1)}, bf16[256,2048]{1,0:T(8,128)(2,1)S(1)}, u32[]{:S(2)}, u32[]{:S(2)}) collective-permute-start(bf16[256,2048]{1,0:T(8,128)(2,1)S(1)} %collective-permute-done.28.refs_5_), channel_id=1, source_target_pairs={{16,24},{20,28},{17,25},{21,29},{18,26},{22,30},{19,27},{23,31}} | collective-permute-start | bytes 3145736 | tf_op jit(solution)/shard_map/ppermute | solution.py:347
  170.0 11.5 %copy-start.13 = (bf16[128,2048]{1,0:T(8,128)(2,1)S(1)}, bf16[128,2048]{1,0:T(8,128)(2,1)}, u32[]{:S(2)}) copy-start(bf16[128,2048]{1,0:T(8,128)(2,1)} %get-tuple-element.42) | copy-start | bytes 1572868
  171.1 34.7 %collective-permute-start.34 = (bf16[128,2048]{1,0:T(8,128)(2,1)}, bf16[128,2048]{1,0:T(8,128)(2,1)}, u32[]{:S(2)}, u32[]{:S(2)}) collective-permute-start(bf16[128,2048]{1,0:T(8,128)(2,1)} %get-tuple-element.79), channel_id=1, source_target_pairs={{16,8},{20,12},{24,16},{28,20},{17,9},{21,13},{25,17},{29,21},{18,... | collective-permute-start | bytes 1572872 | tf_op jit(solution)/shard_map/ppermute | solution.py:343
  172.6 35.9 %collective-permute-start.31 = (bf16[128,2048]{1,0:T(8,128)(2,1)S(1)}, bf16[128,2048]{1,0:T(8,128)(2,1)S(1)}, u32[]{:S(2)}, u32[]{:S(2)}) collective-permute-start(bf16[128,2048]{1,0:T(8,128)(2,1)S(1)} %get-tuple-element.78), channel_id=1, source_target_pairs={{0,8},{4,12},{8,16},{12,20},{1,9},{5,13},{9,17},{13,21},{2,10},{6,... | collective-permute-start | bytes 1572872 | tf_op jit(solution)/shard_map/ppermute | solution.py:339
  180.3 36.4 %collective-permute-start.23 = (bf16[128,2048]{1,0:T(8,128)(2,1)S(1)}, bf16[128,2048]{1,0:T(8,128)(2,1)S(1)}, u32[]{:S(2)}, u32[]{:S(2)}) collective-permute-start(bf16[128,2048]{1,0:T(8,128)(2,1)S(1)} %add_convert_fusion.4), channel_id=1, source_target_pairs={{8,0},{12,4},{16,8},{20,12},{24,16},{28,20},{9,1},{13,5},{17,9},{2... | collective-permute-start | bytes 1572872 | tf_op jit(solution)/shard_map/ppermute | solution.py:343
  195.9 1.5 copy-start.7
  195.9 21.3 %collective-permute-start.20 = (bf16[128,2048]{1,0:T(8,128)(2,1)S(1)}, bf16[128,2048]{1,0:T(8,128)(2,1)S(1)}, u32[]{:S(2)}, u32[]{:S(2)}) collective-permute-start(bf16[128,2048]{1,0:T(8,128)(2,1)S(1)} %add_convert_fusion.5), channel_id=1, source_target_pairs={{0,8},{4,12},{8,16},{12,20},{16,24},{20,28},{1,9},{5,13},{9,17},{1... | collective-permute-start | bytes 1572872 | tf_op jit(solution)/shard_map/ppermute | solution.py:339
  198.4 9.0 %copy-start.12 = (bf16[128,2048]{1,0:T(8,128)(2,1)S(1)}, bf16[128,2048]{1,0:T(8,128)(2,1)}, u32[]{:S(2)}) copy-start(bf16[128,2048]{1,0:T(8,128)(2,1)} %get-tuple-element.54) | copy-start | bytes 1572868
  205.2 11.3 %copy-start.26 = (bf16[320,2048]{1,0:T(8,128)(2,1)S(1)}, bf16[320,2048]{1,0:T(8,128)(2,1)}, u32[]{:S(2)}) copy-start(bf16[320,2048]{1,0:T(8,128)(2,1)} %get-tuple-element.56) | copy-start | bytes 3932164
  205.2 11.4 %copy-start.21 = (f32[2,16,320]{2,1,0:T(8,128)S(1)}, f32[2,16,320]{2,1,0:T(8,128)}, u32[]{:S(2)}) copy-start(f32[2,16,320]{2,1,0:T(8,128)} %get-tuple-element.51) | copy-start | bytes 122884
  205.3 12.0 %copy-start.10 = (f32[128,2048]{1,0:T(8,128)S(1)}, f32[128,2048]{1,0:T(8,128)}, u32[]{:S(2)}) copy-start(f32[128,2048]{1,0:T(8,128)} %get-tuple-element.41) | copy-start | bytes 3145732
  205.3 5.4 %collective-permute-start.38 = (f32[2,16,320]{2,1,0:T(8,128)}, f32[2,16,320]{2,1,0:T(8,128)S(1)}, u32[]{:S(2)}, u32[]{:S(2)}) collective-permute-start(f32[2,16,320]{2,1,0:T(8,128)} %get-tuple-element.51), channel_id=1, source_target_pairs={{0,3},{1,2},{2,1},{3,0},{4,7},{5,6},{6,5},{7,4},{8,11},{9,10},{10,... | collective-permute-start | bytes 122888 | tf_op jit(solution)/shard_map/ppermute | solution.py:353
  205.9 6.1 %collective-permute-start.37 = (f32[2,16,320]{2,1,0:T(8,128)}, f32[2,16,320]{2,1,0:T(8,128)S(1)}, u32[]{:S(2)}, u32[]{:S(2)}) collective-permute-start(f32[2,16,320]{2,1,0:T(8,128)} %get-tuple-element.51), channel_id=1, source_target_pairs={{0,2},{1,3},{2,0},{3,1},{4,6},{5,7},{6,4},{7,5},{8,10},{9,11},{10,... | collective-permute-start | bytes 122888 | tf_op jit(solution)/shard_map/ppermute | solution.py:353
  208.6 14.6 %copy-start.9 = (f32[128,2048]{1,0:T(8,128)S(1)}, f32[128,2048]{1,0:T(8,128)}, u32[]{:S(2)}) copy-start(f32[128,2048]{1,0:T(8,128)} %get-tuple-element.45) | copy-start | bytes 3145732
  208.6 7.9 %collective-permute-start.36 = (f32[2,16,320]{2,1,0:T(8,128)}, f32[2,16,320]{2,1,0:T(8,128)S(1)}, u32[]{:S(2)}, u32[]{:S(2)}) collective-permute-start(f32[2,16,320]{2,1,0:T(8,128)} %get-tuple-element.51), channel_id=1, source_target_pairs={{0,1},{1,0},{2,3},{3,2},{4,5},{5,4},{6,7},{7,6},{8,9},{9,8},{10,11... | collective-permute-start | bytes 122888 | tf_op jit(solution)/shard_map/ppermute | solution.py:353
  210.6 11.1 %collective-permute-start.35 = (bf16[128,2048]{1,0:T(8,128)(2,1)S(1)}, bf16[128,2048]{1,0:T(8,128)(2,1)S(1)}, u32[]{:S(2)}, u32[]{:S(2)}) collective-permute-start(bf16[128,2048]{1,0:T(8,128)(2,1)S(1)} %add_convert_fusion.1), channel_id=1, source_target_pairs={{8,0},{12,4},{16,8},{20,12},{24,16},{28,20},{9,1},{13,5},{17,9},{2... | collective-permute-start | bytes 1572872 | tf_op jit(solution)/shard_map/ppermute | solution.py:343
  211.9 11.2 %collective-permute-start.32 = (bf16[128,2048]{1,0:T(8,128)(2,1)S(1)}, bf16[128,2048]{1,0:T(8,128)(2,1)S(1)}, u32[]{:S(2)}, u32[]{:S(2)}) collective-permute-start(bf16[128,2048]{1,0:T(8,128)(2,1)S(1)} %add_convert_fusion.2), channel_id=1, source_target_pairs={{0,8},{4,12},{8,16},{12,20},{16,24},{20,28},{1,9},{5,13},{9,17},{1... | collective-permute-start | bytes 1572872 | tf_op jit(solution)/shard_map/ppermute | solution.py:339
  216.5 7.9 %collective-permute-start.40 = (bf16[320,2048]{1,0:T(8,128)(2,1)S(1)}, bf16[320,2048]{1,0:T(8,128)(2,1)S(1)}, u32[]{:S(2)}, u32[]{:S(2)}) collective-permute-start(bf16[320,2048]{1,0:T(8,128)(2,1)S(1)} %copy-done.26), channel_id=1, source_target_pairs={{0,4},{4,0},{8,12},{12,8},{16,20},{20,16},{24,28},{28,24},{1,5},{5... | collective-permute-start | bytes 3932168 | tf_op jit(solution)/shard_map/ppermute | solution.py:350
  216.7 3.0 %collective-permute-start.39 = (bf16[16,320]{1,0:T(8,128)(2,1)S(1)}, bf16[16,320]{1,0:T(8,128)(2,1)S(1)}, u32[]{:S(2)}, u32[]{:S(2)}) collective-permute-start(bf16[16,320]{1,0:T(8,128)(2,1)S(1)} %get-tuple-element.81), channel_id=1, source_target_pairs={{0,4},{4,0},{8,12},{12,8},{16,20},{20,16},{24,28},{28,24},{1,5},{5... | collective-permute-start | bytes 30728 | tf_op jit(solution)/shard_map/ppermute | solution.py:350
  (6 other events, 6.2 us)

commit v3 on v2

--- a/solution.py
+++ b/solution.py
@@ -170,19 +170,19 @@
     )(order, local, weight, *[slots] * blocks)
 
 
-def load_rows(place_ref, pieces, rows, sems):
+def load_rows(names, place_ref, pieces, rows, sems):
     me = place_ref[0]
     copies = []
-    tensors = rows.shape[1]
-    for i, piece in enumerate(pieces):
-        blocks = pl.ds(i // tensors * piece.shape[0], piece.shape[0])
-        copies.append(pltpu.make_async_copy(piece, rows.at[blocks, me ^ (i % tensors)], sems.at[i]))
-        copies[-1].start()
+    for (first, ks), piece in zip(names, pieces):
+        blocks = pl.ds(first, piece.shape[1])
+        for j, k in enumerate(ks):
+            copies.append(pltpu.make_async_copy(piece.at[j], rows.at[blocks, me ^ k], sems.at[len(copies)]))
+            copies[-1].start()
     for copy in copies:
         copy.wait()
 
 
-def frozen_kernel(place_ref, own_w_ref, other_w_ref, *refs):
+def frozen_kernel(names, place_ref, own_w_ref, other_w_ref, *refs):
     pieces, (out_ref, rows, sems) = refs[:-3], refs[-3:]
     blocks, tensors, sub, _ = rows.shape
     tokens = tensors * sub
@@ -190,7 +190,7 @@
 
     @pl.when(pl.program_id(0) == 0)
     def _():
-        load_rows(place_ref, pieces, rows, sems)
+        load_rows(names, place_ref, pieces, rows, sems)
 
     for b in range(blocks):
         x = rows[b].reshape(tokens, 2 * depth)
@@ -199,19 +199,19 @@
         out_ref[pl.ds(b * tokens, tokens), :] = product
 
 
-def frozen_part(tensor, weights, pieces):
-    blocks, sub, cols = pieces[0].shape
-    blocks, tensors = 2 * blocks, len(pieces) // 2
+def frozen_part(tensor, weights, names, pieces):
+    _, blocks, sub, cols = pieces[0].shape
+    blocks, tensors = 2 * blocks, sum(len(ks) for _, ks in names) // 2
     rows = blocks * sub * tensors
     width, depth = weights[0].shape
     tile = min(512, width)
     return pl.pallas_call(
-        frozen_kernel,
+        functools.partial(frozen_kernel, names),
         grid=(width // tile,),
         out_shape=jax.ShapeDtypeStruct((rows, width), F32),
         in_specs=[IN_SMEM] + [pl.BlockSpec((tile, depth), lambda n: (n, 0))] * 2 + [ANYWHERE] * len(pieces),
         out_specs=pl.BlockSpec((rows, tile), lambda n: (0, n)),
-        scratch_shapes=[pltpu.VMEM((blocks, tensors, sub, cols), BF16), pltpu.SemaphoreType.DMA((len(pieces),))],
+        scratch_shapes=[pltpu.VMEM((blocks, tensors, sub, cols), BF16), pltpu.SemaphoreType.DMA((2 * tensors,))],
         compiler_params=params(),
         cost_estimate=cost(2 * rows * width * cols, 4 * rows * width + 4 * width * depth),
         name="frozen_part",
@@ -375,7 +375,7 @@
     part = {0: plane_parts[0]}
     for d in range(1, planes):
         part[planes - d] = shift(plane_parts[d], d)
-    ids_again = after(ids_again, *plane_parts)
+    ids_again = after(ids_again, *plane_parts, *grad_rows[1:])
 
     all_ids = lax.all_to_all(jnp.broadcast_to(ids_again, (owners, tokens)), "adapter", 0, 0, tiled=True)
 
@@ -403,11 +403,15 @@
 
     halves = [jnp.stack([part[d] for d in order[i * half : (i + 1) * half]], axis=0) for i in range(2)]
     bits = [1 << i for i in range(tensors.bit_length() - 1)]
-    plane_rows = [{0: halves[0]}, {0: halves[1]}]
+    plane_rows = [[([0], x[None])] for x in halves]
     for step in zip(bits, reversed(bits)):
         for rows, bit in zip(plane_rows, step):
-            rows.update({k ^ bit: flip(x, bit) for k, x in list(rows.items())})
-    plane_rows = [rows[k] for rows in plane_rows for k in range(tensors)]
+            sent = jnp.concatenate([x for _, x in rows], axis=0) if len(rows) > 1 else rows[0][1]
+            rows.append(([k ^ bit for ks, _ in rows for k in ks], flip(sent, bit)))
+    first_rows = [rows[1][1] for rows in plane_rows]
+    row_names = [(i * half, ks) for i, rows in enumerate(plane_rows) for ks, _ in rows]
+    plane_rows = [x for rows in plane_rows for _, x in rows]
+    all_ids = after(all_ids, *first_rows)
     other_weight = swap(weight)
     other_down_t = swap(down_t)
 
@@ -440,12 +444,12 @@
     places = jnp.concatenate([places[:, d : d + 1] for d in order], axis=1).reshape(4, -1)
 
     first_weight = after(weight, places, local, parity_local, attn_places, slot_order, other_down_t)
-    attn_start = after(attn, *plane_rows)
+    attn_start = after(attn, *first_rows)
     going_down, going_up = attn_line(attn_start, 1, -1), attn_line(attn_start, 1, 1)
-    frozen = frozen_part(tensor, (first_weight, other_weight), plane_rows)
+    frozen = frozen_part(tensor, (first_weight, other_weight), row_names, plane_rows)
     grad_slots = after(grad_slots, frozen)
-    low_grads = token_ranks(slot_order, local, up, grad_slots, per_owner)
-    low_grads = sum([flip(low_grads, k) for k in range(1, tensors)], low_grads)
+    part_grads = token_ranks(slot_order, local, up, grad_slots, per_owner)
+    low_grads = sum([flip(part_grads, k) for k in range(1, tensors)], part_grads)
     grad_low = (ADAPTER_SCALE * low_grads).astype(BF16)
     ranks = (grad_low, swap(grad_low))
     downs = (down_t, other_down_t)
@@ -457,33 +461,35 @@
     below, above = [going_down], [going_up]
     for d in range(2, planes):
         if d == 2:
-            going_down, going_up = after((going_down, going_up), *pairs)
+            going_down, going_up = after((going_down, going_up), part_grads)
         going_down, going_up = attn_line(going_down, d, -1), attn_line(going_up, d, 1)
         below.append(going_down)
         above.append(going_up)
     pairs += with_term(1, [BF16] * (planes - 2) + [F32] * 2)
     sums = {d: pairs[2 * i : 2 * i + 2] for i, d in enumerate(order)}
+    going_up, going_down = [None, None], [None, None]
+    for d in range(planes - 1, 0, -1):
+        for i in range(2):
+            up_sum, down_sum = sums[d][i], sums[planes - d][i]
+            if d == planes - 2 and i == 0:
+                up_sum, down_sum = after((up_sum, down_sum), below[1], above[1])
+            if going_up[i] is not None:
+                up_sum = (up_sum.astype(F32) + going_up[i].astype(F32)).astype(BF16)
+                down_sum = (down_sum.astype(F32) + going_down[i].astype(F32)).astype(BF16)
+            last_sums = (up_sum, down_sum)
+            going_up[i], going_down[i] = up_line(up_sum, d), down_line(down_sum, d)
+    below[-1], above[-1] = after((below[-1], above[-1]), *last_sums)
     attn_own, attn_other, parity_inputs = repack(
         plane, attn_places, parity_local, downs, attn, below, above, capacity, per_owner
     )
     attn_slots = [attn_own, swap(attn_other)]
-    going_up, going_down = [None, None], [None, None]
-    for d in range(planes - 1, 0, -1):
-        for i in range(2):
-            up_sum, down_sum = sums[d][i], sums[planes - d][i]
-            if d == 1 and i == 1:
-                up_sum, down_sum = after((up_sum, down_sum), parity_inputs)
-            if going_up[i] is not None:
-                up_sum = (up_sum.astype(F32) + going_up[i].astype(F32)).astype(BF16)
-                down_sum = (down_sum.astype(F32) + going_down[i].astype(F32)).astype(BF16)
-            going_up[i], going_down[i] = up_line(up_sum, d), down_line(down_sum, d)
-    total = [x + up_sum.astype(F32) + down_sum.astype(F32) for x, up_sum, down_sum in zip(sums[0], going_up, going_down)]
-    attention_output_gradient = jnp.concatenate(total, axis=0).astype(BF16)
-
     low_inputs = sum([flip(parity_inputs, k) for k in range(1, tensors)], parity_inputs)
     up_scaled = (ADAPTER_SCALE * low_inputs).astype(BF16)
     up_scaled = jnp.concatenate([up_scaled[0], swap(up_scaled[1])], axis=1)
     down_grad, up_grad = adapter_gradients(slot_order, local, grad_low, up_scaled, attn_slots, grad_slots, per_owner)
+    going_up, going_down = after((going_up, going_down), down_grad)
+    total = [x + up_sum.astype(F32) + down_sum.astype(F32) for x, up_sum, down_sum in zip(sums[0], going_up, going_down)]
+    attention_output_gradient = jnp.concatenate(total, axis=0).astype(BF16)
     return attention_output_gradient, down_grad, up_grad
 
 

time: 237 us -> 233 us (0.983)
  waiting for transfers between devices: 77.7 us -> 63.3 us
  starting transfers between devices: 69.8 us -> 77.1 us
    ppermute x15 -> x13, waiting for transfers between devices: 40.2 us -> 29.9 us  [flip(): return lax.ppermute(x, 'tensor', [(t, t ^ k) for t in range(tensors)])]
    ppermute x6, starting transfers between devices: 22.6 us -> 27.2 us  [up_line(): return lax.ppermute(x, 'adapter', pairs)]
    concatenate x0 -> x2, other arithmetic: none -> 3.31 us  [per_device(): jnp.concatenate([x for _, x in rows], axis=0)]
    ppermute x6, waiting for transfers between devices: 14.7 us -> 11.5 us  [up_line(): return lax.ppermute(x, 'adapter', pairs)]
    ppermute x15 -> x13, starting transfers between devices: 17.2 us -> 16.7 us  [flip(): return lax.ppermute(x, 'tensor', [(t, t ^ k) for t in range(tensors)])]
    unnamed x59 -> x54, local copies, waits for them, and re-layouts: 8.56 us -> 8.94 us
  transfers between devices with their start and end apart: 43 -> 41, of which waited for: 19 -> 15; matrix products, arithmetic and copies ran while one was open for 10% -> 11% of each run, Pallas kernels for 19% -> 24%
where the time goes in v3:
time: 233 us; the launch traced here: 231 us
  starting transfers between devices  77.1 us (33%)
  waiting for transfers between devices  63.3 us (27%)
  Pallas kernels  56 us (24%)
  other arithmetic  17.1 us (7%)
  local copies, waits for them, and re-layouts  16.3 us (7%)
    ppermute x13, waiting for transfers between devices, flip(): return lax.ppermute(x, 'tensor', [(t, t ^ k) for t in range(tensors)])  29.9 us
    ppermute x6, starting transfers between devices, up_line(): return lax.ppermute(x, 'adapter', pairs)  27.2 us
    ppermute x13, starting transfers between devices, flip(): return lax.ppermute(x, 'tensor', [(t, t ^ k) for t in range(tensors)])  16.7 us
    pallas_call x1, Pallas kernels, frozen_part(): pl.pallas_call(functools.partial(frozen_kernel, names), grid=(width // ti...  14.9 us
    pallas_call x2, Pallas kernels, add_term(): pl.pallas_call(functools.partial(term_kernel, per_owner), grid=(width //...  14.1 us
    ppermute x6, waiting for transfers between devices, attn_line(): lax.ppermute(x, 'adapter', [(2 * z + c, 2 * (z + way) + c) for z in plane...  12.2 us
    ppermute x6, waiting for transfers between devices, up_line(): return lax.ppermute(x, 'adapter', pairs)  11.5 us
    ppermute x6, starting transfers between devices, attn_line(): lax.ppermute(x, 'adapter', [(2 * z + c, 2 * (z + way) + c) for z in plane...  10.9 us
  transfers between devices with their start and end apart: 41, of which 15 were waited for; matrix products, arithmetic and copies ran while one was open for 11% of the time, Pallas kernels for 24%

profile of v3, /device:TPU:0, one launch (start us, length us, event | category | flops | bytes accessed | tf_op | source)
XLA Modules:
  0.0 231.2 jit_solution(3218640224102962969)
XLA Ops:
  0.7 2.3 constant_dynamic-slice_fusion.8
  2.9 2.9 %collective-permute-start = (bf16[64,2048]{1,0:T(8,128)(2,1)}, bf16[64,2048]{1,0:T(8,128)(2,1)}, u32[]{:S(2)}, u32[]{:S(2)}) collective-permute-start(bf16[64,2048]{1,0:T(8,128)(2,1)} %get-tuple-element.88), channel_id=1, source_target_pairs={{0,1},{1,0},{2,3},{3,2},{4,5},{5,4},{6,7},{7,6},{8,9},{9,8},{10,11... | collective-permute-start | bytes 786440 | tf_op jit(solution)/shard_map/ppermute | solution.py:353
  5.9 1.5 collective-permute-start.1
  8.2 2.1 collective-permute-start.4
  10.3 2.1 collective-permute-start.3
  12.6 0.9 fusion.13
  13.7 2.8 %collective-permute-start.6 = (bf16[64,2048]{1,0:T(8,128)(2,1)S(1)}, bf16[64,2048]{1,0:T(8,128)(2,1)}, u32[]{:S(2)}, u32[]{:S(2)}) collective-permute-start(bf16[64,2048]{1,0:T(8,128)(2,1)S(1)} %pad_maximum_fusion.5), channel_id=1, source_target_pairs={{0,16},{4,20},{8,24},{12,28},{16,0},{20,4},{24,8},{28,12},{1,17},{... | collective-permute-start | bytes 786440 | tf_op jit(solution)/shard_map/ppermute | solution.py:335
  16.5 2.4 %copy.11 = bf16[2048,512]{0,1:T(8,128)(2,1)} copy(bf16[2048,512]{1,0:T(8,128)(2,1)S(1)} %copy-done.6) | data formatting | bytes 4194304 | tf_op args[4]
  20.7 4.9 %all-to-all-start = ((s32[8,1,256]{2,1,0:T(1,128)}), s32[8,1,256]{2,1,0:T(1,128)S(1)}, u32[]{:S(2)}, u32[]{:S(2)}) async-start(s32[8,1,256]{2,1,0:T(1,128)} %broadcast_in_dim.37), calls=%async_computation | async-start | bytes 16384 | tf_op jit(solution)/shard_map/all_to_all | solution.py:380
  25.6 3.2 %pack_rows.1 = bf16[640,2048]{1,0:T(8,128)(2,1)} custom-call(s32[1,256]{1,0:T(1,128)} %bitcast.71, bf16[64,2048]{1,0:T(8,128)(2,1)} %get-tuple-element.43.refs_0_, bf16[64,2048]{1,0:T(8,128)(2,1)} %collective-permute-done.refs_1_, bf16[64,2048]{1,0:T(8,128)(2,1)} %collective-permute-done.1.refs_2_, bf16[64,2048]{1,0:T(8,128)(2,1)} %collective-permute-done.2.refs_3_), custom_call_target="tpu_custom_call" | custom-call | flops 10485760 | bytes 57344 | tf_op jit(solution)/shard_map/pack_rows/pallas_call | solution.py:43
  28.8 6.0 %collective-permute-done.6 = bf16[64,2048]{1,0:T(8,128)(2,1)} collective-permute-done((bf16[64,2048]{1,0:T(8,128)(2,1)S(1)}, bf16[64,2048]{1,0:T(8,128)(2,1)}, u32[]{:S(2)}, u32[]{:S(2)}) %collective-permute-start.6) | collective-permute-done | bytes 262176 | tf_op jit(solution)/shard_map/ppermute | solution.py:335
  34.8 3.6 %all-to-all-start.1 = ((bf16[8,80,2048]{2,1,0:T(8,128)(2,1)}), bf16[8,80,2048]{2,1,0:T(8,128)(2,1)S(1)}, u32[]{:S(2)}, u32[]{:S(2)}) async-start(bf16[8,80,2048]{2,1,0:T(8,128)(2,1)} %bitcast.63), calls=%async_computation.1 | async-start | bytes 5242880 | tf_op jit(solution)/shard_map/all_to_all | solution.py:399
  38.5 1.1 maximum_bitcast_fusion.refs_0_
  39.6 1.6 collective-permute-start.5
  41.1 1.0 maximum_bitcast_fusion.1.refs_3_
  42.1 1.6 collective-permute-start.7
  44.4 9.5 %collective-permute-done.5.refs_1_ = bf16[1,2,64,2048]{3,2,1,0:T(8,128)(2,1)S(1)} collective-permute-done((bf16[1,2,64,2048]{3,2,1,0:T(8,128)(2,1)S(1)}, bf16[1,2,64,2048]{3,2,1,0:T(8,128)(2,1)S(1)}, u32[]{:S(2)}, u32[]{:S(2)}) %collective-permute-start.5) | collective-permute-done | bytes 524320 | tf_op jit(solution)/shard_map/ppermute | solution.py:353
  53.9 2.3 collective-permute-done.7.refs_4_
  56.2 0.8 copy-done.8
  61.2 2.2 pad_maximum_fusion
  63.4 1.5 collective-permute-start.10
  64.9 1.1 pad_maximum_fusion.1
  67.6 1.3 collective-permute-start.16
  68.9 5.5 %collective-permute-start.17 = (bf16[256,2048]{1,0:T(8,128)(2,1)}, bf16[256,2048]{1,0:T(8,128)(2,1)}, u32[]{:S(2)}, u32[]{:S(2)}) collective-permute-start(bf16[256,2048]{1,0:T(8,128)(2,1)} %refs_0_.1), channel_id=1, source_target_pairs={{0,8},{4,12},{8,16},{12,20},{16,24},{20,28},{1,9},{5,13},{9,17},{1... | collective-permute-start | bytes 3145736 | tf_op jit(solution)/shard_map/ppermute | solution.py:347
  76.7 11.4 %collective-permute-done.10.refs_2_ = bf16[2,2,64,2048]{3,2,1,0:T(8,128)(2,1)} collective-permute-done((bf16[2,2,64,2048]{3,2,1,0:T(8,128)(2,1)}, bf16[2,2,64,2048]{3,2,1,0:T(8,128)(2,1)}, u32[]{:S(2)}, u32[]{:S(2)}) %collective-permute-start.10) | collective-permute-done | bytes 1048608 | tf_op jit(solution)/shard_map/ppermute | solution.py:353
  88.1 2.4 %collective-permute-done.11.refs_5_ = bf16[2,2,64,2048]{3,2,1,0:T(8,128)(2,1)} collective-permute-done((bf16[2,2,64,2048]{3,2,1,0:T(8,128)(2,1)}, bf16[2,2,64,2048]{3,2,1,0:T(8,128)(2,1)}, u32[]{:S(2)}, u32[]{:S(2)}) %collective-permute-start.11) | collective-permute-done | bytes 1048608 | tf_op jit(solution)/shard_map/ppermute | solution.py:353
  90.4 14.9 %frozen_part.1.frozen_ref = f32[1024,2048]{1,0:T(8,128)} custom-call(s32[1]{0:T(128)} %bitcast.place_ref, bf16[2048,1024]{1,0:T(8,128)(2,1)} %own_w_ref, bf16[2048,1024]{1,0:T(8,128)(2,1)} %collective-permute-done.9.other_w_ref, bf16[1,2,64,2048]{3,2,1,0:T(8,128)(2,1)} %copy-done.1, bf16[1,2,64,2048]{3,2,1,0:T(8,128)(2,1)} %copy-done.7, ...), custom_call_target="tpu_custom_call" | custom-call | flops 134217728 | bytes 262144 | tf_op jit(solution)/shard_map/frozen_part/pallas_call | solution.py:208
  105.4 1.5 copy-done
  106.8 6.4 %token_ranks.1 = f32[16,640]{1,0:T(8,128)} custom-call(s32[8]{0:T(128)} %pad_add_fusion.4.order_ref, s32[1,640]{1,0:T(1,128)} %pad_add_fusion.2.local_ref, bf16[512,2048]{1,0:T(8,128)(2,1)} %weight_ref.1, bf16[640,2048]{1,0:T(8,128)(2,1)} %bitcast.47, bf16[640,2048]{1,0:T(8,128)(2,1)} %bitcast.48, bf16[640,2048]{1,0:T(8,128)(2,1)} %bitcast.49, ...), custom_call_target="tpu_custom_call" | custom-call | flops 20971520 | bytes 73728 | tf_op jit(solution)/shard_map/token_ranks/pallas_call | solution.py:153
  113.7 1.5 collective-permute-start.13
  115.3 1.5 collective-permute-start.12
  116.7 1.6 collective-permute-done.14
  118.4 1.1 collective-permute-done.12
  120.4 1.3 collective-permute-start.18
  123.0 6.9 %add_term.3 = (bf16[128,2048]{1,0:T(8,128)(2,1)}, bf16[128,2048]{1,0:T(8,128)(2,1)}, bf16[128,2048]{1,0:T(8,128)(2,1)}, bf16[128,2048]{1,0:T(8,128)(2,1)}) custom-call(f32[1024,2048]{1,0:T(8,128)} %frozen_part.1.frozen_ref, s32[4,1024]{1,0:T(4,128)} %bitcast.68, bf16[16,640]{1,0:T(8,128)(2,1)} %copy-done.21, bf16[16,640]{1,0:T(8,128)(2,1)} %copy-done.23, ...), custom_call_target="tpu_custom_call" | custom-call | flops 33554432 | bytes 163840 | tf_op jit(solution)/shard_map/add_term/pallas_call | solution.py:253
  130.6 7.4 %collective-permute-start.23 = (bf16[128,2048]{1,0:T(8,128)(2,1)}, bf16[128,2048]{1,0:T(8,128)(2,1)S(1)}, u32[]{:S(2)}, u32[]{:S(2)}) collective-permute-start(bf16[128,2048]{1,0:T(8,128)(2,1)} %get-tuple-element.59), channel_id=1, source_target_pairs={{0,8},{4,12},{1,9},{5,13},{2,10},{6,14},{3,11},{7,15}} | collective-permute-start | bytes 1572872 | tf_op jit(solution)/shard_map/ppermute | solution.py:339
  138.0 1.5 collective-permute-start.20
  139.5 7.2 %add_term.2 = (bf16[128,2048]{1,0:T(8,128)(2,1)}, bf16[128,2048]{1,0:T(8,128)(2,1)}, f32[128,2048]{1,0:T(8,128)}, f32[128,2048]{1,0:T(8,128)}) custom-call(f32[1024,2048]{1,0:T(8,128)} %frozen_part.1.frozen_ref, s32[4,1024]{1,0:T(4,128)} %bitcast.69, bf16[16,640]{1,0:T(8,128)(2,1)} %copy-done.21, bf16[16,640]{1,0:T(8,128)(2,1)} %copy-done.23, ...), custom_call_target="tpu_custom_call" | custom-call | flops 33554432 | bytes 163840 | tf_op jit(solution)/shard_map/add_term/pallas_call | solution.py:253
  146.7 0.8 collective-permute-start.26
  147.5 3.1 %collective-permute-done.23 = bf16[128,2048]{1,0:T(8,128)(2,1)S(1)} collective-permute-done((bf16[128,2048]{1,0:T(8,128)(2,1)}, bf16[128,2048]{1,0:T(8,128)(2,1)S(1)}, u32[]{:S(2)}, u32[]{:S(2)}) %collective-permute-start.23) | collective-permute-done | bytes 524320 | tf_op jit(solution)/shard_map/ppermute | solution.py:339
  150.6 1.3 fusion.1
  152.0 4.4 %collective-permute-start.24 = (bf16[128,2048]{1,0:T(8,128)(2,1)S(1)}, bf16[128,2048]{1,0:T(8,128)(2,1)S(1)}, u32[]{:S(2)}, u32[]{:S(2)}) collective-permute-start(bf16[128,2048]{1,0:T(8,128)(2,1)S(1)} %get-tuple-element.91), channel_id=1, source_target_pairs={{0,8},{4,12},{8,16},{12,20},{1,9},{5,13},{9,17},{13,21},{2,10},{6,... | collective-permute-start | bytes 1572872 | tf_op jit(solution)/shard_map/ppermute | solution.py:339
  157.2 4.7 %collective-permute-done.20 = bf16[128,2048]{1,0:T(8,128)(2,1)S(1)} collective-permute-done((bf16[128,2048]{1,0:T(8,128)(2,1)}, bf16[128,2048]{1,0:T(8,128)(2,1)S(1)}, u32[]{:S(2)}, u32[]{:S(2)}) %collective-permute-start.20) | collective-permute-done | bytes 524320 | tf_op jit(solution)/shard_map/ppermute | solution.py:339
  161.9 0.9 add_convert_fusion.7
  162.8 4.3 %collective-permute-start.21 = (bf16[128,2048]{1,0:T(8,128)(2,1)}, bf16[128,2048]{1,0:T(8,128)(2,1)S(1)}, u32[]{:S(2)}, u32[]{:S(2)}) collective-permute-start(bf16[128,2048]{1,0:T(8,128)(2,1)} %add_convert_fusion.7), channel_id=1, source_target_pairs={{0,8},{4,12},{8,16},{12,20},{1,9},{5,13},{9,17},{13,21},{2,10},{6,... | collective-permute-start | bytes 1572872 | tf_op jit(solution)/shard_map/ppermute | solution.py:339
  167.1 1.3 collective-permute-start.32
  169.3 3.7 %collective-permute-done.24 = bf16[128,2048]{1,0:T(8,128)(2,1)S(1)} collective-permute-done((bf16[128,2048]{1,0:T(8,128)(2,1)S(1)}, bf16[128,2048]{1,0:T(8,128)(2,1)S(1)}, u32[]{:S(2)}, u32[]{:S(2)}) %collective-permute-start.24) | collective-permute-done | bytes 524320 | tf_op jit(solution)/shard_map/ppermute | solution.py:339
  173.0 0.9 collective-permute-start.27
  174.0 5.0 %collective-permute-start.25 = (bf16[128,2048]{1,0:T(8,128)(2,1)S(1)}, bf16[128,2048]{1,0:T(8,128)(2,1)S(1)}, u32[]{:S(2)}, u32[]{:S(2)}) collective-permute-start(bf16[128,2048]{1,0:T(8,128)(2,1)S(1)} %add_convert_fusion.5), channel_id=1, source_target_pairs={{0,8},{4,12},{8,16},{12,20},{16,24},{20,28},{1,9},{5,13},{9,17},{1... | collective-permute-start | bytes 1572872 | tf_op jit(solution)/shard_map/ppermute | solution.py:339
  179.2 12.2 %collective-permute-done.32.refs_3_ = bf16[256,2048]{1,0:T(8,128)(2,1)S(1)} collective-permute-done((bf16[256,2048]{1,0:T(8,128)(2,1)S(1)}, bf16[256,2048]{1,0:T(8,128)(2,1)S(1)}, u32[]{:S(2)}, u32[]{:S(2)}) %collective-permute-start.32) | collective-permute-done | bytes 1048608 | tf_op jit(solution)/shard_map/ppermute | solution.py:347
  191.4 1.0 copy-done.13
  192.8 6.8 %repack.1 = (bf16[320,2048]{1,0:T(8,128)(2,1)}, bf16[320,2048]{1,0:T(8,128)(2,1)}, f32[2,16,320]{2,1,0:T(8,128)}) custom-call(s32[1]{0:T(128)} %bitcast.18.plane_ref, s32[1,1024]{1,0:T(1,128)} %bitcast.70, s32[2,320]{1,0:T(2,128)} %pad_add_fusion.1.local_ref, bf16[512,2048]{1,0:T(8,128)(2,1)} %bitcast.14.refs_2_.own_d_ref, ...), custom_call_target="tpu_custom_call" | custom-call | flops 31457280 | bytes 106496 | tf_op jit(solution)/shard_map/repack/pallas_call | solution.py:107
  199.5 1.1 collective-permute-start.36
  200.7 1.9 collective-permute-start.35
  203.2 1.6 collective-permute-done.36
  204.8 1.3 collective-permute-start.31
  206.1 4.6 %collective-permute-start.22 = (bf16[128,2048]{1,0:T(8,128)(2,1)S(1)}, bf16[128,2048]{1,0:T(8,128)(2,1)S(1)}, u32[]{:S(2)}, u32[]{:S(2)}) collective-permute-start(bf16[128,2048]{1,0:T(8,128)(2,1)S(1)} %add_convert_fusion.6), channel_id=1, source_target_pairs={{0,8},{4,12},{8,16},{12,20},{16,24},{20,28},{1,9},{5,13},{9,17},{1... | collective-permute-start | bytes 1572872 | tf_op jit(solution)/shard_map/ppermute | solution.py:339
  210.8 0.8 multiply_convert_fusion
  212.4 1.5 collective-permute-done.37
  213.9 1.3 collective-permute-start.28
  215.8 1.1 copy-done.10
  216.9 10.6 %adapter_gradients.1 = (f32[2048,512]{1,0:T(8,128)}, f32[512,2048]{1,0:T(8,128)}) custom-call(s32[8]{0:T(128)} %pad_add_fusion.4.order_ref, s32[1,640]{1,0:T(1,128)} %pad_add_fusion.2.local_ref, bf16[16,640]{1,0:T(8,128)(2,1)} %copy-done.21, bf16[16,640]{1,0:T(8,128)(2,1)} %pad_maximum_fusion.7.up_ranks_ref, bf16[320,2048]{1,0:T(8,128)(2,1)} %get-tuple-element.64.own_ref, ...), custom_call_target="tpu_custom_call" | custom-call | flops 41943040 | bytes 212992 | tf_op jit(solution)/shard_map/adapter_gradients/pallas_call | solution.py:293
  227.6 2.1 collective-permute-done.28
  230.1 1.1 pad_maximum_fusion.2
  (142 shorter events, 19.7 us)
Async XLA Ops:
  0.6 6.8 %copy-start.4 = (bf16[64,8192]{1,0:T(8,128)(2,1)S(1)}, bf16[64,8192]{1,0:T(8,128)(2,1)}, u32[]{:S(2)}) copy-start(bf16[64,8192]{1,0:T(8,128)(2,1)} %param.7) | copy-start | bytes 3145732
  2.9 9.5 %copy-start.24 = (s32[256]{0:T(256)S(1)}, s32[256]{0:T(256)}, u32[]{:S(2)}) copy-start(s32[256]{0:T(256)} %param.8) | copy-start | bytes 3076
  2.9 10.7 %collective-permute-start = (bf16[64,2048]{1,0:T(8,128)(2,1)}, bf16[64,2048]{1,0:T(8,128)(2,1)}, u32[]{:S(2)}, u32[]{:S(2)}) collective-permute-start(bf16[64,2048]{1,0:T(8,128)(2,1)} %get-tuple-element.88), channel_id=1, source_target_pairs={{0,1},{1,0},{2,3},{3,2},{4,5},{5,4},{6,7},{7,6},{8,9},{9,8},{10,11... | collective-permute-start | bytes 786440 | tf_op jit(solution)/shard_map/ppermute | solution.py:353
  5.9 13.7 %collective-permute-start.1 = (bf16[64,2048]{1,0:T(8,128)(2,1)}, bf16[64,2048]{1,0:T(8,128)(2,1)}, u32[]{:S(2)}, u32[]{:S(2)}) collective-permute-start(bf16[64,2048]{1,0:T(8,128)(2,1)} %get-tuple-element.87), channel_id=1, source_target_pairs={{0,2},{1,3},{2,0},{3,1},{4,6},{5,7},{6,4},{7,5},{8,10},{9,11},{10,... | collective-permute-start | bytes 786440 | tf_op jit(solution)/shard_map/ppermute | solution.py:353
  7.4 12.2 %collective-permute-start.2 = (bf16[64,2048]{1,0:T(8,128)(2,1)}, bf16[64,2048]{1,0:T(8,128)(2,1)}, u32[]{:S(2)}, u32[]{:S(2)}) collective-permute-start(bf16[64,2048]{1,0:T(8,128)(2,1)} %get-tuple-element.86), channel_id=1, source_target_pairs={{0,3},{1,2},{2,1},{3,0},{4,7},{5,6},{6,5},{7,4},{8,11},{9,10},{10,... | collective-permute-start | bytes 786440 | tf_op jit(solution)/shard_map/ppermute | solution.py:353
  7.4 9.1 %copy-start.6 = (bf16[2048,512]{1,0:T(8,128)(2,1)S(1)}, bf16[2048,512]{1,0:T(8,128)(2,1)}, u32[]{:S(2)}) copy-start(bf16[2048,512]{1,0:T(8,128)(2,1)} %param.10) | copy-start | bytes 6291460
  8.2 20.6 %collective-permute-start.4 = (bf16[64,2048]{1,0:T(8,128)(2,1)S(1)}, bf16[64,2048]{1,0:T(8,128)(2,1)S(1)}, u32[]{:S(2)}, u32[]{:S(2)}) collective-permute-start(bf16[64,2048]{1,0:T(8,128)(2,1)S(1)} %pad_maximum_fusion.4), channel_id=1, source_target_pairs={{0,8},{4,12},{8,16},{12,20},{16,24},{20,28},{24,0},{28,4},{1,9},{5... | collective-permute-start | bytes 786440 | tf_op jit(solution)/shard_map/ppermute | solution.py:335
  10.3 18.5 %collective-permute-start.3 = (bf16[64,2048]{1,0:T(8,128)(2,1)S(1)}, bf16[64,2048]{1,0:T(8,128)(2,1)}, u32[]{:S(2)}, u32[]{:S(2)}) collective-permute-start(bf16[64,2048]{1,0:T(8,128)(2,1)S(1)} %pad_maximum_fusion.6), channel_id=1, source_target_pairs={{0,24},{4,28},{8,0},{12,4},{16,8},{20,12},{24,16},{28,20},{1,25},{... | collective-permute-start | bytes 786440 | tf_op jit(solution)/shard_map/ppermute | solution.py:335
  13.7 21.2 %collective-permute-start.6 = (bf16[64,2048]{1,0:T(8,128)(2,1)S(1)}, bf16[64,2048]{1,0:T(8,128)(2,1)}, u32[]{:S(2)}, u32[]{:S(2)}) collective-permute-start(bf16[64,2048]{1,0:T(8,128)(2,1)S(1)} %pad_maximum_fusion.5), channel_id=1, source_target_pairs={{0,16},{4,20},{8,24},{12,28},{16,0},{20,4},{24,8},{28,12},{1,17},{... | collective-permute-start | bytes 786440 | tf_op jit(solution)/shard_map/ppermute | solution.py:335
  19.6 49.3 %collective-permute-start.8 = (bf16[512,2048]{1,0:T(8,128)(2,1)}, bf16[512,2048]{1,0:T(8,128)(2,1)}, u32[]{:S(2)}, u32[]{:S(2)}) collective-permute-start(bf16[512,2048]{1,0:T(8,128)(2,1)} %bitcast.14.refs_2_.own_d_ref), channel_id=1, source_target_pairs={{0,4},{4,0},{8,12},{12,8},{16,20},{20,16},{24,28},{28,24},{1,5},{5... | collective-permute-start | bytes 6291464 | tf_op jit(solution)/shard_map/ppermute | solution.py:350
  19.6 70.9 %collective-permute-start.9 = (bf16[2048,1024]{1,0:T(8,128)(2,1)}, bf16[2048,1024]{1,0:T(8,128)(2,1)}, u32[]{:S(2)}, u32[]{:S(2)}) collective-permute-start(bf16[2048,1024]{1,0:T(8,128)(2,1)} %own_w_ref), channel_id=1, source_target_pairs={{0,4},{4,0},{8,12},{12,8},{16,20},{20,16},{24,28},{28,24},{1,5},{5... | collective-permute-start | bytes 12582920 | tf_op jit(solution)/shard_map/ppermute | solution.py:350
  20.7 14.2 %all-to-all-start = ((s32[8,1,256]{2,1,0:T(1,128)}), s32[8,1,256]{2,1,0:T(1,128)S(1)}, u32[]{:S(2)}, u32[]{:S(2)}) async-start(s32[8,1,256]{2,1,0:T(1,128)} %broadcast_in_dim.37), calls=%async_computation | async-start | bytes 16384 | tf_op jit(solution)/shard_map/all_to_all | solution.py:380
  28.8 6.1 %copy-start.22 = (bf16[64,2048]{1,0:T(8,128)(2,1)}, bf16[64,2048]{1,0:T(8,128)(2,1)S(1)}, u32[]{:S(2)}) copy-start(bf16[64,2048]{1,0:T(8,128)(2,1)S(1)} %collective-permute-done.4) | copy-start | bytes 786436
  34.8 70.5 %all-to-all-start.1 = ((bf16[8,80,2048]{2,1,0:T(8,128)(2,1)}), bf16[8,80,2048]{2,1,0:T(8,128)(2,1)S(1)}, u32[]{:S(2)}, u32[]{:S(2)}) async-start(bf16[8,80,2048]{2,1,0:T(8,128)(2,1)} %bitcast.63), calls=%async_computation.1 | async-start | bytes 5242880 | tf_op jit(solution)/shard_map/all_to_all | solution.py:399
  39.6 26.5 %copy-start.1 = (bf16[1,2,64,2048]{3,2,1,0:T(8,128)(2,1)}, bf16[1,2,64,2048]{3,2,1,0:T(8,128)(2,1)S(1)}, u32[]{:S(2)}) copy-start(bf16[1,2,64,2048]{3,2,1,0:T(8,128)(2,1)S(1)} %maximum_bitcast_fusion.refs_0_) | copy-start | bytes 1572868
  39.6 14.3 %collective-permute-start.5 = (bf16[1,2,64,2048]{3,2,1,0:T(8,128)(2,1)S(1)}, bf16[1,2,64,2048]{3,2,1,0:T(8,128)(2,1)S(1)}, u32[]{:S(2)}, u32[]{:S(2)}) collective-permute-start(bf16[1,2,64,2048]{3,2,1,0:T(8,128)(2,1)S(1)} %maximum_bitcast_fusion.refs_0_), channel_id=1, source_target_pairs={{0,1},{1,0},{2,3},{3,2},{4,5},{5,4},{6,7},{7,6},{8,9},{9,8},{10,11... | collective-permute-start | bytes 1572872 | tf_op jit(solution)/shard_map/ppermute | solution.py:353
  42.1 11.8 %copy-start.2 = (bf16[1,2,64,2048]{3,2,1,0:T(8,128)(2,1)}, bf16[1,2,64,2048]{3,2,1,0:T(8,128)(2,1)S(1)}, u32[]{:S(2)}) copy-start(bf16[1,2,64,2048]{3,2,1,0:T(8,128)(2,1)S(1)} %maximum_bitcast_fusion.1.refs_3_) | copy-start | bytes 1572868
  42.1 14.0 %collective-permute-start.7 = (bf16[1,2,64,2048]{3,2,1,0:T(8,128)(2,1)S(1)}, bf16[1,2,64,2048]{3,2,1,0:T(8,128)(2,1)S(1)}, u32[]{:S(2)}, u32[]{:S(2)}) collective-permute-start(bf16[1,2,64,2048]{3,2,1,0:T(8,128)(2,1)S(1)} %maximum_bitcast_fusion.1.refs_3_), channel_id=1, source_target_pairs={{0,2},{1,3},{2,0},{3,1},{4,6},{5,7},{6,4},{7,5},{8,10},{9,11},{10,... | collective-permute-start | bytes 1572872 | tf_op jit(solution)/shard_map/ppermute | solution.py:353
  53.9 2.3 copy-start.7
  61.2 3.7 %copy-start.3 = (bf16[1,2,64,2048]{3,2,1,0:T(8,128)(2,1)S(1)}, bf16[1,2,64,2048]{3,2,1,0:T(8,128)(2,1)}, u32[]{:S(2)}) copy-start(bf16[1,2,64,2048]{3,2,1,0:T(8,128)(2,1)} %copy-done.2) | copy-start | bytes 1572868
  61.2 3.7 %copy-start.9 = (bf16[1,2,64,2048]{3,2,1,0:T(8,128)(2,1)S(1)}, bf16[1,2,64,2048]{3,2,1,0:T(8,128)(2,1)}, u32[]{:S(2)}) copy-start(bf16[1,2,64,2048]{3,2,1,0:T(8,128)(2,1)} %copy-done.8) | copy-start | bytes 1572868
  63.4 24.7 %collective-permute-start.10 = (bf16[2,2,64,2048]{3,2,1,0:T(8,128)(2,1)}, bf16[2,2,64,2048]{3,2,1,0:T(8,128)(2,1)}, u32[]{:S(2)}, u32[]{:S(2)}) collective-permute-start(bf16[2,2,64,2048]{3,2,1,0:T(8,128)(2,1)} %pad_maximum_fusion), channel_id=1, source_target_pairs={{0,2},{1,3},{2,0},{3,1},{4,6},{5,7},{6,4},{7,5},{8,10},{9,11},{10,... | collective-permute-start | bytes 3145736 | tf_op jit(solution)/shard_map/ppermute | solution.py:353
  66.0 24.4 %collective-permute-start.11 = (bf16[2,2,64,2048]{3,2,1,0:T(8,128)(2,1)}, bf16[2,2,64,2048]{3,2,1,0:T(8,128)(2,1)}, u32[]{:S(2)}, u32[]{:S(2)}) collective-permute-start(bf16[2,2,64,2048]{3,2,1,0:T(8,128)(2,1)} %pad_maximum_fusion.1), channel_id=1, source_target_pairs={{0,1},{1,0},{2,3},{3,2},{4,5},{5,4},{6,7},{7,6},{8,9},{9,8},{10,11... | collective-permute-start | bytes 3145736 | tf_op jit(solution)/shard_map/ppermute | solution.py:353
  67.6 52.8 %collective-permute-start.16 = (bf16[256,2048]{1,0:T(8,128)(2,1)}, bf16[256,2048]{1,0:T(8,128)(2,1)}, u32[]{:S(2)}, u32[]{:S(2)}) collective-permute-start(bf16[256,2048]{1,0:T(8,128)(2,1)} %refs_0_.1), channel_id=1, source_target_pairs={{8,0},{12,4},{16,8},{20,12},{24,16},{28,20},{9,1},{13,5},{17,9},{2... | collective-permute-start | bytes 3145736 | tf_op jit(solution)/shard_map/ppermute | solution.py:347
  68.9 51.5 %collective-permute-start.17 = (bf16[256,2048]{1,0:T(8,128)(2,1)}, bf16[256,2048]{1,0:T(8,128)(2,1)}, u32[]{:S(2)}, u32[]{:S(2)}) collective-permute-start(bf16[256,2048]{1,0:T(8,128)(2,1)} %refs_0_.1), channel_id=1, source_target_pairs={{0,8},{4,12},{8,16},{12,20},{16,24},{20,28},{1,9},{5,13},{9,17},{1... | collective-permute-start | bytes 3145736 | tf_op jit(solution)/shard_map/ppermute | solution.py:347
  105.4 1.5 copy-start
  113.3 5.1 %collective-permute-start.14 = (f32[16,640]{1,0:T(8,128)}, f32[16,640]{1,0:T(8,128)S(1)}, u32[]{:S(2)}, u32[]{:S(2)}) collective-permute-start(f32[16,640]{1,0:T(8,128)} %token_ranks.1), channel_id=1, source_target_pairs={{0,3},{1,2},{2,1},{3,0},{4,7},{5,6},{6,5},{7,4},{8,11},{9,10},{10,... | collective-permute-start | bytes 122888 | tf_op jit(solution)/shard_map/ppermute | solution.py:353
  113.7 4.7 %collective-permute-start.13 = (f32[16,640]{1,0:T(8,128)}, f32[16,640]{1,0:T(8,128)S(1)}, u32[]{:S(2)}, u32[]{:S(2)}) collective-permute-start(f32[16,640]{1,0:T(8,128)} %token_ranks.1), channel_id=1, source_target_pairs={{0,2},{1,3},{2,0},{3,1},{4,6},{5,7},{6,4},{7,5},{8,10},{9,11},{10,... | collective-permute-start | bytes 122888 | tf_op jit(solution)/shard_map/ppermute | solution.py:353
  115.3 4.2 %collective-permute-start.12 = (f32[16,640]{1,0:T(8,128)}, f32[16,640]{1,0:T(8,128)S(1)}, u32[]{:S(2)}, u32[]{:S(2)}) collective-permute-start(f32[16,640]{1,0:T(8,128)} %token_ranks.1), channel_id=1, source_target_pairs={{0,1},{1,0},{2,3},{3,2},{4,5},{5,4},{6,7},{7,6},{8,9},{9,8},{10,11... | collective-permute-start | bytes 122888 | tf_op jit(solution)/shard_map/ppermute | solution.py:353
  120.3 2.2 copy-start.21
  120.3 2.1 collective-permute-start.15
  120.4 36.0 %collective-permute-start.18 = (bf16[256,2048]{1,0:T(8,128)(2,1)}, bf16[256,2048]{1,0:T(8,128)(2,1)S(1)}, u32[]{:S(2)}, u32[]{:S(2)}) collective-permute-start(bf16[256,2048]{1,0:T(8,128)(2,1)} %collective-permute-done.16.refs_1_), channel_id=1, source_target_pairs={{8,0},{12,4},{16,8},{20,12},{9,1},{13,5},{17,9},{21,13},{10,2},{14... | collective-permute-start | bytes 3145736 | tf_op jit(solution)/shard_map/ppermute | solution.py:347
  121.7 35.5 %collective-permute-start.19 = (bf16[256,2048]{1,0:T(8,128)(2,1)}, bf16[256,2048]{1,0:T(8,128)(2,1)S(1)}, u32[]{:S(2)}, u32[]{:S(2)}) collective-permute-start(bf16[256,2048]{1,0:T(8,128)(2,1)} %collective-permute-done.17.refs_4_), channel_id=1, source_target_pairs={{8,16},{12,20},{16,24},{20,28},{9,17},{13,21},{17,25},{21,29},{10,... | collective-permute-start | bytes 3145736 | tf_op jit(solution)/shard_map/ppermute | solution.py:347
  129.9 16.7 %collective-permute-start.29 = (bf16[128,2048]{1,0:T(8,128)(2,1)}, bf16[128,2048]{1,0:T(8,128)(2,1)S(1)}, u32[]{:S(2)}, u32[]{:S(2)}) collective-permute-start(bf16[128,2048]{1,0:T(8,128)(2,1)} %get-tuple-element.57), channel_id=1, source_target_pairs={{24,16},{28,20},{25,17},{29,21},{26,18},{30,22},{27,19},{31,23}} | collective-permute-start | bytes 1572872 | tf_op jit(solution)/shard_map/ppermute | solution.py:343
  130.6 20.0 %collective-permute-start.23 = (bf16[128,2048]{1,0:T(8,128)(2,1)}, bf16[128,2048]{1,0:T(8,128)(2,1)S(1)}, u32[]{:S(2)}, u32[]{:S(2)}) collective-permute-start(bf16[128,2048]{1,0:T(8,128)(2,1)} %get-tuple-element.59), channel_id=1, source_target_pairs={{0,8},{4,12},{1,9},{5,13},{2,10},{6,14},{3,11},{7,15}} | collective-permute-start | bytes 1572872 | tf_op jit(solution)/shard_map/ppermute | solution.py:339
  138.0 8.7 %copy-start.18 = (bf16[128,2048]{1,0:T(8,128)(2,1)S(1)}, bf16[128,2048]{1,0:T(8,128)(2,1)}, u32[]{:S(2)}) copy-start(bf16[128,2048]{1,0:T(8,128)(2,1)} %get-tuple-element.50) | copy-start | bytes 1572868
  138.0 23.8 %collective-permute-start.20 = (bf16[128,2048]{1,0:T(8,128)(2,1)}, bf16[128,2048]{1,0:T(8,128)(2,1)S(1)}, u32[]{:S(2)}, u32[]{:S(2)}) collective-permute-start(bf16[128,2048]{1,0:T(8,128)(2,1)} %get-tuple-element.56), channel_id=1, source_target_pairs={{0,8},{4,12},{1,9},{5,13},{2,10},{6,14},{3,11},{7,15}} | collective-permute-start | bytes 1572872 | tf_op jit(solution)/shard_map/ppermute | solution.py:339
  146.7 15.2 %copy-start.5 = (bf16[128,2048]{1,0:T(8,128)(2,1)S(1)}, bf16[128,2048]{1,0:T(8,128)(2,1)}, u32[]{:S(2)}) copy-start(bf16[128,2048]{1,0:T(8,128)(2,1)} %get-tuple-element.60) | copy-start | bytes 1572868
  146.7 21.7 %collective-permute-start.26 = (bf16[128,2048]{1,0:T(8,128)(2,1)S(1)}, bf16[128,2048]{1,0:T(8,128)(2,1)S(1)}, u32[]{:S(2)}, u32[]{:S(2)}) collective-permute-start(bf16[128,2048]{1,0:T(8,128)(2,1)S(1)} %copy-done.18), channel_id=1, source_target_pairs={{24,16},{28,20},{25,17},{29,21},{26,18},{30,22},{27,19},{31,23}} | collective-permute-start | bytes 1572872 | tf_op jit(solution)/shard_map/ppermute | solution.py:343
  152.0 21.9 %copy-start.20 = (bf16[128,2048]{1,0:T(8,128)(2,1)S(1)}, bf16[128,2048]{1,0:T(8,128)(2,1)}, u32[]{:S(2)}) copy-start(bf16[128,2048]{1,0:T(8,128)(2,1)} %get-tuple-element.57) | copy-start | bytes 1572868
  152.0 21.0 %collective-permute-start.24 = (bf16[128,2048]{1,0:T(8,128)(2,1)S(1)}, bf16[128,2048]{1,0:T(8,128)(2,1)S(1)}, u32[]{:S(2)}, u32[]{:S(2)}) collective-permute-start(bf16[128,2048]{1,0:T(8,128)(2,1)S(1)} %get-tuple-element.91), channel_id=1, source_target_pairs={{0,8},{4,12},{8,16},{12,20},{1,9},{5,13},{9,17},{13,21},{2,10},{6,... | collective-permute-start | bytes 1572872 | tf_op jit(solution)/shard_map/ppermute | solution.py:339
  156.4 17.6 %copy-start.11 = (bf16[256,2048]{1,0:T(8,128)(2,1)}, bf16[256,2048]{1,0:T(8,128)(2,1)S(1)}, u32[]{:S(2)}) copy-start(bf16[256,2048]{1,0:T(8,128)(2,1)S(1)} %collective-permute-done.18.refs_2_) | copy-start | bytes 3145732
  156.5 17.6 %collective-permute-start.30 = (bf16[128,2048]{1,0:T(8,128)(2,1)S(1)}, bf16[128,2048]{1,0:T(8,128)(2,1)S(1)}, u32[]{:S(2)}, u32[]{:S(2)}) collective-permute-start(bf16[128,2048]{1,0:T(8,128)(2,1)S(1)} %get-tuple-element.90), channel_id=1, source_target_pairs={{16,8},{20,12},{24,16},{28,20},{17,9},{21,13},{25,17},{29,21},{18,... | collective-permute-start | bytes 1572872 | tf_op jit(solution)/shard_map/ppermute | solution.py:343
  157.2 16.8 %copy-start.12 = (bf16[256,2048]{1,0:T(8,128)(2,1)}, bf16[256,2048]{1,0:T(8,128)(2,1)S(1)}, u32[]{:S(2)}) copy-start(bf16[256,2048]{1,0:T(8,128)(2,1)S(1)} %collective-permute-done.19.refs_5_) | copy-start | bytes 3145732
  157.2 21.9 %copy-start.19 = (bf16[128,2048]{1,0:T(8,128)(2,1)S(1)}, bf16[128,2048]{1,0:T(8,128)(2,1)}, u32[]{:S(2)}) copy-start(bf16[128,2048]{1,0:T(8,128)(2,1)} %get-tuple-element.59) | copy-start | bytes 1572868
  162.8 39.7 %collective-permute-start.21 = (bf16[128,2048]{1,0:T(8,128)(2,1)}, bf16[128,2048]{1,0:T(8,128)(2,1)S(1)}, u32[]{:S(2)}, u32[]{:S(2)}) collective-permute-start(bf16[128,2048]{1,0:T(8,128)(2,1)} %add_convert_fusion.7), channel_id=1, source_target_pairs={{0,8},{4,12},{8,16},{12,20},{1,9},{5,13},{9,17},{13,21},{2,10},{6,... | collective-permute-start | bytes 1572872 | tf_op jit(solution)/shard_map/ppermute | solution.py:339
  167.1 24.3 %collective-permute-start.32 = (bf16[256,2048]{1,0:T(8,128)(2,1)S(1)}, bf16[256,2048]{1,0:T(8,128)(2,1)S(1)}, u32[]{:S(2)}, u32[]{:S(2)}) collective-permute-start(bf16[256,2048]{1,0:T(8,128)(2,1)S(1)} %collective-permute-done.18.refs_2_), channel_id=1, source_target_pairs={{8,0},{12,4},{9,1},{13,5},{10,2},{14,6},{11,3},{15,7}} | collective-permute-start | bytes 3145736 | tf_op jit(solution)/shard_map/ppermute | solution.py:347
  168.4 23.0 %collective-permute-start.33 = (bf16[256,2048]{1,0:T(8,128)(2,1)S(1)}, bf16[256,2048]{1,0:T(8,128)(2,1)S(1)}, u32[]{:S(2)}, u32[]{:S(2)}) collective-permute-start(bf16[256,2048]{1,0:T(8,128)(2,1)S(1)} %collective-permute-done.19.refs_5_), channel_id=1, source_target_pairs={{16,24},{20,28},{17,25},{21,29},{18,26},{22,30},{19,27},{23,31}} | collective-permute-start | bytes 3145736 | tf_op jit(solution)/shard_map/ppermute | solution.py:347
  173.0 38.7 %collective-permute-start.27 = (bf16[128,2048]{1,0:T(8,128)(2,1)S(1)}, bf16[128,2048]{1,0:T(8,128)(2,1)S(1)}, u32[]{:S(2)}, u32[]{:S(2)}) collective-permute-start(bf16[128,2048]{1,0:T(8,128)(2,1)S(1)} %add_convert_fusion.4), channel_id=1, source_target_pairs={{16,8},{20,12},{24,16},{28,20},{17,9},{21,13},{25,17},{29,21},{18,... | collective-permute-start | bytes 1572872 | tf_op jit(solution)/shard_map/ppermute | solution.py:343
  174.0 53.5 %collective-permute-start.25 = (bf16[128,2048]{1,0:T(8,128)(2,1)S(1)}, bf16[128,2048]{1,0:T(8,128)(2,1)S(1)}, u32[]{:S(2)}, u32[]{:S(2)}) collective-permute-start(bf16[128,2048]{1,0:T(8,128)(2,1)S(1)} %add_convert_fusion.5), channel_id=1, source_target_pairs={{0,8},{4,12},{8,16},{12,20},{16,24},{20,28},{1,9},{5,13},{9,17},{1... | collective-permute-start | bytes 1572872 | tf_op jit(solution)/shard_map/ppermute | solution.py:339
  191.4 1.0 copy-start.13
  191.4 1.3 copy-start.14
  199.5 12.7 %copy-start.17 = (bf16[128,2048]{1,0:T(8,128)(2,1)S(1)}, bf16[128,2048]{1,0:T(8,128)(2,1)}, u32[]{:S(2)}) copy-start(bf16[128,2048]{1,0:T(8,128)(2,1)} %get-tuple-element.56) | copy-start | bytes 1572868
  199.5 5.3 %collective-permute-start.36 = (f32[2,16,320]{2,1,0:T(8,128)}, f32[2,16,320]{2,1,0:T(8,128)S(1)}, u32[]{:S(2)}, u32[]{:S(2)}) collective-permute-start(f32[2,16,320]{2,1,0:T(8,128)} %get-tuple-element.63), channel_id=1, source_target_pairs={{0,3},{1,2},{2,1},{3,0},{4,7},{5,6},{6,5},{7,4},{8,11},{9,10},{10,... | collective-permute-start | bytes 122888 | tf_op jit(solution)/shard_map/ppermute | solution.py:353
  200.7 5.5 %collective-permute-start.35 = (f32[2,16,320]{2,1,0:T(8,128)}, f32[2,16,320]{2,1,0:T(8,128)S(1)}, u32[]{:S(2)}, u32[]{:S(2)}) collective-permute-start(f32[2,16,320]{2,1,0:T(8,128)} %get-tuple-element.63), channel_id=1, source_target_pairs={{0,2},{1,3},{2,0},{3,1},{4,6},{5,7},{6,4},{7,5},{8,10},{9,11},{10,... | collective-permute-start | bytes 122888 | tf_op jit(solution)/shard_map/ppermute | solution.py:353
  202.5 8.2 %collective-permute-start.34 = (f32[2,16,320]{2,1,0:T(8,128)}, f32[2,16,320]{2,1,0:T(8,128)S(1)}, u32[]{:S(2)}, u32[]{:S(2)}) collective-permute-start(f32[2,16,320]{2,1,0:T(8,128)} %get-tuple-element.63), channel_id=1, source_target_pairs={{0,1},{1,0},{2,3},{3,2},{4,5},{5,4},{6,7},{7,6},{8,9},{9,8},{10,11... | collective-permute-start | bytes 122888 | tf_op jit(solution)/shard_map/ppermute | solution.py:353
  204.8 22.7 %collective-permute-start.31 = (bf16[128,2048]{1,0:T(8,128)(2,1)S(1)}, bf16[128,2048]{1,0:T(8,128)(2,1)S(1)}, u32[]{:S(2)}, u32[]{:S(2)}) collective-permute-start(bf16[128,2048]{1,0:T(8,128)(2,1)S(1)} %add_convert_fusion.2), channel_id=1, source_target_pairs={{8,0},{12,4},{16,8},{20,12},{24,16},{28,20},{9,1},{13,5},{17,9},{2... | collective-permute-start | bytes 1572872 | tf_op jit(solution)/shard_map/ppermute | solution.py:343
  206.1 21.4 %collective-permute-start.22 = (bf16[128,2048]{1,0:T(8,128)(2,1)S(1)}, bf16[128,2048]{1,0:T(8,128)(2,1)S(1)}, u32[]{:S(2)}, u32[]{:S(2)}) collective-permute-start(bf16[128,2048]{1,0:T(8,128)(2,1)S(1)} %add_convert_fusion.6), channel_id=1, source_target_pairs={{0,8},{4,12},{8,16},{12,20},{16,24},{20,28},{1,9},{5,13},{9,17},{1... | collective-permute-start | bytes 1572872 | tf_op jit(solution)/shard_map/ppermute | solution.py:339
  210.7 5.1 %collective-permute-start.38 = (bf16[320,2048]{1,0:T(8,128)(2,1)}, bf16[320,2048]{1,0:T(8,128)(2,1)S(1)}, u32[]{:S(2)}, u32[]{:S(2)}) collective-permute-start(bf16[320,2048]{1,0:T(8,128)(2,1)} %get-tuple-element.65), channel_id=1, source_target_pairs={{0,4},{4,0},{8,12},{12,8},{16,20},{20,16},{24,28},{28,24},{1,5},{5... | collective-permute-start | bytes 3932168 | tf_op jit(solution)/shard_map/ppermute | solution.py:350
  211.7 2.2 collective-permute-start.37
  213.9 15.8 %collective-permute-start.28 = (bf16[128,2048]{1,0:T(8,128)(2,1)S(1)}, bf16[128,2048]{1,0:T(8,128)(2,1)S(1)}, u32[]{:S(2)}, u32[]{:S(2)}) collective-permute-start(bf16[128,2048]{1,0:T(8,128)(2,1)S(1)} %add_convert_fusion.3), channel_id=1, source_target_pairs={{8,0},{12,4},{16,8},{20,12},{24,16},{28,20},{9,1},{13,5},{17,9},{2... | collective-permute-start | bytes 1572872 | tf_op jit(solution)/shard_map/ppermute | solution.py:343
  215.8 1.1 copy-start.10
  216.9 12.8 %copy-start.16 = (f32[128,2048]{1,0:T(8,128)S(1)}, f32[128,2048]{1,0:T(8,128)}, u32[]{:S(2)}) copy-start(f32[128,2048]{1,0:T(8,128)} %get-tuple-element.69) | copy-start | bytes 3145732
  227.5 2.4 %copy-start.15 = (f32[128,2048]{1,0:T(8,128)S(1)}, f32[128,2048]{1,0:T(8,128)}, u32[]{:S(2)}) copy-start(f32[128,2048]{1,0:T(8,128)} %get-tuple-element.49) | copy-start | bytes 3145732
  (2 other events, 1.4 us)

commit v4 on v3

--- a/solution.py
+++ b/solution.py
@@ -269,16 +269,17 @@
 
 
 def gradients_kernel(per_owner, blocks, order_ref, local_ref, grad_ranks_ref, up_ranks_ref, own_ref, other_ref, *refs):
-    grad, (down_ref, up_ref, wide_grad, wide_up) = refs[:blocks], refs[blocks:]
+    grad, (down_ref, up_ref, flat_grad, wide_up) = refs[:blocks], refs[blocks:]
 
     @pl.when(pl.program_id(0) == 0)
     def _():
         local = local_ref[...]
-        spread_rows(wide_grad, 0, local, grad_ranks_ref[...].astype(F32), per_owner)
+        spread_rows(wide_up, 0, local, grad_ranks_ref[...].astype(F32), per_owner)
+        flat_grad[...] = wide_up[...].T
         spread_rows(wide_up, 0, local, up_ranks_ref[...].astype(F32), per_owner)
 
     rows = jnp.concatenate([own_ref[...], other_ref[...]], axis=0)
-    down_ref[...] = jnp.dot(wide_grad[...], rows, preferred_element_type=F32).T
+    down_ref[...] = lax.dot_general(rows, flat_grad[...], (((0,), (0,)), ((), ())), preferred_element_type=F32)
     rows = jnp.concatenate([piece[...] for piece in grad], axis=0)
     up_ref[...] = jnp.dot(wide_up[...], rows, preferred_element_type=F32)
 
@@ -307,7 +308,7 @@
                 pl.BlockSpec((tile, rank_cols), lambda n, order: (n, 0)),
                 pl.BlockSpec((rank_cols, tile), column),
             ),
-            scratch_shapes=[pltpu.VMEM((rank_cols, total), BF16)] * 2,
+            scratch_shapes=[pltpu.VMEM((total, rank_cols), BF16), pltpu.VMEM((rank_cols, total), BF16)],
         ),
         compiler_params=params(),
         cost_estimate=cost(4 * total * width * rank_cols, 4 * total * width + 8 * rank_cols * width),
@@ -415,21 +416,23 @@
     other_weight = swap(weight)
     other_down_t = swap(down_t)
 
-    all_owner, all_place = placing(all_ids)
     ahead = [2 * ((plane + jnp.arange(planes)) % planes) + c for c in (core, 1 - core)]
     slot_order = jnp.concatenate(ahead)
+    near_ids = all_ids[slot_order]
+    near_owner, near_place = placing(near_ids)
 
     def labels(owner, blocks):
-        mine = (all_owner[blocks] == owner)[:, None, :]
-        mine &= all_place[blocks][:, None, :] == jnp.arange(capacity, dtype=I32)[:, None]
-        from_first = all_ids[blocks][:, None, :] - owner * per_owner
+        mine = (near_owner[blocks] == owner)[:, None, :]
+        mine &= near_place[blocks][:, None, :] == jnp.arange(capacity, dtype=I32)[:, None]
+        from_first = near_ids[blocks][:, None, :] - owner * per_owner
         return (jnp.sum(jnp.where(mine, from_first + 1, 0), axis=-1) - 1).reshape(1, -1)
 
-    here, there = (labels(me, blocks) for blocks in ahead)
+    parity = slice(0, planes)
+    here, there = labels(me, parity), labels(me, slice(planes, owners))
     local = jnp.concatenate([here, there], axis=1)
-    parity_local = jnp.concatenate([here, labels(me ^ 1, ahead[0])], axis=0)
-
-    parity_ids, parity_owner, parity_place = (x[ahead[0]] for x in (all_ids, all_owner, all_place))
+    parity_local = jnp.concatenate([here, labels(me ^ 1, parity)], axis=0)
+
+    parity_ids, parity_owner, parity_place = near_ids[parity], near_owner[parity], near_place[parity]
     attn_places = jnp.where(parity_owner == me, parity_place, -1)
     attn_places = jnp.where(parity_owner == (me ^ 1), parity_place + capacity, attn_places).reshape(1, -1)
     base = capacity * jnp.arange(planes, dtype=I32)[:, None]
@@ -461,7 +464,7 @@
     below, above = [going_down], [going_up]
     for d in range(2, planes):
         if d == 2:
-            going_down, going_up = after((going_down, going_up), part_grads)
+            going_down, going_up = after((going_down, going_up), *pairs)
         going_down, going_up = attn_line(going_down, d, -1), attn_line(going_up, d, 1)
         below.append(going_down)
         above.append(going_up)
@@ -471,12 +474,11 @@
     for d in range(planes - 1, 0, -1):
         for i in range(2):
             up_sum, down_sum = sums[d][i], sums[planes - d][i]
-            if d == planes - 2 and i == 0:
-                up_sum, down_sum = after((up_sum, down_sum), below[1], above[1])
             if going_up[i] is not None:
                 up_sum = (up_sum.astype(F32) + going_up[i].astype(F32)).astype(BF16)
                 down_sum = (down_sum.astype(F32) + going_down[i].astype(F32)).astype(BF16)
-            last_sums = (up_sum, down_sum)
+            if i == 0:
+                last_sums = (up_sum, down_sum)
             going_up[i], going_down[i] = up_line(up_sum, d), down_line(down_sum, d)
     below[-1], above[-1] = after((below[-1], above[-1]), *last_sums)
     attn_own, attn_other, parity_inputs = repack(

time: 233 us -> 224 us (0.961)
  local copies, waits for them, and re-layouts: 16.3 us -> 12 us
    ppermute x6, waiting for transfers between devices: 12.2 us -> 3.31 us  [attn_line(): lax.ppermute(x, 'adapter', [(2 * z + c, 2 * (z + way) + c) for z in plane...]
    ppermute x6, waiting for transfers between devices: 2.12 us -> 8.71 us  [down_line(): return lax.ppermute(x, 'adapter', pairs)]
    gather x6 -> x1, local copies, waits for them, and re-layouts: 3.37 us -> 0.56 us  [per_device(): near_ids = all_ids[slot_order]]
    unnamed x54 -> x48, local copies, waits for them, and re-layouts: 8.94 us -> 8.16 us
  transfers between devices with their start and end apart: 41 -> 41, of which waited for: 15 -> 18; matrix products, arithmetic and copies ran while one was open for 11% -> 9% of each run, Pallas kernels for 24% -> 25%
where the time goes in v4:
time: 224 us; the launch traced here: 223 us
  starting transfers between devices  76.5 us (34%)
  waiting for transfers between devices  62.1 us (28%)
  Pallas kernels  55.7 us (25%)
  other arithmetic  15.3 us (7%)
  local copies, waits for them, and re-layouts  12 us (5%)
    ppermute x13, waiting for transfers between devices, flip(): return lax.ppermute(x, 'tensor', [(t, t ^ k) for t in range(tensors)])  31.1 us
    ppermute x6, starting transfers between devices, up_line(): return lax.ppermute(x, 'adapter', pairs)  26.1 us
    ppermute x13, starting transfers between devices, flip(): return lax.ppermute(x, 'tensor', [(t, t ^ k) for t in range(tensors)])  16.8 us
    pallas_call x1, Pallas kernels, frozen_part(): pl.pallas_call(functools.partial(frozen_kernel, names), grid=(width // ti...  14.9 us
    pallas_call x2, Pallas kernels, add_term(): pl.pallas_call(functools.partial(term_kernel, per_owner), grid=(width //...  14.2 us
    ppermute x6, waiting for transfers between devices, up_line(): return lax.ppermute(x, 'adapter', pairs)  11.4 us
    ppermute x6, starting transfers between devices, attn_line(): lax.ppermute(x, 'adapter', [(2 * z + c, 2 * (z + way) + c) for z in plane...  11 us
    pallas_call x1, Pallas kernels, adapter_gradients(): pl.pallas_call(functools.partial(gradients_kernel, per_owner, blocks), ou...  10.2 us
  transfers between devices with their start and end apart: 41, of which 18 were waited for; matrix products, arithmetic and copies ran while one was open for 9% of the time, Pallas kernels for 25%

profile of v4, /device:TPU:0, one launch (start us, length us, event | category | flops | bytes accessed | tf_op | source)
XLA Modules:
  0.0 223.0 jit_solution(2001467428842727734)
XLA Ops:
  0.7 2.3 %constant_dynamic-slice_fusion.8 = (bf16[64,2048]{1,0:T(8,128)(2,1)}, bf16[64,2048]{1,0:T(8,128)(2,1)}, bf16[64,2048]{1,0:T(8,128)(2,1)}, bf16[64,2048]{1,0:T(8,128)(2,1)}) fusion(bf16[64,8192]{1,0:T(8,128)(2,1)} %param.7, s32[]{:T(128)S(6)} %select_n.162, s32[]{:T(128)S(6)} %select_n.161, s32[]{:T(128)S(6)} %select_n.160, s32[]{:T(128)S(6)} %select_n.159), kind=kLoop, calls=%fused_computation.74 | loop fusion | bytes 2097168 | tf_op jit(solution)/shard_map/dynamic_slice | solution.py:360
  2.9 3.0 %collective-permute-start = (bf16[64,2048]{1,0:T(8,128)(2,1)}, bf16[64,2048]{1,0:T(8,128)(2,1)}, u32[]{:S(2)}, u32[]{:S(2)}) collective-permute-start(bf16[64,2048]{1,0:T(8,128)(2,1)} %get-tuple-element.84), channel_id=1, source_target_pairs={{0,1},{1,0},{2,3},{3,2},{4,5},{5,4},{6,7},{7,6},{8,9},{9,8},{10,11... | collective-permute-start | bytes 786440 | tf_op jit(solution)/shard_map/ppermute | solution.py:354
  5.9 1.5 collective-permute-start.1
  7.5 2.1 collective-permute-start.4
  9.7 2.1 collective-permute-start.3
  12.0 1.4 collective-permute-done.refs_1_
  13.3 3.2 %collective-permute-start.6 = (bf16[64,2048]{1,0:T(8,128)(2,1)S(1)}, bf16[64,2048]{1,0:T(8,128)(2,1)}, u32[]{:S(2)}, u32[]{:S(2)}) collective-permute-start(bf16[64,2048]{1,0:T(8,128)(2,1)S(1)} %pad_maximum_fusion.5), channel_id=1, source_target_pairs={{0,16},{4,20},{8,24},{12,28},{16,0},{20,4},{24,8},{28,12},{1,17},{... | collective-permute-start | bytes 786440 | tf_op jit(solution)/shard_map/ppermute | solution.py:336
  16.5 2.4 %copy.11 = bf16[2048,512]{0,1:T(8,128)(2,1)} copy(bf16[2048,512]{1,0:T(8,128)(2,1)S(1)} %copy-done.4) | data formatting | bytes 4194304 | tf_op args[4]
  20.7 4.9 %all-to-all-start = ((s32[8,1,256]{2,1,0:T(1,128)}), s32[8,1,256]{2,1,0:T(1,128)S(1)}, u32[]{:S(2)}, u32[]{:S(2)}) async-start(s32[8,1,256]{2,1,0:T(1,128)} %broadcast_in_dim.59), calls=%async_computation | async-start | bytes 16384 | tf_op jit(solution)/shard_map/all_to_all | solution.py:381
  26.2 3.2 %pack_rows.1 = bf16[640,2048]{1,0:T(8,128)(2,1)} custom-call(s32[1,256]{1,0:T(1,128)} %bitcast.63, bf16[64,2048]{1,0:T(8,128)(2,1)} %get-tuple-element.41.refs_0_, bf16[64,2048]{1,0:T(8,128)(2,1)} %collective-permute-done.refs_1_, bf16[64,2048]{1,0:T(8,128)(2,1)} %collective-permute-done.1.refs_2_, bf16[64,2048]{1,0:T(8,128)(2,1)} %collective-permute-done.2.refs_3_), custom_call_target="tpu_custom_call" | custom-call | flops 10485760 | bytes 57344 | tf_op jit(solution)/shard_map/pack_rows/pallas_call | solution.py:43
  29.4 4.8 %collective-permute-done.6 = bf16[64,2048]{1,0:T(8,128)(2,1)} collective-permute-done((bf16[64,2048]{1,0:T(8,128)(2,1)S(1)}, bf16[64,2048]{1,0:T(8,128)(2,1)}, u32[]{:S(2)}, u32[]{:S(2)}) %collective-permute-start.6) | collective-permute-done | bytes 262176 | tf_op jit(solution)/shard_map/ppermute | solution.py:336
  34.2 3.6 %all-to-all-start.1 = ((bf16[8,80,2048]{2,1,0:T(8,128)(2,1)}), bf16[8,80,2048]{2,1,0:T(8,128)(2,1)S(1)}, u32[]{:S(2)}, u32[]{:S(2)}) async-start(bf16[8,80,2048]{2,1,0:T(8,128)(2,1)} %bitcast.57), calls=%async_computation.1 | async-start | bytes 5242880 | tf_op jit(solution)/shard_map/all_to_all | solution.py:400
  37.9 1.0 maximum_bitcast_fusion.refs_0_
  38.9 1.6 collective-permute-start.5
  40.5 1.0 maximum_bitcast_fusion.1.refs_3_
  41.5 1.6 collective-permute-start.7
  43.9 9.4 %collective-permute-done.5.refs_1_ = bf16[1,2,64,2048]{3,2,1,0:T(8,128)(2,1)S(1)} collective-permute-done((bf16[1,2,64,2048]{3,2,1,0:T(8,128)(2,1)S(1)}, bf16[1,2,64,2048]{3,2,1,0:T(8,128)(2,1)S(1)}, u32[]{:S(2)}, u32[]{:S(2)}) %collective-permute-start.5) | collective-permute-done | bytes 524320 | tf_op jit(solution)/shard_map/ppermute | solution.py:354
  53.2 2.3 %collective-permute-done.7.refs_4_ = bf16[1,2,64,2048]{3,2,1,0:T(8,128)(2,1)S(1)} collective-permute-done((bf16[1,2,64,2048]{3,2,1,0:T(8,128)(2,1)S(1)}, bf16[1,2,64,2048]{3,2,1,0:T(8,128)(2,1)S(1)}, u32[]{:S(2)}, u32[]{:S(2)}) %collective-permute-start.7) | collective-permute-done | bytes 524320 | tf_op jit(solution)/shard_map/ppermute | solution.py:354
  55.5 1.1 pad_maximum_fusion
  56.7 1.5 collective-permute-start.10
  58.2 1.1 pad_maximum_fusion.1
  60.5 0.8 convert_reduce_fusion
  62.3 1.3 collective-permute-start.28
  63.6 5.5 %collective-permute-start.29 = (bf16[256,2048]{1,0:T(8,128)(2,1)}, bf16[256,2048]{1,0:T(8,128)(2,1)}, u32[]{:S(2)}, u32[]{:S(2)}) collective-permute-start(bf16[256,2048]{1,0:T(8,128)(2,1)} %refs_0_.1), channel_id=1, source_target_pairs={{0,8},{4,12},{8,16},{12,20},{16,24},{20,28},{1,9},{5,13},{9,17},{1... | collective-permute-start | bytes 3145736 | tf_op jit(solution)/shard_map/ppermute | solution.py:348
  71.4 9.9 %collective-permute-done.10.refs_2_ = bf16[2,2,64,2048]{3,2,1,0:T(8,128)(2,1)} collective-permute-done((bf16[2,2,64,2048]{3,2,1,0:T(8,128)(2,1)}, bf16[2,2,64,2048]{3,2,1,0:T(8,128)(2,1)}, u32[]{:S(2)}, u32[]{:S(2)}) %collective-permute-start.10) | collective-permute-done | bytes 1048608 | tf_op jit(solution)/shard_map/ppermute | solution.py:354
  81.4 2.4 %collective-permute-done.11.refs_5_ = bf16[2,2,64,2048]{3,2,1,0:T(8,128)(2,1)} collective-permute-done((bf16[2,2,64,2048]{3,2,1,0:T(8,128)(2,1)}, bf16[2,2,64,2048]{3,2,1,0:T(8,128)(2,1)}, u32[]{:S(2)}, u32[]{:S(2)}) %collective-permute-start.11) | collective-permute-done | bytes 1048608 | tf_op jit(solution)/shard_map/ppermute | solution.py:354
  83.8 14.9 %frozen_part.1.frozen_ref = f32[1024,2048]{1,0:T(8,128)} custom-call(s32[1]{0:T(128)} %bitcast.place_ref, bf16[2048,1024]{1,0:T(8,128)(2,1)} %own_w_ref, bf16[2048,1024]{1,0:T(8,128)(2,1)} %collective-permute-done.9.other_w_ref, bf16[1,2,64,2048]{3,2,1,0:T(8,128)(2,1)} %copy-done.1, bf16[1,2,64,2048]{3,2,1,0:T(8,128)(2,1)} %copy-done.5, ...), custom_call_target="tpu_custom_call" | custom-call | flops 134217728 | bytes 262144 | tf_op jit(solution)/shard_map/frozen_part/pallas_call | solution.py:208
  98.7 1.5 copy-done
  100.2 6.4 %token_ranks.1 = f32[16,640]{1,0:T(8,128)} custom-call(s32[8]{0:T(128)} %pad_add_fusion.4.order_ref, s32[1,640]{1,0:T(1,128)} %pad_add_fusion.2.local_ref, bf16[512,2048]{1,0:T(8,128)(2,1)} %weight_ref.1, bf16[640,2048]{1,0:T(8,128)(2,1)} %bitcast.41, bf16[640,2048]{1,0:T(8,128)(2,1)} %bitcast.42, bf16[640,2048]{1,0:T(8,128)(2,1)} %bitcast.43, ...), custom_call_target="tpu_custom_call" | custom-call | flops 20971520 | bytes 73728 | tf_op jit(solution)/shard_map/token_ranks/pallas_call | solution.py:153
  106.6 2.3 %collective-permute-start.14 = (f32[16,640]{1,0:T(8,128)}, f32[16,640]{1,0:T(8,128)S(1)}, u32[]{:S(2)}, u32[]{:S(2)}) collective-permute-start(f32[16,640]{1,0:T(8,128)} %token_ranks.1), channel_id=1, source_target_pairs={{0,3},{1,2},{2,1},{3,0},{4,7},{5,6},{6,5},{7,4},{8,11},{9,10},{10,... | collective-permute-start | bytes 122888 | tf_op jit(solution)/shard_map/ppermute | solution.py:354
  110.1 1.6 collective-permute-done.14
  111.7 1.4 collective-permute-done.13
  113.6 0.8 multiply_convert_fusion.1.refs_0_.grad_ranks_ref
  114.5 1.2 collective-permute-done.15.refs_1_
  116.3 6.9 %add_term.3 = (bf16[128,2048]{1,0:T(8,128)(2,1)}, bf16[128,2048]{1,0:T(8,128)(2,1)}, bf16[128,2048]{1,0:T(8,128)(2,1)}, bf16[128,2048]{1,0:T(8,128)(2,1)}) custom-call(f32[1024,2048]{1,0:T(8,128)} %frozen_part.1.frozen_ref, s32[4,1024]{1,0:T(4,128)} %bitcast.60, bf16[16,640]{1,0:T(8,128)(2,1)} %copy-done.19, bf16[16,640]{1,0:T(8,128)(2,1)} %copy-done.20, ...), custom_call_target="tpu_custom_call" | custom-call | flops 33554432 | bytes 163840 | tf_op jit(solution)/shard_map/add_term/pallas_call | solution.py:253
  123.2 1.4 collective-permute-start.30
  126.1 6.4 %collective-permute-start.16 = (bf16[128,2048]{1,0:T(8,128)(2,1)}, bf16[128,2048]{1,0:T(8,128)(2,1)S(1)}, u32[]{:S(2)}, u32[]{:S(2)}) collective-permute-start(bf16[128,2048]{1,0:T(8,128)(2,1)} %get-tuple-element.50), channel_id=1, source_target_pairs={{0,8},{4,12},{1,9},{5,13},{2,10},{6,14},{3,11},{7,15}} | collective-permute-start | bytes 1572872 | tf_op jit(solution)/shard_map/ppermute | solution.py:340
  133.1 7.3 %add_term.2 = (bf16[128,2048]{1,0:T(8,128)(2,1)}, bf16[128,2048]{1,0:T(8,128)(2,1)}, f32[128,2048]{1,0:T(8,128)}, f32[128,2048]{1,0:T(8,128)}) custom-call(f32[1024,2048]{1,0:T(8,128)} %frozen_part.1.frozen_ref, s32[4,1024]{1,0:T(4,128)} %bitcast.61, bf16[16,640]{1,0:T(8,128)(2,1)} %copy-done.19, bf16[16,640]{1,0:T(8,128)(2,1)} %copy-done.20, ...), custom_call_target="tpu_custom_call" | custom-call | flops 33554432 | bytes 163840 | tf_op jit(solution)/shard_map/add_term/pallas_call | solution.py:253
  140.5 1.5 collective-permute-start.19
  141.9 3.1 %collective-permute-done.16 = bf16[128,2048]{1,0:T(8,128)(2,1)S(1)} collective-permute-done((bf16[128,2048]{1,0:T(8,128)(2,1)}, bf16[128,2048]{1,0:T(8,128)(2,1)S(1)}, u32[]{:S(2)}, u32[]{:S(2)}) %collective-permute-start.16) | collective-permute-done | bytes 524320 | tf_op jit(solution)/shard_map/ppermute | solution.py:340
  145.1 1.4 fusion.1
  146.5 4.3 %collective-permute-start.17 = (bf16[128,2048]{1,0:T(8,128)(2,1)S(1)}, bf16[128,2048]{1,0:T(8,128)(2,1)S(1)}, u32[]{:S(2)}, u32[]{:S(2)}) collective-permute-start(bf16[128,2048]{1,0:T(8,128)(2,1)S(1)} %get-tuple-element.89), channel_id=1, source_target_pairs={{0,8},{4,12},{8,16},{12,20},{1,9},{5,13},{9,17},{13,21},{2,10},{6,... | collective-permute-start | bytes 1572872 | tf_op jit(solution)/shard_map/ppermute | solution.py:340
  151.5 1.3 collective-permute-start.31
  153.6 2.6 %collective-permute-done.19 = bf16[128,2048]{1,0:T(8,128)(2,1)S(1)} collective-permute-done((bf16[128,2048]{1,0:T(8,128)(2,1)S(1)}, bf16[128,2048]{1,0:T(8,128)(2,1)S(1)}, u32[]{:S(2)}, u32[]{:S(2)}) %collective-permute-start.19) | collective-permute-done | bytes 524320 | tf_op jit(solution)/shard_map/ppermute | solution.py:340
  156.2 1.1 fusion.3
  157.3 4.4 %collective-permute-start.20 = (bf16[128,2048]{1,0:T(8,128)(2,1)}, bf16[128,2048]{1,0:T(8,128)(2,1)S(1)}, u32[]{:S(2)}, u32[]{:S(2)}) collective-permute-start(bf16[128,2048]{1,0:T(8,128)(2,1)} %get-tuple-element.87), channel_id=1, source_target_pairs={{0,8},{4,12},{8,16},{12,20},{1,9},{5,13},{9,17},{13,21},{2,10},{6,... | collective-permute-start | bytes 1572872 | tf_op jit(solution)/shard_map/ppermute | solution.py:340
  161.8 5.7 %collective-permute-done.17 = bf16[128,2048]{1,0:T(8,128)(2,1)S(1)} collective-permute-done((bf16[128,2048]{1,0:T(8,128)(2,1)S(1)}, bf16[128,2048]{1,0:T(8,128)(2,1)S(1)}, u32[]{:S(2)}, u32[]{:S(2)}) %collective-permute-start.17) | collective-permute-done | bytes 524320 | tf_op jit(solution)/shard_map/ppermute | solution.py:340
  167.4 0.9 collective-permute-start.26
  168.5 5.0 %collective-permute-start.18 = (bf16[128,2048]{1,0:T(8,128)(2,1)S(1)}, bf16[128,2048]{1,0:T(8,128)(2,1)S(1)}, u32[]{:S(2)}, u32[]{:S(2)}) collective-permute-start(bf16[128,2048]{1,0:T(8,128)(2,1)S(1)} %add_convert_fusion.5), channel_id=1, source_target_pairs={{0,8},{4,12},{8,16},{12,20},{16,24},{20,28},{1,9},{5,13},{9,17},{1... | collective-permute-start | bytes 1572872 | tf_op jit(solution)/shard_map/ppermute | solution.py:340
  173.6 3.3 %collective-permute-done.31.refs_3_ = bf16[256,2048]{1,0:T(8,128)(2,1)S(1)} collective-permute-done((bf16[256,2048]{1,0:T(8,128)(2,1)S(1)}, bf16[256,2048]{1,0:T(8,128)(2,1)S(1)}, u32[]{:S(2)}, u32[]{:S(2)}) %collective-permute-start.31) | collective-permute-done | bytes 1048608 | tf_op jit(solution)/shard_map/ppermute | solution.py:348
  176.9 1.0 copy-done.10
  178.3 6.8 %repack.1 = (bf16[320,2048]{1,0:T(8,128)(2,1)}, bf16[320,2048]{1,0:T(8,128)(2,1)}, f32[2,16,320]{2,1,0:T(8,128)}) custom-call(s32[1]{0:T(128)} %bitcast.18.plane_ref, s32[1,1024]{1,0:T(1,128)} %bitcast.62, s32[2,320]{1,0:T(2,128)} %pad_add_fusion.1.local_ref, bf16[512,2048]{1,0:T(8,128)(2,1)} %bitcast.14.refs_2_.own_d_ref, ...), custom_call_target="tpu_custom_call" | custom-call | flops 31457280 | bytes 106496 | tf_op jit(solution)/shard_map/repack/pallas_call | solution.py:107
  185.1 1.6 collective-permute-start.36
  187.3 1.4 collective-permute-start.34
  188.8 1.6 collective-permute-done.36
  190.4 1.3 collective-permute-start.24
  191.7 4.6 %collective-permute-start.21 = (bf16[128,2048]{1,0:T(8,128)(2,1)S(1)}, bf16[128,2048]{1,0:T(8,128)(2,1)S(1)}, u32[]{:S(2)}, u32[]{:S(2)}) collective-permute-start(bf16[128,2048]{1,0:T(8,128)(2,1)S(1)} %add_convert_fusion.4), channel_id=1, source_target_pairs={{0,8},{4,12},{8,16},{12,20},{16,24},{20,28},{1,9},{5,13},{9,17},{1... | collective-permute-start | bytes 1572872 | tf_op jit(solution)/shard_map/ppermute | solution.py:340
  196.4 0.8 multiply_convert_fusion
  197.9 1.5 collective-permute-done.37
  199.4 1.3 collective-permute-start.27
  201.4 1.1 copy-done.7
  202.5 10.2 %adapter_gradients.1 = (f32[2048,512]{1,0:T(8,128)}, f32[512,2048]{1,0:T(8,128)}) custom-call(s32[8]{0:T(128)} %pad_add_fusion.4.order_ref, s32[1,640]{1,0:T(1,128)} %pad_add_fusion.2.local_ref, bf16[16,640]{1,0:T(8,128)(2,1)} %copy-done.19, bf16[16,640]{1,0:T(8,128)(2,1)} %pad_maximum_fusion.7.up_ranks_ref, bf16[320,2048]{1,0:T(8,128)(2,1)} %get-tuple-element.60.own_ref, ...), custom_call_target="tpu_custom_call" | custom-call | flops 41943040 | bytes 212992 | tf_op jit(solution)/shard_map/adapter_gradients/pallas_call | solution.py:294
  212.8 8.7 %collective-permute-done.27 = bf16[128,2048]{1,0:T(8,128)(2,1)S(1)} collective-permute-done((bf16[128,2048]{1,0:T(8,128)(2,1)S(1)}, bf16[128,2048]{1,0:T(8,128)(2,1)S(1)}, u32[]{:S(2)}, u32[]{:S(2)}) %collective-permute-start.27) | collective-permute-done | bytes 524320 | tf_op jit(solution)/shard_map/ppermute | solution.py:344
  221.9 1.1 pad_maximum_fusion.2
  (128 shorter events, 17.3 us)
Async XLA Ops:
  0.6 6.8 %copy-start.3 = (bf16[64,8192]{1,0:T(8,128)(2,1)S(1)}, bf16[64,8192]{1,0:T(8,128)(2,1)}, u32[]{:S(2)}) copy-start(bf16[64,8192]{1,0:T(8,128)(2,1)} %param.7) | copy-start | bytes 3145732
  2.9 8.8 %copy-start.21 = (s32[256]{0:T(256)S(1)}, s32[256]{0:T(256)}, u32[]{:S(2)}) copy-start(s32[256]{0:T(256)} %param.8) | copy-start | bytes 3076
  2.9 13.6 %copy-start.4 = (bf16[2048,512]{1,0:T(8,128)(2,1)S(1)}, bf16[2048,512]{1,0:T(8,128)(2,1)}, u32[]{:S(2)}) copy-start(bf16[2048,512]{1,0:T(8,128)(2,1)} %param.10) | copy-start | bytes 6291460
  2.9 10.4 %collective-permute-start = (bf16[64,2048]{1,0:T(8,128)(2,1)}, bf16[64,2048]{1,0:T(8,128)(2,1)}, u32[]{:S(2)}, u32[]{:S(2)}) collective-permute-start(bf16[64,2048]{1,0:T(8,128)(2,1)} %get-tuple-element.84), channel_id=1, source_target_pairs={{0,1},{1,0},{2,3},{3,2},{4,5},{5,4},{6,7},{7,6},{8,9},{9,8},{10,11... | collective-permute-start | bytes 786440 | tf_op jit(solution)/shard_map/ppermute | solution.py:354
  5.9 13.7 %collective-permute-start.1 = (bf16[64,2048]{1,0:T(8,128)(2,1)}, bf16[64,2048]{1,0:T(8,128)(2,1)}, u32[]{:S(2)}, u32[]{:S(2)}) collective-permute-start(bf16[64,2048]{1,0:T(8,128)(2,1)} %get-tuple-element.83), channel_id=1, source_target_pairs={{0,2},{1,3},{2,0},{3,1},{4,6},{5,7},{6,4},{7,5},{8,10},{9,11},{10,... | collective-permute-start | bytes 786440 | tf_op jit(solution)/shard_map/ppermute | solution.py:354
  7.4 12.2 %collective-permute-start.2 = (bf16[64,2048]{1,0:T(8,128)(2,1)}, bf16[64,2048]{1,0:T(8,128)(2,1)}, u32[]{:S(2)}, u32[]{:S(2)}) collective-permute-start(bf16[64,2048]{1,0:T(8,128)(2,1)} %get-tuple-element.82), channel_id=1, source_target_pairs={{0,3},{1,2},{2,1},{3,0},{4,7},{5,6},{6,5},{7,4},{8,11},{9,10},{10,... | collective-permute-start | bytes 786440 | tf_op jit(solution)/shard_map/ppermute | solution.py:354
  7.5 21.9 %collective-permute-start.4 = (bf16[64,2048]{1,0:T(8,128)(2,1)S(1)}, bf16[64,2048]{1,0:T(8,128)(2,1)S(1)}, u32[]{:S(2)}, u32[]{:S(2)}) collective-permute-start(bf16[64,2048]{1,0:T(8,128)(2,1)S(1)} %pad_maximum_fusion.4), channel_id=1, source_target_pairs={{0,8},{4,12},{8,16},{12,20},{16,24},{20,28},{24,0},{28,4},{1,9},{5... | collective-permute-start | bytes 786440 | tf_op jit(solution)/shard_map/ppermute | solution.py:336
  9.7 19.8 %collective-permute-start.3 = (bf16[64,2048]{1,0:T(8,128)(2,1)S(1)}, bf16[64,2048]{1,0:T(8,128)(2,1)}, u32[]{:S(2)}, u32[]{:S(2)}) collective-permute-start(bf16[64,2048]{1,0:T(8,128)(2,1)S(1)} %pad_maximum_fusion.6), channel_id=1, source_target_pairs={{0,24},{4,28},{8,0},{12,4},{16,8},{20,12},{24,16},{28,20},{1,25},{... | collective-permute-start | bytes 786440 | tf_op jit(solution)/shard_map/ppermute | solution.py:336
  13.3 20.9 %collective-permute-start.6 = (bf16[64,2048]{1,0:T(8,128)(2,1)S(1)}, bf16[64,2048]{1,0:T(8,128)(2,1)}, u32[]{:S(2)}, u32[]{:S(2)}) collective-permute-start(bf16[64,2048]{1,0:T(8,128)(2,1)S(1)} %pad_maximum_fusion.5), channel_id=1, source_target_pairs={{0,16},{4,20},{8,24},{12,28},{16,0},{20,4},{24,8},{28,12},{1,17},{... | collective-permute-start | bytes 786440 | tf_op jit(solution)/shard_map/ppermute | solution.py:336
  19.6 44.0 %collective-permute-start.8 = (bf16[512,2048]{1,0:T(8,128)(2,1)}, bf16[512,2048]{1,0:T(8,128)(2,1)}, u32[]{:S(2)}, u32[]{:S(2)}) collective-permute-start(bf16[512,2048]{1,0:T(8,128)(2,1)} %bitcast.14.refs_2_.own_d_ref), channel_id=1, source_target_pairs={{0,4},{4,0},{8,12},{12,8},{16,20},{20,16},{24,28},{28,24},{1,5},{5... | collective-permute-start | bytes 6291464 | tf_op jit(solution)/shard_map/ppermute | solution.py:351
  19.6 64.2 %collective-permute-start.9 = (bf16[2048,1024]{1,0:T(8,128)(2,1)}, bf16[2048,1024]{1,0:T(8,128)(2,1)}, u32[]{:S(2)}, u32[]{:S(2)}) collective-permute-start(bf16[2048,1024]{1,0:T(8,128)(2,1)} %own_w_ref), channel_id=1, source_target_pairs={{0,4},{4,0},{8,12},{12,8},{16,20},{20,16},{24,28},{28,24},{1,5},{5... | collective-permute-start | bytes 12582920 | tf_op jit(solution)/shard_map/ppermute | solution.py:351
  20.7 13.5 %all-to-all-start = ((s32[8,1,256]{2,1,0:T(1,128)}), s32[8,1,256]{2,1,0:T(1,128)S(1)}, u32[]{:S(2)}, u32[]{:S(2)}) async-start(s32[8,1,256]{2,1,0:T(1,128)} %broadcast_in_dim.59), calls=%async_computation | async-start | bytes 16384 | tf_op jit(solution)/shard_map/all_to_all | solution.py:381
  34.2 64.5 %all-to-all-start.1 = ((bf16[8,80,2048]{2,1,0:T(8,128)(2,1)}), bf16[8,80,2048]{2,1,0:T(8,128)(2,1)S(1)}, u32[]{:S(2)}, u32[]{:S(2)}) async-start(bf16[8,80,2048]{2,1,0:T(8,128)(2,1)} %bitcast.57), calls=%async_computation.1 | async-start | bytes 5242880 | tf_op jit(solution)/shard_map/all_to_all | solution.py:400
  38.9 20.4 %copy-start.1 = (bf16[1,2,64,2048]{3,2,1,0:T(8,128)(2,1)}, bf16[1,2,64,2048]{3,2,1,0:T(8,128)(2,1)S(1)}, u32[]{:S(2)}) copy-start(bf16[1,2,64,2048]{3,2,1,0:T(8,128)(2,1)S(1)} %maximum_bitcast_fusion.refs_0_) | copy-start | bytes 1572868
  38.9 14.3 %collective-permute-start.5 = (bf16[1,2,64,2048]{3,2,1,0:T(8,128)(2,1)S(1)}, bf16[1,2,64,2048]{3,2,1,0:T(8,128)(2,1)S(1)}, u32[]{:S(2)}, u32[]{:S(2)}) collective-permute-start(bf16[1,2,64,2048]{3,2,1,0:T(8,128)(2,1)S(1)} %maximum_bitcast_fusion.refs_0_), channel_id=1, source_target_pairs={{0,1},{1,0},{2,3},{3,2},{4,5},{5,4},{6,7},{7,6},{8,9},{9,8},{10,11... | collective-permute-start | bytes 1572872 | tf_op jit(solution)/shard_map/ppermute | solution.py:354
  41.5 17.8 %copy-start.2 = (bf16[1,2,64,2048]{3,2,1,0:T(8,128)(2,1)}, bf16[1,2,64,2048]{3,2,1,0:T(8,128)(2,1)S(1)}, u32[]{:S(2)}) copy-start(bf16[1,2,64,2048]{3,2,1,0:T(8,128)(2,1)S(1)} %maximum_bitcast_fusion.1.refs_3_) | copy-start | bytes 1572868
  41.5 14.0 %collective-permute-start.7 = (bf16[1,2,64,2048]{3,2,1,0:T(8,128)(2,1)S(1)}, bf16[1,2,64,2048]{3,2,1,0:T(8,128)(2,1)S(1)}, u32[]{:S(2)}, u32[]{:S(2)}) collective-permute-start(bf16[1,2,64,2048]{3,2,1,0:T(8,128)(2,1)S(1)} %maximum_bitcast_fusion.1.refs_3_), channel_id=1, source_target_pairs={{0,2},{1,3},{2,0},{3,1},{4,6},{5,7},{6,4},{7,5},{8,10},{9,11},{10,... | collective-permute-start | bytes 1572872 | tf_op jit(solution)/shard_map/ppermute | solution.py:354
  53.2 6.1 %copy-start.5 = (bf16[1,2,64,2048]{3,2,1,0:T(8,128)(2,1)}, bf16[1,2,64,2048]{3,2,1,0:T(8,128)(2,1)S(1)}, u32[]{:S(2)}) copy-start(bf16[1,2,64,2048]{3,2,1,0:T(8,128)(2,1)S(1)} %collective-permute-done.5.refs_1_) | copy-start | bytes 1572868
  55.5 3.8 %copy-start.6 = (bf16[1,2,64,2048]{3,2,1,0:T(8,128)(2,1)}, bf16[1,2,64,2048]{3,2,1,0:T(8,128)(2,1)S(1)}, u32[]{:S(2)}) copy-start(bf16[1,2,64,2048]{3,2,1,0:T(8,128)(2,1)S(1)} %collective-permute-done.7.refs_4_) | copy-start | bytes 1572868
  56.7 24.7 %collective-permute-start.10 = (bf16[2,2,64,2048]{3,2,1,0:T(8,128)(2,1)}, bf16[2,2,64,2048]{3,2,1,0:T(8,128)(2,1)}, u32[]{:S(2)}, u32[]{:S(2)}) collective-permute-start(bf16[2,2,64,2048]{3,2,1,0:T(8,128)(2,1)} %pad_maximum_fusion), channel_id=1, source_target_pairs={{0,2},{1,3},{2,0},{3,1},{4,6},{5,7},{6,4},{7,5},{8,10},{9,11},{10,... | collective-permute-start | bytes 3145736 | tf_op jit(solution)/shard_map/ppermute | solution.py:354
  59.3 24.5 %collective-permute-start.11 = (bf16[2,2,64,2048]{3,2,1,0:T(8,128)(2,1)}, bf16[2,2,64,2048]{3,2,1,0:T(8,128)(2,1)}, u32[]{:S(2)}, u32[]{:S(2)}) collective-permute-start(bf16[2,2,64,2048]{3,2,1,0:T(8,128)(2,1)} %pad_maximum_fusion.1), channel_id=1, source_target_pairs={{0,1},{1,0},{2,3},{3,2},{4,5},{5,4},{6,7},{7,6},{8,9},{9,8},{10,11... | collective-permute-start | bytes 3145736 | tf_op jit(solution)/shard_map/ppermute | solution.py:354
  62.3 60.9 %collective-permute-start.28 = (bf16[256,2048]{1,0:T(8,128)(2,1)}, bf16[256,2048]{1,0:T(8,128)(2,1)}, u32[]{:S(2)}, u32[]{:S(2)}) collective-permute-start(bf16[256,2048]{1,0:T(8,128)(2,1)} %refs_0_.1), channel_id=1, source_target_pairs={{8,0},{12,4},{16,8},{20,12},{24,16},{28,20},{9,1},{13,5},{17,9},{2... | collective-permute-start | bytes 3145736 | tf_op jit(solution)/shard_map/ppermute | solution.py:348
  63.6 59.6 %collective-permute-start.29 = (bf16[256,2048]{1,0:T(8,128)(2,1)}, bf16[256,2048]{1,0:T(8,128)(2,1)}, u32[]{:S(2)}, u32[]{:S(2)}) collective-permute-start(bf16[256,2048]{1,0:T(8,128)(2,1)} %refs_0_.1), channel_id=1, source_target_pairs={{0,8},{4,12},{8,16},{12,20},{16,24},{20,28},{1,9},{5,13},{9,17},{1... | collective-permute-start | bytes 3145736 | tf_op jit(solution)/shard_map/ppermute | solution.py:348
  98.7 1.5 copy-start
  106.6 5.1 %collective-permute-start.14 = (f32[16,640]{1,0:T(8,128)}, f32[16,640]{1,0:T(8,128)S(1)}, u32[]{:S(2)}, u32[]{:S(2)}) collective-permute-start(f32[16,640]{1,0:T(8,128)} %token_ranks.1), channel_id=1, source_target_pairs={{0,3},{1,2},{2,1},{3,0},{4,7},{5,6},{6,5},{7,4},{8,11},{9,10},{10,... | collective-permute-start | bytes 122888 | tf_op jit(solution)/shard_map/ppermute | solution.py:354
  108.9 4.2 %collective-permute-start.13 = (f32[16,640]{1,0:T(8,128)}, f32[16,640]{1,0:T(8,128)S(1)}, u32[]{:S(2)}, u32[]{:S(2)}) collective-permute-start(f32[16,640]{1,0:T(8,128)} %token_ranks.1), channel_id=1, source_target_pairs={{0,2},{1,3},{2,0},{3,1},{4,6},{5,7},{6,4},{7,5},{8,10},{9,11},{10,... | collective-permute-start | bytes 122888 | tf_op jit(solution)/shard_map/ppermute | solution.py:354
  109.4 4.2 %collective-permute-start.12 = (f32[16,640]{1,0:T(8,128)}, f32[16,640]{1,0:T(8,128)S(1)}, u32[]{:S(2)}, u32[]{:S(2)}) collective-permute-start(f32[16,640]{1,0:T(8,128)} %token_ranks.1), channel_id=1, source_target_pairs={{0,1},{1,0},{2,3},{3,2},{4,5},{5,4},{6,7},{7,6},{8,9},{9,8},{10,11... | collective-permute-start | bytes 122888 | tf_op jit(solution)/shard_map/ppermute | solution.py:354
  114.4 1.3 copy-start.19
  114.4 1.3 collective-permute-start.15
  115.7 0.6 copy-start.20
  123.2 17.3 %copy-start.14 = (bf16[128,2048]{1,0:T(8,128)(2,1)S(1)}, bf16[128,2048]{1,0:T(8,128)(2,1)}, u32[]{:S(2)}) copy-start(bf16[128,2048]{1,0:T(8,128)(2,1)} %get-tuple-element.53) | copy-start | bytes 1572868
  123.2 28.3 %collective-permute-start.30 = (bf16[256,2048]{1,0:T(8,128)(2,1)}, bf16[256,2048]{1,0:T(8,128)(2,1)S(1)}, u32[]{:S(2)}, u32[]{:S(2)}) collective-permute-start(bf16[256,2048]{1,0:T(8,128)(2,1)} %collective-permute-done.28.refs_1_), channel_id=1, source_target_pairs={{8,0},{12,4},{16,8},{20,12},{9,1},{13,5},{17,9},{21,13},{10,2},{14... | collective-permute-start | bytes 3145736 | tf_op jit(solution)/shard_map/ppermute | solution.py:348
  124.6 28.2 %collective-permute-start.32 = (bf16[256,2048]{1,0:T(8,128)(2,1)}, bf16[256,2048]{1,0:T(8,128)(2,1)S(1)}, u32[]{:S(2)}, u32[]{:S(2)}) collective-permute-start(bf16[256,2048]{1,0:T(8,128)(2,1)} %collective-permute-done.29.refs_4_), channel_id=1, source_target_pairs={{8,16},{12,20},{16,24},{20,28},{9,17},{13,21},{17,25},{21,29},{10,... | collective-permute-start | bytes 3145736 | tf_op jit(solution)/shard_map/ppermute | solution.py:348
  125.4 15.1 %collective-permute-start.22 = (bf16[128,2048]{1,0:T(8,128)(2,1)}, bf16[128,2048]{1,0:T(8,128)(2,1)S(1)}, u32[]{:S(2)}, u32[]{:S(2)}) collective-permute-start(bf16[128,2048]{1,0:T(8,128)(2,1)} %get-tuple-element.48), channel_id=1, source_target_pairs={{24,16},{28,20},{25,17},{29,21},{26,18},{30,22},{27,19},{31,23}} | collective-permute-start | bytes 1572872 | tf_op jit(solution)/shard_map/ppermute | solution.py:344
  126.1 19.0 %collective-permute-start.16 = (bf16[128,2048]{1,0:T(8,128)(2,1)}, bf16[128,2048]{1,0:T(8,128)(2,1)S(1)}, u32[]{:S(2)}, u32[]{:S(2)}) collective-permute-start(bf16[128,2048]{1,0:T(8,128)(2,1)} %get-tuple-element.50), channel_id=1, source_target_pairs={{0,8},{4,12},{1,9},{5,13},{2,10},{6,14},{3,11},{7,15}} | collective-permute-start | bytes 1572872 | tf_op jit(solution)/shard_map/ppermute | solution.py:340
  132.4 18.4 %collective-permute-start.25 = (bf16[128,2048]{1,0:T(8,128)(2,1)}, bf16[128,2048]{1,0:T(8,128)(2,1)S(1)}, u32[]{:S(2)}, u32[]{:S(2)}) collective-permute-start(bf16[128,2048]{1,0:T(8,128)(2,1)} %get-tuple-element.51), channel_id=1, source_target_pairs={{24,16},{28,20},{25,17},{29,21},{26,18},{30,22},{27,19},{31,23}} | collective-permute-start | bytes 1572872 | tf_op jit(solution)/shard_map/ppermute | solution.py:344
  140.4 15.8 %copy-start.18 = (bf16[128,2048]{1,0:T(8,128)(2,1)S(1)}, bf16[128,2048]{1,0:T(8,128)(2,1)}, u32[]{:S(2)}) copy-start(bf16[128,2048]{1,0:T(8,128)(2,1)} %get-tuple-element.52) | copy-start | bytes 1572868
  140.5 15.7 %collective-permute-start.19 = (bf16[128,2048]{1,0:T(8,128)(2,1)S(1)}, bf16[128,2048]{1,0:T(8,128)(2,1)S(1)}, u32[]{:S(2)}, u32[]{:S(2)}) collective-permute-start(bf16[128,2048]{1,0:T(8,128)(2,1)S(1)} %copy-done.14), channel_id=1, source_target_pairs={{0,8},{4,12},{1,9},{5,13},{2,10},{6,14},{3,11},{7,15}} | collective-permute-start | bytes 1572872 | tf_op jit(solution)/shard_map/ppermute | solution.py:340
  145.1 23.2 %copy-start.17 = (bf16[128,2048]{1,0:T(8,128)(2,1)S(1)}, bf16[128,2048]{1,0:T(8,128)(2,1)}, u32[]{:S(2)}) copy-start(bf16[128,2048]{1,0:T(8,128)(2,1)} %get-tuple-element.48) | copy-start | bytes 1572868
  146.5 21.0 %collective-permute-start.17 = (bf16[128,2048]{1,0:T(8,128)(2,1)S(1)}, bf16[128,2048]{1,0:T(8,128)(2,1)S(1)}, u32[]{:S(2)}, u32[]{:S(2)}) collective-permute-start(bf16[128,2048]{1,0:T(8,128)(2,1)S(1)} %get-tuple-element.89), channel_id=1, source_target_pairs={{0,8},{4,12},{8,16},{12,20},{1,9},{5,13},{9,17},{13,21},{2,10},{6,... | collective-permute-start | bytes 1572872 | tf_op jit(solution)/shard_map/ppermute | solution.py:340
  150.8 17.7 %collective-permute-start.23 = (bf16[128,2048]{1,0:T(8,128)(2,1)S(1)}, bf16[128,2048]{1,0:T(8,128)(2,1)S(1)}, u32[]{:S(2)}, u32[]{:S(2)}) collective-permute-start(bf16[128,2048]{1,0:T(8,128)(2,1)S(1)} %get-tuple-element.88), channel_id=1, source_target_pairs={{16,8},{20,12},{24,16},{28,20},{17,9},{21,13},{25,17},{29,21},{18,... | collective-permute-start | bytes 1572872 | tf_op jit(solution)/shard_map/ppermute | solution.py:344
  151.5 16.9 %copy-start.8 = (bf16[256,2048]{1,0:T(8,128)(2,1)}, bf16[256,2048]{1,0:T(8,128)(2,1)S(1)}, u32[]{:S(2)}) copy-start(bf16[256,2048]{1,0:T(8,128)(2,1)S(1)} %collective-permute-done.30.refs_2_) | copy-start | bytes 3145732
  151.5 25.4 %collective-permute-start.31 = (bf16[256,2048]{1,0:T(8,128)(2,1)S(1)}, bf16[256,2048]{1,0:T(8,128)(2,1)S(1)}, u32[]{:S(2)}, u32[]{:S(2)}) collective-permute-start(bf16[256,2048]{1,0:T(8,128)(2,1)S(1)} %collective-permute-done.30.refs_2_), channel_id=1, source_target_pairs={{8,0},{12,4},{9,1},{13,5},{10,2},{14,6},{11,3},{15,7}} | collective-permute-start | bytes 3145736 | tf_op jit(solution)/shard_map/ppermute | solution.py:348
  152.8 15.6 %copy-start.9 = (bf16[256,2048]{1,0:T(8,128)(2,1)}, bf16[256,2048]{1,0:T(8,128)(2,1)S(1)}, u32[]{:S(2)}) copy-start(bf16[256,2048]{1,0:T(8,128)(2,1)S(1)} %collective-permute-done.32.refs_5_) | copy-start | bytes 3145732
  152.8 24.1 %collective-permute-start.33 = (bf16[256,2048]{1,0:T(8,128)(2,1)S(1)}, bf16[256,2048]{1,0:T(8,128)(2,1)S(1)}, u32[]{:S(2)}, u32[]{:S(2)}) collective-permute-start(bf16[256,2048]{1,0:T(8,128)(2,1)S(1)} %collective-permute-done.32.refs_5_), channel_id=1, source_target_pairs={{16,24},{20,28},{17,25},{21,29},{18,26},{22,30},{19,27},{23,31}} | collective-permute-start | bytes 3145736 | tf_op jit(solution)/shard_map/ppermute | solution.py:348
  156.2 17.3 %copy-start.16 = (bf16[128,2048]{1,0:T(8,128)(2,1)S(1)}, bf16[128,2048]{1,0:T(8,128)(2,1)}, u32[]{:S(2)}) copy-start(bf16[128,2048]{1,0:T(8,128)(2,1)} %get-tuple-element.50) | copy-start | bytes 1572868
  157.3 30.0 %collective-permute-start.20 = (bf16[128,2048]{1,0:T(8,128)(2,1)}, bf16[128,2048]{1,0:T(8,128)(2,1)S(1)}, u32[]{:S(2)}, u32[]{:S(2)}) collective-permute-start(bf16[128,2048]{1,0:T(8,128)(2,1)} %get-tuple-element.87), channel_id=1, source_target_pairs={{0,8},{4,12},{8,16},{12,20},{1,9},{5,13},{9,17},{13,21},{2,10},{6,... | collective-permute-start | bytes 1572872 | tf_op jit(solution)/shard_map/ppermute | solution.py:340
  167.4 29.8 %collective-permute-start.26 = (bf16[128,2048]{1,0:T(8,128)(2,1)S(1)}, bf16[128,2048]{1,0:T(8,128)(2,1)S(1)}, u32[]{:S(2)}, u32[]{:S(2)}) collective-permute-start(bf16[128,2048]{1,0:T(8,128)(2,1)S(1)} %get-tuple-element.86), channel_id=1, source_target_pairs={{16,8},{20,12},{24,16},{28,20},{17,9},{21,13},{25,17},{29,21},{18,... | collective-permute-start | bytes 1572872 | tf_op jit(solution)/shard_map/ppermute | solution.py:344
  168.5 44.3 %collective-permute-start.18 = (bf16[128,2048]{1,0:T(8,128)(2,1)S(1)}, bf16[128,2048]{1,0:T(8,128)(2,1)S(1)}, u32[]{:S(2)}, u32[]{:S(2)}) collective-permute-start(bf16[128,2048]{1,0:T(8,128)(2,1)S(1)} %add_convert_fusion.5), channel_id=1, source_target_pairs={{0,8},{4,12},{8,16},{12,20},{16,24},{20,28},{1,9},{5,13},{9,17},{1... | collective-permute-start | bytes 1572872 | tf_op jit(solution)/shard_map/ppermute | solution.py:340
  176.9 1.0 copy-start.10
  176.9 1.4 copy-start.11
  178.3 10.4 %copy-start.15 = (bf16[128,2048]{1,0:T(8,128)(2,1)S(1)}, bf16[128,2048]{1,0:T(8,128)(2,1)}, u32[]{:S(2)}) copy-start(bf16[128,2048]{1,0:T(8,128)(2,1)} %get-tuple-element.51) | copy-start | bytes 1572868
  185.1 5.3 %collective-permute-start.36 = (f32[2,16,320]{2,1,0:T(8,128)}, f32[2,16,320]{2,1,0:T(8,128)S(1)}, u32[]{:S(2)}, u32[]{:S(2)}) collective-permute-start(f32[2,16,320]{2,1,0:T(8,128)} %get-tuple-element.59), channel_id=1, source_target_pairs={{0,3},{1,2},{2,1},{3,0},{4,7},{5,6},{6,5},{7,4},{8,11},{9,10},{10,... | collective-permute-start | bytes 122888 | tf_op jit(solution)/shard_map/ppermute | solution.py:354
  186.7 5.0 %collective-permute-start.35 = (f32[2,16,320]{2,1,0:T(8,128)}, f32[2,16,320]{2,1,0:T(8,128)S(1)}, u32[]{:S(2)}, u32[]{:S(2)}) collective-permute-start(f32[2,16,320]{2,1,0:T(8,128)} %get-tuple-element.59), channel_id=1, source_target_pairs={{0,2},{1,3},{2,0},{3,1},{4,6},{5,7},{6,4},{7,5},{8,10},{9,11},{10,... | collective-permute-start | bytes 122888 | tf_op jit(solution)/shard_map/ppermute | solution.py:354
  187.3 9.0 %collective-permute-start.34 = (f32[2,16,320]{2,1,0:T(8,128)}, f32[2,16,320]{2,1,0:T(8,128)S(1)}, u32[]{:S(2)}, u32[]{:S(2)}) collective-permute-start(f32[2,16,320]{2,1,0:T(8,128)} %get-tuple-element.59), channel_id=1, source_target_pairs={{0,1},{1,0},{2,3},{3,2},{4,5},{5,4},{6,7},{7,6},{8,9},{9,8},{10,11... | collective-permute-start | bytes 122888 | tf_op jit(solution)/shard_map/ppermute | solution.py:354
  190.4 22.4 %collective-permute-start.24 = (bf16[128,2048]{1,0:T(8,128)(2,1)S(1)}, bf16[128,2048]{1,0:T(8,128)(2,1)S(1)}, u32[]{:S(2)}, u32[]{:S(2)}) collective-permute-start(bf16[128,2048]{1,0:T(8,128)(2,1)S(1)} %add_convert_fusion.3), channel_id=1, source_target_pairs={{8,0},{12,4},{16,8},{20,12},{24,16},{28,20},{9,1},{13,5},{17,9},{2... | collective-permute-start | bytes 1572872 | tf_op jit(solution)/shard_map/ppermute | solution.py:344
  191.7 21.1 %collective-permute-start.21 = (bf16[128,2048]{1,0:T(8,128)(2,1)S(1)}, bf16[128,2048]{1,0:T(8,128)(2,1)S(1)}, u32[]{:S(2)}, u32[]{:S(2)}) collective-permute-start(bf16[128,2048]{1,0:T(8,128)(2,1)S(1)} %add_convert_fusion.4), channel_id=1, source_target_pairs={{0,8},{4,12},{8,16},{12,20},{16,24},{20,28},{1,9},{5,13},{9,17},{1... | collective-permute-start | bytes 1572872 | tf_op jit(solution)/shard_map/ppermute | solution.py:340
  196.3 5.1 %collective-permute-start.38 = (bf16[320,2048]{1,0:T(8,128)(2,1)}, bf16[320,2048]{1,0:T(8,128)(2,1)S(1)}, u32[]{:S(2)}, u32[]{:S(2)}) collective-permute-start(bf16[320,2048]{1,0:T(8,128)(2,1)} %get-tuple-element.61), channel_id=1, source_target_pairs={{0,4},{4,0},{8,12},{12,8},{16,20},{20,16},{24,28},{28,24},{1,5},{5... | collective-permute-start | bytes 3932168 | tf_op jit(solution)/shard_map/ppermute | solution.py:351
  197.2 2.2 collective-permute-start.37
  199.4 22.1 %collective-permute-start.27 = (bf16[128,2048]{1,0:T(8,128)(2,1)S(1)}, bf16[128,2048]{1,0:T(8,128)(2,1)S(1)}, u32[]{:S(2)}, u32[]{:S(2)}) collective-permute-start(bf16[128,2048]{1,0:T(8,128)(2,1)S(1)} %add_convert_fusion.2), channel_id=1, source_target_pairs={{8,0},{12,4},{16,8},{20,12},{24,16},{28,20},{9,1},{13,5},{17,9},{2... | collective-permute-start | bytes 1572872 | tf_op jit(solution)/shard_map/ppermute | solution.py:344
  201.4 1.1 copy-start.7
  202.5 19.0 %copy-start.13 = (f32[128,2048]{1,0:T(8,128)S(1)}, f32[128,2048]{1,0:T(8,128)}, u32[]{:S(2)}) copy-start(f32[128,2048]{1,0:T(8,128)} %get-tuple-element.65) | copy-start | bytes 3145732
  212.7 8.9 %copy-start.12 = (f32[128,2048]{1,0:T(8,128)S(1)}, f32[128,2048]{1,0:T(8,128)}, u32[]{:S(2)}) copy-start(f32[128,2048]{1,0:T(8,128)} %get-tuple-element.47) | copy-start | bytes 3145732

commit v5 on v4

--- a/solution.py
+++ b/solution.py
@@ -149,7 +149,7 @@
     blocks, width = order.shape[0], weight.shape[1]
     total = local.shape[1]
     rank_cols = weight.shape[0]
-    tile = min(512, width)
+    tile = min(1024, width)
     return pl.pallas_call(
         functools.partial(ranks_kernel, per_owner, blocks),
         out_shape=jax.ShapeDtypeStruct((ADAPTER_RANK, total), F32),
@@ -247,7 +247,7 @@
 def add_term(frozen, first, rows, places, ranks, downs, per_owner, types):
     width = frozen.shape[1]
     rank_cols = downs[0].shape[0]
-    tile = min(512, width)
+    tile = min(1024, width)
     column = lambda n: (0, n)
     each = rows // len(types)
     return pl.pallas_call(
@@ -288,7 +288,7 @@
     total, width = grad.shape
     blocks = order.shape[0]
     rank_cols = per_owner * ADAPTER_RANK
-    tile = min(256, width)
+    tile = min(512, width)
     whole = lambda n, order: (0, 0)
     column = lambda n, order: (0, n)
     return pl.pallas_call(
@@ -399,7 +399,7 @@
         x = x.reshape(owners, capacity, width)
         return lax.all_to_all(x, "adapter", 0, 0, tiled=True).reshape(slot_count, width)
 
-    grad_packed = after(grad_packed, *(part[d] for d in range(1, planes)))
+    grad_packed = after(grad_packed, part[1], part[planes - 1])
     grad_slots = to_owners(grad_packed)
 
     halves = [jnp.stack([part[d] for d in order[i * half : (i + 1) * half]], axis=0) for i in range(2)]

time: 224 us -> 222 us (level)
  waiting for transfers between devices: 62.1 us -> 66.7 us
  Pallas kernels: 55.7 us -> 51.9 us
  starting transfers between devices: 76.5 us -> 73.8 us
    ppermute x3, waiting for transfers between devices: 4.79 us -> 0.01 us  [shift(): return lax.ppermute(x, 'adapter', pairs)]
    all_to_all x1, waiting for transfers between devices: 0.01 us -> 4.76 us  [per_device(): lax.all_to_all(jnp.broadcast_to(ids_again, (owners, tokens)), 'adapter',...]
    unnamed x48 -> x52, local copies, waits for them, and re-layouts: 8.16 us -> 8.16 us
  transfers between devices with their start and end apart: 41 -> 41, of which waited for: 18 -> 18; matrix products, arithmetic and copies ran while one was open for 9% -> 9% of each run, Pallas kernels for 25% -> 24%
where the time goes in v5:
time: 222 us; the launch traced here: 221 us
  starting transfers between devices  73.8 us (33%)
  waiting for transfers between devices  66.7 us (30%)
  Pallas kernels  51.9 us (23%)
  other arithmetic  15.1 us (7%)
  local copies, waits for them, and re-layouts  12 us (5%)
    ppermute x13, waiting for transfers between devices, flip(): return lax.ppermute(x, 'tensor', [(t, t ^ k) for t in range(tensors)])  32.4 us
    ppermute x6, starting transfers between devices, up_line(): return lax.ppermute(x, 'adapter', pairs)  25.5 us
    ppermute x13, starting transfers between devices, flip(): return lax.ppermute(x, 'tensor', [(t, t ^ k) for t in range(tensors)])  16.8 us
    pallas_call x1, Pallas kernels, frozen_part(): pl.pallas_call(functools.partial(frozen_kernel, names), grid=(width // ti...  14.9 us
    pallas_call x2, Pallas kernels, add_term(): pl.pallas_call(functools.partial(term_kernel, per_owner), grid=(width //...  13 us
    ppermute x6, waiting for transfers between devices, up_line(): return lax.ppermute(x, 'adapter', pairs)  12 us
    ppermute x6, starting transfers between devices, attn_line(): lax.ppermute(x, 'adapter', [(2 * z + c, 2 * (z + way) + c) for z in plane...  11 us
    ppermute x6, waiting for transfers between devices, down_line(): return lax.ppermute(x, 'adapter', pairs)  9.78 us
  transfers between devices with their start and end apart: 41, of which 18 were waited for; matrix products, arithmetic and copies ran while one was open for 9% of the time, Pallas kernels for 24%

profile of v5, /device:TPU:0, one launch (start us, length us, event | category | flops | bytes accessed | tf_op | source)
XLA Modules:
  0.0 220.9 jit_solution(12917214620768712209)
XLA Ops:
  0.7 2.3 %constant_dynamic-slice_fusion.8 = (bf16[64,2048]{1,0:T(8,128)(2,1)}, bf16[64,2048]{1,0:T(8,128)(2,1)}, bf16[64,2048]{1,0:T(8,128)(2,1)}, bf16[64,2048]{1,0:T(8,128)(2,1)}) fusion(bf16[64,8192]{1,0:T(8,128)(2,1)} %param.7, s32[]{:T(128)S(6)} %select_n.162, s32[]{:T(128)S(6)} %select_n.161, s32[]{:T(128)S(6)} %select_n.160, s32[]{:T(128)S(6)} %select_n.159), kind=kLoop, calls=%fused_computation.74 | loop fusion | bytes 2097168 | tf_op jit(solution)/shard_map/dynamic_slice | solution.py:360
  2.9 3.0 %collective-permute-start = (bf16[64,2048]{1,0:T(8,128)(2,1)}, bf16[64,2048]{1,0:T(8,128)(2,1)}, u32[]{:S(2)}, u32[]{:S(2)}) collective-permute-start(bf16[64,2048]{1,0:T(8,128)(2,1)} %get-tuple-element.84), channel_id=1, source_target_pairs={{0,1},{1,0},{2,3},{3,2},{4,5},{5,4},{6,7},{7,6},{8,9},{9,8},{10,11... | collective-permute-start | bytes 786440 | tf_op jit(solution)/shard_map/ppermute | solution.py:354
  5.9 1.5 collective-permute-start.1
  7.5 2.1 collective-permute-start.4
  9.6 2.1 collective-permute-start.3
  12.7 2.4 %copy.11 = bf16[2048,512]{0,1:T(8,128)(2,1)} copy(bf16[2048,512]{1,0:T(8,128)(2,1)S(1)} %copy-done.4) | data formatting | bytes 4194304 | tf_op args[4]
  15.2 1.3 collective-permute-start.6
  16.5 3.1 %collective-permute-done.1.refs_2_ = bf16[64,2048]{1,0:T(8,128)(2,1)} collective-permute-done((bf16[64,2048]{1,0:T(8,128)(2,1)}, bf16[64,2048]{1,0:T(8,128)(2,1)}, u32[]{:S(2)}, u32[]{:S(2)}) %collective-permute-start.1) | collective-permute-done | bytes 262176 | tf_op jit(solution)/shard_map/ppermute | solution.py:354
  20.7 4.9 %all-to-all-start = ((s32[8,1,256]{2,1,0:T(1,128)}), s32[8,1,256]{2,1,0:T(1,128)S(1)}, u32[]{:S(2)}, u32[]{:S(2)}) async-start(s32[8,1,256]{2,1,0:T(1,128)} %broadcast_in_dim.59), calls=%async_computation | async-start | bytes 16384 | tf_op jit(solution)/shard_map/all_to_all | solution.py:381
  26.2 3.2 %pack_rows.1 = bf16[640,2048]{1,0:T(8,128)(2,1)} custom-call(s32[1,256]{1,0:T(1,128)} %bitcast.65, bf16[64,2048]{1,0:T(8,128)(2,1)} %get-tuple-element.41.refs_0_, bf16[64,2048]{1,0:T(8,128)(2,1)} %collective-permute-done.refs_1_, bf16[64,2048]{1,0:T(8,128)(2,1)} %collective-permute-done.1.refs_2_, bf16[64,2048]{1,0:T(8,128)(2,1)} %collective-permute-done.2.refs_3_), custom_call_target="tpu_custom_call" | custom-call | flops 10485760 | bytes 57344 | tf_op jit(solution)/shard_map/pack_rows/pallas_call | solution.py:43
  29.4 4.8 %all-to-all-done = s32[8,1,256]{2,1,0:T(1,128)S(1)} async-done(((s32[8,1,256]{2,1,0:T(1,128)}), s32[8,1,256]{2,1,0:T(1,128)S(1)}, u32[]{:S(2)}, u32[]{:S(2)}) %all-to-all-start) | async-done | bytes 8224 | tf_op jit(solution)/shard_map/all_to_all | solution.py:381
  34.2 3.6 %all-to-all-start.1 = ((bf16[8,80,2048]{2,1,0:T(8,128)(2,1)}), bf16[8,80,2048]{2,1,0:T(8,128)(2,1)S(1)}, u32[]{:S(2)}, u32[]{:S(2)}) async-start(bf16[8,80,2048]{2,1,0:T(8,128)(2,1)} %bitcast.57), calls=%async_computation.1 | async-start | bytes 5242880 | tf_op jit(solution)/shard_map/all_to_all | solution.py:400
  37.9 1.1 maximum_bitcast_fusion.refs_0_
  39.0 1.6 collective-permute-start.5
  40.6 1.6 collective-permute-start.7
  43.0 10.3 %collective-permute-done.5.refs_1_ = bf16[1,2,64,2048]{3,2,1,0:T(8,128)(2,1)S(1)} collective-permute-done((bf16[1,2,64,2048]{3,2,1,0:T(8,128)(2,1)S(1)}, bf16[1,2,64,2048]{3,2,1,0:T(8,128)(2,1)S(1)}, u32[]{:S(2)}, u32[]{:S(2)}) %collective-permute-start.5) | collective-permute-done | bytes 524320 | tf_op jit(solution)/shard_map/ppermute | solution.py:354
  53.3 1.3 collective-permute-done.7.refs_4_
  54.6 1.1 pad_maximum_fusion
  55.8 1.5 collective-permute-start.10
  57.3 1.1 pad_maximum_fusion.1
  59.6 0.8 convert_reduce_fusion
  61.4 1.3 collective-permute-start.28
  62.7 5.5 %collective-permute-start.29 = (bf16[256,2048]{1,0:T(8,128)(2,1)}, bf16[256,2048]{1,0:T(8,128)(2,1)}, u32[]{:S(2)}, u32[]{:S(2)}) collective-permute-start(bf16[256,2048]{1,0:T(8,128)(2,1)} %refs_0_.1), channel_id=1, source_target_pairs={{0,8},{4,12},{8,16},{12,20},{16,24},{20,28},{1,9},{5,13},{9,17},{1... | collective-permute-start | bytes 3145736 | tf_op jit(solution)/shard_map/ppermute | solution.py:348
  70.5 10.0 %collective-permute-done.10.refs_2_ = bf16[2,2,64,2048]{3,2,1,0:T(8,128)(2,1)} collective-permute-done((bf16[2,2,64,2048]{3,2,1,0:T(8,128)(2,1)}, bf16[2,2,64,2048]{3,2,1,0:T(8,128)(2,1)}, u32[]{:S(2)}, u32[]{:S(2)}) %collective-permute-start.10) | collective-permute-done | bytes 1048608 | tf_op jit(solution)/shard_map/ppermute | solution.py:354
  80.5 2.4 %collective-permute-done.11.refs_5_ = bf16[2,2,64,2048]{3,2,1,0:T(8,128)(2,1)} collective-permute-done((bf16[2,2,64,2048]{3,2,1,0:T(8,128)(2,1)}, bf16[2,2,64,2048]{3,2,1,0:T(8,128)(2,1)}, u32[]{:S(2)}, u32[]{:S(2)}) %collective-permute-start.11) | collective-permute-done | bytes 1048608 | tf_op jit(solution)/shard_map/ppermute | solution.py:354
  82.9 14.9 %frozen_part.1.frozen_ref = f32[1024,2048]{1,0:T(8,128)} custom-call(s32[1]{0:T(128)} %bitcast.place_ref, bf16[2048,1024]{1,0:T(8,128)(2,1)} %own_w_ref, bf16[2048,1024]{1,0:T(8,128)(2,1)} %collective-permute-done.9.other_w_ref, bf16[1,2,64,2048]{3,2,1,0:T(8,128)(2,1)} %copy-done.1, bf16[1,2,64,2048]{3,2,1,0:T(8,128)(2,1)} %copy-done.5, ...), custom_call_target="tpu_custom_call" | custom-call | flops 134217728 | bytes 262144 | tf_op jit(solution)/shard_map/frozen_part/pallas_call | solution.py:208
  97.8 0.7 all-to-all-done.1
  98.6 1.5 copy-done
  100.0 5.6 %token_ranks.1 = f32[16,640]{1,0:T(8,128)} custom-call(s32[8]{0:T(128)} %pad_add_fusion.4.order_ref, s32[1,640]{1,0:T(1,128)} %pad_add_fusion.2.local_ref, bf16[512,2048]{1,0:T(8,128)(2,1)} %weight_ref.1, bf16[640,2048]{1,0:T(8,128)(2,1)} %bitcast.41, bf16[640,2048]{1,0:T(8,128)(2,1)} %bitcast.42, bf16[640,2048]{1,0:T(8,128)(2,1)} %bitcast.43, ...), custom_call_target="tpu_custom_call" | custom-call | flops 20971520 | bytes 73728 | tf_op jit(solution)/shard_map/token_ranks/pallas_call | solution.py:153
  105.6 2.4 %collective-permute-start.14 = (f32[16,640]{1,0:T(8,128)}, f32[16,640]{1,0:T(8,128)S(1)}, u32[]{:S(2)}, u32[]{:S(2)}) collective-permute-start(f32[16,640]{1,0:T(8,128)} %token_ranks.1), channel_id=1, source_target_pairs={{0,3},{1,2},{2,1},{3,0},{4,7},{5,6},{6,5},{7,4},{8,11},{9,10},{10,... | collective-permute-start | bytes 122888 | tf_op jit(solution)/shard_map/ppermute | solution.py:354
  109.1 1.6 collective-permute-done.14
  110.8 1.5 collective-permute-done.13
  112.8 0.8 multiply_convert_fusion.1.refs_0_.grad_ranks_ref
  113.7 1.2 collective-permute-done.15.refs_1_
  115.5 6.4 %add_term.3 = (bf16[128,2048]{1,0:T(8,128)(2,1)}, bf16[128,2048]{1,0:T(8,128)(2,1)}, bf16[128,2048]{1,0:T(8,128)(2,1)}, bf16[128,2048]{1,0:T(8,128)(2,1)}) custom-call(f32[1024,2048]{1,0:T(8,128)} %frozen_part.1.frozen_ref, s32[4,1024]{1,0:T(4,128)} %bitcast.62, bf16[16,640]{1,0:T(8,128)(2,1)} %copy-done.19, bf16[16,640]{1,0:T(8,128)(2,1)} %copy-done.22, ...), custom_call_target="tpu_custom_call" | custom-call | flops 33554432 | bytes 163840 | tf_op jit(solution)/shard_map/add_term/pallas_call | solution.py:253
  121.9 1.4 collective-permute-start.30
  123.4 0.7 collective-permute-start.32
  124.8 5.6 %collective-permute-start.16 = (bf16[128,2048]{1,0:T(8,128)(2,1)}, bf16[128,2048]{1,0:T(8,128)(2,1)S(1)}, u32[]{:S(2)}, u32[]{:S(2)}) collective-permute-start(bf16[128,2048]{1,0:T(8,128)(2,1)} %get-tuple-element.50), channel_id=1, source_target_pairs={{0,8},{4,12},{1,9},{5,13},{2,10},{6,14},{3,11},{7,15}} | collective-permute-start | bytes 1572872 | tf_op jit(solution)/shard_map/ppermute | solution.py:340
  131.1 6.6 %add_term.2 = (bf16[128,2048]{1,0:T(8,128)(2,1)}, bf16[128,2048]{1,0:T(8,128)(2,1)}, f32[128,2048]{1,0:T(8,128)}, f32[128,2048]{1,0:T(8,128)}) custom-call(f32[1024,2048]{1,0:T(8,128)} %frozen_part.1.frozen_ref, s32[4,1024]{1,0:T(4,128)} %bitcast.63, bf16[16,640]{1,0:T(8,128)(2,1)} %copy-done.19, bf16[16,640]{1,0:T(8,128)(2,1)} %copy-done.22, ...), custom_call_target="tpu_custom_call" | custom-call | flops 33554432 | bytes 163840 | tf_op jit(solution)/shard_map/add_term/pallas_call | solution.py:253
  137.7 1.5 collective-permute-start.19
  139.1 3.9 %collective-permute-done.16 = bf16[128,2048]{1,0:T(8,128)(2,1)S(1)} collective-permute-done((bf16[128,2048]{1,0:T(8,128)(2,1)}, bf16[128,2048]{1,0:T(8,128)(2,1)S(1)}, u32[]{:S(2)}, u32[]{:S(2)}) %collective-permute-start.16) | collective-permute-done | bytes 524320 | tf_op jit(solution)/shard_map/ppermute | solution.py:340
  143.0 1.4 fusion.1
  144.4 4.5 %collective-permute-start.17 = (bf16[128,2048]{1,0:T(8,128)(2,1)S(1)}, bf16[128,2048]{1,0:T(8,128)(2,1)S(1)}, u32[]{:S(2)}, u32[]{:S(2)}) collective-permute-start(bf16[128,2048]{1,0:T(8,128)(2,1)S(1)} %get-tuple-element.89), channel_id=1, source_target_pairs={{0,8},{4,12},{8,16},{12,20},{1,9},{5,13},{9,17},{13,21},{2,10},{6,... | collective-permute-start | bytes 1572872 | tf_op jit(solution)/shard_map/ppermute | solution.py:340
  149.7 1.3 collective-permute-start.31
  151.7 2.4 %collective-permute-done.19 = bf16[128,2048]{1,0:T(8,128)(2,1)S(1)} collective-permute-done((bf16[128,2048]{1,0:T(8,128)(2,1)S(1)}, bf16[128,2048]{1,0:T(8,128)(2,1)S(1)}, u32[]{:S(2)}, u32[]{:S(2)}) %collective-permute-start.19) | collective-permute-done | bytes 524320 | tf_op jit(solution)/shard_map/ppermute | solution.py:340
  154.1 1.1 fusion.3
  155.3 4.4 %collective-permute-start.20 = (bf16[128,2048]{1,0:T(8,128)(2,1)}, bf16[128,2048]{1,0:T(8,128)(2,1)S(1)}, u32[]{:S(2)}, u32[]{:S(2)}) collective-permute-start(bf16[128,2048]{1,0:T(8,128)(2,1)} %get-tuple-element.87), channel_id=1, source_target_pairs={{0,8},{4,12},{8,16},{12,20},{1,9},{5,13},{9,17},{13,21},{2,10},{6,... | collective-permute-start | bytes 1572872 | tf_op jit(solution)/shard_map/ppermute | solution.py:340
  159.7 5.7 %collective-permute-done.17 = bf16[128,2048]{1,0:T(8,128)(2,1)S(1)} collective-permute-done((bf16[128,2048]{1,0:T(8,128)(2,1)S(1)}, bf16[128,2048]{1,0:T(8,128)(2,1)S(1)}, u32[]{:S(2)}, u32[]{:S(2)}) %collective-permute-start.17) | collective-permute-done | bytes 524320 | tf_op jit(solution)/shard_map/ppermute | solution.py:340
  166.2 5.0 %collective-permute-start.18 = (bf16[128,2048]{1,0:T(8,128)(2,1)S(1)}, bf16[128,2048]{1,0:T(8,128)(2,1)S(1)}, u32[]{:S(2)}, u32[]{:S(2)}) collective-permute-start(bf16[128,2048]{1,0:T(8,128)(2,1)S(1)} %add_convert_fusion.5), channel_id=1, source_target_pairs={{0,8},{4,12},{8,16},{12,20},{16,24},{20,28},{1,9},{5,13},{9,17},{1... | collective-permute-start | bytes 1572872 | tf_op jit(solution)/shard_map/ppermute | solution.py:340
  171.4 4.3 %collective-permute-done.31.refs_3_ = bf16[256,2048]{1,0:T(8,128)(2,1)S(1)} collective-permute-done((bf16[256,2048]{1,0:T(8,128)(2,1)S(1)}, bf16[256,2048]{1,0:T(8,128)(2,1)S(1)}, u32[]{:S(2)}, u32[]{:S(2)}) %collective-permute-start.31) | collective-permute-done | bytes 1048608 | tf_op jit(solution)/shard_map/ppermute | solution.py:348
  175.7 1.0 copy-done.10
  177.0 6.8 %repack.1 = (bf16[320,2048]{1,0:T(8,128)(2,1)}, bf16[320,2048]{1,0:T(8,128)(2,1)}, f32[2,16,320]{2,1,0:T(8,128)}) custom-call(s32[1]{0:T(128)} %bitcast.18.plane_ref, s32[1,1024]{1,0:T(1,128)} %bitcast.64, s32[2,320]{1,0:T(2,128)} %pad_add_fusion.1.local_ref, bf16[512,2048]{1,0:T(8,128)(2,1)} %bitcast.14.refs_2_.own_d_ref, ...), custom_call_target="tpu_custom_call" | custom-call | flops 31457280 | bytes 106496 | tf_op jit(solution)/shard_map/repack/pallas_call | solution.py:107
  183.9 1.6 collective-permute-start.36
  185.9 1.5 collective-permute-start.34
  187.6 1.6 collective-permute-done.36
  189.1 1.3 collective-permute-start.24
  190.4 4.6 %collective-permute-start.21 = (bf16[128,2048]{1,0:T(8,128)(2,1)S(1)}, bf16[128,2048]{1,0:T(8,128)(2,1)S(1)}, u32[]{:S(2)}, u32[]{:S(2)}) collective-permute-start(bf16[128,2048]{1,0:T(8,128)(2,1)S(1)} %add_convert_fusion.4), channel_id=1, source_target_pairs={{0,8},{4,12},{8,16},{12,20},{16,24},{20,28},{1,9},{5,13},{9,17},{1... | collective-permute-start | bytes 1572872 | tf_op jit(solution)/shard_map/ppermute | solution.py:340
  195.1 0.8 multiply_convert_fusion
  196.7 1.5 collective-permute-done.37
  198.2 1.3 collective-permute-start.27
  200.1 1.1 copy-done.7
  201.2 8.4 %adapter_gradients.1 = (f32[2048,512]{1,0:T(8,128)}, f32[512,2048]{1,0:T(8,128)}) custom-call(s32[8]{0:T(128)} %pad_add_fusion.4.order_ref, s32[1,640]{1,0:T(1,128)} %pad_add_fusion.2.local_ref, bf16[16,640]{1,0:T(8,128)(2,1)} %copy-done.19, bf16[16,640]{1,0:T(8,128)(2,1)} %pad_maximum_fusion.7.up_ranks_ref, bf16[320,2048]{1,0:T(8,128)(2,1)} %get-tuple-element.60.own_ref, ...), custom_call_target="tpu_custom_call" | custom-call | flops 41943040 | bytes 212992 | tf_op jit(solution)/shard_map/adapter_gradients/pallas_call | solution.py:294
  209.7 9.8 %collective-permute-done.27 = bf16[128,2048]{1,0:T(8,128)(2,1)S(1)} collective-permute-done((bf16[128,2048]{1,0:T(8,128)(2,1)S(1)}, bf16[128,2048]{1,0:T(8,128)(2,1)S(1)}, u32[]{:S(2)}, u32[]{:S(2)}) %collective-permute-start.27) | collective-permute-done | bytes 524320 | tf_op jit(solution)/shard_map/ppermute | solution.py:344
  219.8 1.1 pad_maximum_fusion.2
  (132 shorter events, 17.1 us)
Async XLA Ops:
  0.6 6.8 %copy-start.3 = (bf16[64,8192]{1,0:T(8,128)(2,1)S(1)}, bf16[64,8192]{1,0:T(8,128)(2,1)}, u32[]{:S(2)}) copy-start(bf16[64,8192]{1,0:T(8,128)(2,1)} %param.7) | copy-start | bytes 3145732
  2.9 8.8 %copy-start.23 = (s32[256]{0:T(256)S(1)}, s32[256]{0:T(256)}, u32[]{:S(2)}) copy-start(s32[256]{0:T(256)} %param.8) | copy-start | bytes 3076
  2.9 9.8 %copy-start.4 = (bf16[2048,512]{1,0:T(8,128)(2,1)S(1)}, bf16[2048,512]{1,0:T(8,128)(2,1)}, u32[]{:S(2)}) copy-start(bf16[2048,512]{1,0:T(8,128)(2,1)} %param.10) | copy-start | bytes 6291460
  2.9 12.2 %collective-permute-start = (bf16[64,2048]{1,0:T(8,128)(2,1)}, bf16[64,2048]{1,0:T(8,128)(2,1)}, u32[]{:S(2)}, u32[]{:S(2)}) collective-permute-start(bf16[64,2048]{1,0:T(8,128)(2,1)} %get-tuple-element.84), channel_id=1, source_target_pairs={{0,1},{1,0},{2,3},{3,2},{4,5},{5,4},{6,7},{7,6},{8,9},{9,8},{10,11... | collective-permute-start | bytes 786440 | tf_op jit(solution)/shard_map/ppermute | solution.py:354
  5.9 13.7 %collective-permute-start.1 = (bf16[64,2048]{1,0:T(8,128)(2,1)}, bf16[64,2048]{1,0:T(8,128)(2,1)}, u32[]{:S(2)}, u32[]{:S(2)}) collective-permute-start(bf16[64,2048]{1,0:T(8,128)(2,1)} %get-tuple-element.83), channel_id=1, source_target_pairs={{0,2},{1,3},{2,0},{3,1},{4,6},{5,7},{6,4},{7,5},{8,10},{9,11},{10,... | collective-permute-start | bytes 786440 | tf_op jit(solution)/shard_map/ppermute | solution.py:354
  7.4 12.2 %collective-permute-start.2 = (bf16[64,2048]{1,0:T(8,128)(2,1)}, bf16[64,2048]{1,0:T(8,128)(2,1)}, u32[]{:S(2)}, u32[]{:S(2)}) collective-permute-start(bf16[64,2048]{1,0:T(8,128)(2,1)} %get-tuple-element.82), channel_id=1, source_target_pairs={{0,3},{1,2},{2,1},{3,0},{4,7},{5,6},{6,5},{7,4},{8,11},{9,10},{10,... | collective-permute-start | bytes 786440 | tf_op jit(solution)/shard_map/ppermute | solution.py:354
  7.5 21.9 %collective-permute-start.4 = (bf16[64,2048]{1,0:T(8,128)(2,1)S(1)}, bf16[64,2048]{1,0:T(8,128)(2,1)S(1)}, u32[]{:S(2)}, u32[]{:S(2)}) collective-permute-start(bf16[64,2048]{1,0:T(8,128)(2,1)S(1)} %pad_maximum_fusion.4), channel_id=1, source_target_pairs={{0,8},{4,12},{8,16},{12,20},{16,24},{20,28},{24,0},{28,4},{1,9},{5... | collective-permute-start | bytes 786440 | tf_op jit(solution)/shard_map/ppermute | solution.py:336
  9.6 19.8 %collective-permute-start.3 = (bf16[64,2048]{1,0:T(8,128)(2,1)S(1)}, bf16[64,2048]{1,0:T(8,128)(2,1)S(1)}, u32[]{:S(2)}, u32[]{:S(2)}) collective-permute-start(bf16[64,2048]{1,0:T(8,128)(2,1)S(1)} %pad_maximum_fusion.6), channel_id=1, source_target_pairs={{0,24},{4,28},{8,0},{12,4},{16,8},{20,12},{24,16},{28,20},{1,25},{... | collective-permute-start | bytes 786440 | tf_op jit(solution)/shard_map/ppermute | solution.py:336
  15.2 25.4 %collective-permute-start.6 = (bf16[64,2048]{1,0:T(8,128)(2,1)}, bf16[64,2048]{1,0:T(8,128)(2,1)S(1)}, u32[]{:S(2)}, u32[]{:S(2)}) collective-permute-start(bf16[64,2048]{1,0:T(8,128)(2,1)} %pad_maximum_fusion.5), channel_id=1, source_target_pairs={{0,16},{4,20},{8,24},{12,28},{16,0},{20,4},{24,8},{28,12},{1,17},{... | collective-permute-start | bytes 786440 | tf_op jit(solution)/shard_map/ppermute | solution.py:336
  19.6 43.1 %collective-permute-start.8 = (bf16[512,2048]{1,0:T(8,128)(2,1)}, bf16[512,2048]{1,0:T(8,128)(2,1)}, u32[]{:S(2)}, u32[]{:S(2)}) collective-permute-start(bf16[512,2048]{1,0:T(8,128)(2,1)} %bitcast.14.refs_2_.own_d_ref), channel_id=1, source_target_pairs={{0,4},{4,0},{8,12},{12,8},{16,20},{20,16},{24,28},{28,24},{1,5},{5... | collective-permute-start | bytes 6291464 | tf_op jit(solution)/shard_map/ppermute | solution.py:351
  19.6 63.3 %collective-permute-start.9 = (bf16[2048,1024]{1,0:T(8,128)(2,1)}, bf16[2048,1024]{1,0:T(8,128)(2,1)}, u32[]{:S(2)}, u32[]{:S(2)}) collective-permute-start(bf16[2048,1024]{1,0:T(8,128)(2,1)} %own_w_ref), channel_id=1, source_target_pairs={{0,4},{4,0},{8,12},{12,8},{16,20},{20,16},{24,28},{28,24},{1,5},{5... | collective-permute-start | bytes 12582920 | tf_op jit(solution)/shard_map/ppermute | solution.py:351
  20.7 13.5 %all-to-all-start = ((s32[8,1,256]{2,1,0:T(1,128)}), s32[8,1,256]{2,1,0:T(1,128)S(1)}, u32[]{:S(2)}, u32[]{:S(2)}) async-start(s32[8,1,256]{2,1,0:T(1,128)} %broadcast_in_dim.59), calls=%async_computation | async-start | bytes 16384 | tf_op jit(solution)/shard_map/all_to_all | solution.py:381
  29.4 4.8 %copy-start.20 = (bf16[64,2048]{1,0:T(8,128)(2,1)}, bf16[64,2048]{1,0:T(8,128)(2,1)S(1)}, u32[]{:S(2)}) copy-start(bf16[64,2048]{1,0:T(8,128)(2,1)S(1)} %collective-permute-done.4) | copy-start | bytes 786436
  29.4 4.8 %copy-start.21 = (bf16[64,2048]{1,0:T(8,128)(2,1)}, bf16[64,2048]{1,0:T(8,128)(2,1)S(1)}, u32[]{:S(2)}) copy-start(bf16[64,2048]{1,0:T(8,128)(2,1)S(1)} %collective-permute-done.3) | copy-start | bytes 786436
  34.2 64.4 %all-to-all-start.1 = ((bf16[8,80,2048]{2,1,0:T(8,128)(2,1)}), bf16[8,80,2048]{2,1,0:T(8,128)(2,1)S(1)}, u32[]{:S(2)}, u32[]{:S(2)}) async-start(bf16[8,80,2048]{2,1,0:T(8,128)(2,1)} %bitcast.57), calls=%async_computation.1 | async-start | bytes 5242880 | tf_op jit(solution)/shard_map/all_to_all | solution.py:400
  39.0 19.4 %copy-start.1 = (bf16[1,2,64,2048]{3,2,1,0:T(8,128)(2,1)}, bf16[1,2,64,2048]{3,2,1,0:T(8,128)(2,1)S(1)}, u32[]{:S(2)}) copy-start(bf16[1,2,64,2048]{3,2,1,0:T(8,128)(2,1)S(1)} %maximum_bitcast_fusion.refs_0_) | copy-start | bytes 1572868
  39.0 14.3 %collective-permute-start.5 = (bf16[1,2,64,2048]{3,2,1,0:T(8,128)(2,1)S(1)}, bf16[1,2,64,2048]{3,2,1,0:T(8,128)(2,1)S(1)}, u32[]{:S(2)}, u32[]{:S(2)}) collective-permute-start(bf16[1,2,64,2048]{3,2,1,0:T(8,128)(2,1)S(1)} %maximum_bitcast_fusion.refs_0_), channel_id=1, source_target_pairs={{0,1},{1,0},{2,3},{3,2},{4,5},{5,4},{6,7},{7,6},{8,9},{9,8},{10,11... | collective-permute-start | bytes 1572872 | tf_op jit(solution)/shard_map/ppermute | solution.py:354
  40.6 17.8 %copy-start.2 = (bf16[1,2,64,2048]{3,2,1,0:T(8,128)(2,1)}, bf16[1,2,64,2048]{3,2,1,0:T(8,128)(2,1)S(1)}, u32[]{:S(2)}) copy-start(bf16[1,2,64,2048]{3,2,1,0:T(8,128)(2,1)S(1)} %maximum_bitcast_fusion.1.refs_3_) | copy-start | bytes 1572868
  40.6 14.0 %collective-permute-start.7 = (bf16[1,2,64,2048]{3,2,1,0:T(8,128)(2,1)S(1)}, bf16[1,2,64,2048]{3,2,1,0:T(8,128)(2,1)S(1)}, u32[]{:S(2)}, u32[]{:S(2)}) collective-permute-start(bf16[1,2,64,2048]{3,2,1,0:T(8,128)(2,1)S(1)} %maximum_bitcast_fusion.1.refs_3_), channel_id=1, source_target_pairs={{0,2},{1,3},{2,0},{3,1},{4,6},{5,7},{6,4},{7,5},{8,10},{9,11},{10,... | collective-permute-start | bytes 1572872 | tf_op jit(solution)/shard_map/ppermute | solution.py:354
  53.3 5.1 %copy-start.5 = (bf16[1,2,64,2048]{3,2,1,0:T(8,128)(2,1)}, bf16[1,2,64,2048]{3,2,1,0:T(8,128)(2,1)S(1)}, u32[]{:S(2)}) copy-start(bf16[1,2,64,2048]{3,2,1,0:T(8,128)(2,1)S(1)} %collective-permute-done.5.refs_1_) | copy-start | bytes 1572868
  54.6 3.8 %copy-start.6 = (bf16[1,2,64,2048]{3,2,1,0:T(8,128)(2,1)}, bf16[1,2,64,2048]{3,2,1,0:T(8,128)(2,1)S(1)}, u32[]{:S(2)}) copy-start(bf16[1,2,64,2048]{3,2,1,0:T(8,128)(2,1)S(1)} %collective-permute-done.7.refs_4_) | copy-start | bytes 1572868
  55.8 24.7 %collective-permute-start.10 = (bf16[2,2,64,2048]{3,2,1,0:T(8,128)(2,1)}, bf16[2,2,64,2048]{3,2,1,0:T(8,128)(2,1)}, u32[]{:S(2)}, u32[]{:S(2)}) collective-permute-start(bf16[2,2,64,2048]{3,2,1,0:T(8,128)(2,1)} %pad_maximum_fusion), channel_id=1, source_target_pairs={{0,2},{1,3},{2,0},{3,1},{4,6},{5,7},{6,4},{7,5},{8,10},{9,11},{10,... | collective-permute-start | bytes 3145736 | tf_op jit(solution)/shard_map/ppermute | solution.py:354
  58.4 24.5 %collective-permute-start.11 = (bf16[2,2,64,2048]{3,2,1,0:T(8,128)(2,1)}, bf16[2,2,64,2048]{3,2,1,0:T(8,128)(2,1)}, u32[]{:S(2)}, u32[]{:S(2)}) collective-permute-start(bf16[2,2,64,2048]{3,2,1,0:T(8,128)(2,1)} %pad_maximum_fusion.1), channel_id=1, source_target_pairs={{0,1},{1,0},{2,3},{3,2},{4,5},{5,4},{6,7},{7,6},{8,9},{9,8},{10,11... | collective-permute-start | bytes 3145736 | tf_op jit(solution)/shard_map/ppermute | solution.py:354
  61.4 60.5 %collective-permute-start.28 = (bf16[256,2048]{1,0:T(8,128)(2,1)}, bf16[256,2048]{1,0:T(8,128)(2,1)}, u32[]{:S(2)}, u32[]{:S(2)}) collective-permute-start(bf16[256,2048]{1,0:T(8,128)(2,1)} %refs_0_.1), channel_id=1, source_target_pairs={{8,0},{12,4},{16,8},{20,12},{24,16},{28,20},{9,1},{13,5},{17,9},{2... | collective-permute-start | bytes 3145736 | tf_op jit(solution)/shard_map/ppermute | solution.py:348
  62.7 59.2 %collective-permute-start.29 = (bf16[256,2048]{1,0:T(8,128)(2,1)}, bf16[256,2048]{1,0:T(8,128)(2,1)}, u32[]{:S(2)}, u32[]{:S(2)}) collective-permute-start(bf16[256,2048]{1,0:T(8,128)(2,1)} %refs_0_.1), channel_id=1, source_target_pairs={{0,8},{4,12},{8,16},{12,20},{16,24},{20,28},{1,9},{5,13},{9,17},{1... | collective-permute-start | bytes 3145736 | tf_op jit(solution)/shard_map/ppermute | solution.py:348
  98.6 1.5 copy-start
  105.6 5.1 %collective-permute-start.14 = (f32[16,640]{1,0:T(8,128)}, f32[16,640]{1,0:T(8,128)S(1)}, u32[]{:S(2)}, u32[]{:S(2)}) collective-permute-start(f32[16,640]{1,0:T(8,128)} %token_ranks.1), channel_id=1, source_target_pairs={{0,3},{1,2},{2,1},{3,0},{4,7},{5,6},{6,5},{7,4},{8,11},{9,10},{10,... | collective-permute-start | bytes 122888 | tf_op jit(solution)/shard_map/ppermute | solution.py:354
  108.1 4.2 %collective-permute-start.13 = (f32[16,640]{1,0:T(8,128)}, f32[16,640]{1,0:T(8,128)S(1)}, u32[]{:S(2)}, u32[]{:S(2)}) collective-permute-start(f32[16,640]{1,0:T(8,128)} %token_ranks.1), channel_id=1, source_target_pairs={{0,2},{1,3},{2,0},{3,1},{4,6},{5,7},{6,4},{7,5},{8,10},{9,11},{10,... | collective-permute-start | bytes 122888 | tf_op jit(solution)/shard_map/ppermute | solution.py:354
  108.6 4.2 %collective-permute-start.12 = (f32[16,640]{1,0:T(8,128)}, f32[16,640]{1,0:T(8,128)S(1)}, u32[]{:S(2)}, u32[]{:S(2)}) collective-permute-start(f32[16,640]{1,0:T(8,128)} %token_ranks.1), channel_id=1, source_target_pairs={{0,1},{1,0},{2,3},{3,2},{4,5},{5,4},{6,7},{7,6},{8,9},{9,8},{10,11... | collective-permute-start | bytes 122888 | tf_op jit(solution)/shard_map/ppermute | solution.py:354
  113.6 1.3 copy-start.19
  113.6 1.3 collective-permute-start.15
  121.9 15.7 %copy-start.14 = (bf16[128,2048]{1,0:T(8,128)(2,1)S(1)}, bf16[128,2048]{1,0:T(8,128)(2,1)}, u32[]{:S(2)}) copy-start(bf16[128,2048]{1,0:T(8,128)(2,1)} %get-tuple-element.53) | copy-start | bytes 1572868
  121.9 27.7 %collective-permute-start.30 = (bf16[256,2048]{1,0:T(8,128)(2,1)}, bf16[256,2048]{1,0:T(8,128)(2,1)S(1)}, u32[]{:S(2)}, u32[]{:S(2)}) collective-permute-start(bf16[256,2048]{1,0:T(8,128)(2,1)} %collective-permute-done.28.refs_1_), channel_id=1, source_target_pairs={{8,0},{12,4},{16,8},{20,12},{9,1},{13,5},{17,9},{21,13},{10,2},{14... | collective-permute-start | bytes 3145736 | tf_op jit(solution)/shard_map/ppermute | solution.py:348
  123.4 27.6 %collective-permute-start.32 = (bf16[256,2048]{1,0:T(8,128)(2,1)}, bf16[256,2048]{1,0:T(8,128)(2,1)S(1)}, u32[]{:S(2)}, u32[]{:S(2)}) collective-permute-start(bf16[256,2048]{1,0:T(8,128)(2,1)} %collective-permute-done.29.refs_4_), channel_id=1, source_target_pairs={{8,16},{12,20},{16,24},{20,28},{9,17},{13,21},{17,25},{21,29},{10,... | collective-permute-start | bytes 3145736 | tf_op jit(solution)/shard_map/ppermute | solution.py:348
  124.1 13.5 %collective-permute-start.22 = (bf16[128,2048]{1,0:T(8,128)(2,1)}, bf16[128,2048]{1,0:T(8,128)(2,1)S(1)}, u32[]{:S(2)}, u32[]{:S(2)}) collective-permute-start(bf16[128,2048]{1,0:T(8,128)(2,1)} %get-tuple-element.48), channel_id=1, source_target_pairs={{24,16},{28,20},{25,17},{29,21},{26,18},{30,22},{27,19},{31,23}} | collective-permute-start | bytes 1572872 | tf_op jit(solution)/shard_map/ppermute | solution.py:344
  124.8 18.2 %collective-permute-start.16 = (bf16[128,2048]{1,0:T(8,128)(2,1)}, bf16[128,2048]{1,0:T(8,128)(2,1)S(1)}, u32[]{:S(2)}, u32[]{:S(2)}) collective-permute-start(bf16[128,2048]{1,0:T(8,128)(2,1)} %get-tuple-element.50), channel_id=1, source_target_pairs={{0,8},{4,12},{1,9},{5,13},{2,10},{6,14},{3,11},{7,15}} | collective-permute-start | bytes 1572872 | tf_op jit(solution)/shard_map/ppermute | solution.py:340
  130.4 18.5 %collective-permute-start.25 = (bf16[128,2048]{1,0:T(8,128)(2,1)}, bf16[128,2048]{1,0:T(8,128)(2,1)S(1)}, u32[]{:S(2)}, u32[]{:S(2)}) collective-permute-start(bf16[128,2048]{1,0:T(8,128)(2,1)} %get-tuple-element.51), channel_id=1, source_target_pairs={{24,16},{28,20},{25,17},{29,21},{26,18},{30,22},{27,19},{31,23}} | collective-permute-start | bytes 1572872 | tf_op jit(solution)/shard_map/ppermute | solution.py:344
  137.7 16.5 %copy-start.18 = (bf16[128,2048]{1,0:T(8,128)(2,1)S(1)}, bf16[128,2048]{1,0:T(8,128)(2,1)}, u32[]{:S(2)}) copy-start(bf16[128,2048]{1,0:T(8,128)(2,1)} %get-tuple-element.52) | copy-start | bytes 1572868
  137.7 16.5 %collective-permute-start.19 = (bf16[128,2048]{1,0:T(8,128)(2,1)S(1)}, bf16[128,2048]{1,0:T(8,128)(2,1)S(1)}, u32[]{:S(2)}, u32[]{:S(2)}) collective-permute-start(bf16[128,2048]{1,0:T(8,128)(2,1)S(1)} %copy-done.14), channel_id=1, source_target_pairs={{0,8},{4,12},{1,9},{5,13},{2,10},{6,14},{3,11},{7,15}} | collective-permute-start | bytes 1572872 | tf_op jit(solution)/shard_map/ppermute | solution.py:340
  143.0 23.1 %copy-start.17 = (bf16[128,2048]{1,0:T(8,128)(2,1)S(1)}, bf16[128,2048]{1,0:T(8,128)(2,1)}, u32[]{:S(2)}) copy-start(bf16[128,2048]{1,0:T(8,128)(2,1)} %get-tuple-element.48) | copy-start | bytes 1572868
  144.4 21.0 %collective-permute-start.17 = (bf16[128,2048]{1,0:T(8,128)(2,1)S(1)}, bf16[128,2048]{1,0:T(8,128)(2,1)S(1)}, u32[]{:S(2)}, u32[]{:S(2)}) collective-permute-start(bf16[128,2048]{1,0:T(8,128)(2,1)S(1)} %get-tuple-element.89), channel_id=1, source_target_pairs={{0,8},{4,12},{8,16},{12,20},{1,9},{5,13},{9,17},{13,21},{2,10},{6,... | collective-permute-start | bytes 1572872 | tf_op jit(solution)/shard_map/ppermute | solution.py:340
  148.9 17.3 %collective-permute-start.23 = (bf16[128,2048]{1,0:T(8,128)(2,1)S(1)}, bf16[128,2048]{1,0:T(8,128)(2,1)S(1)}, u32[]{:S(2)}, u32[]{:S(2)}) collective-permute-start(bf16[128,2048]{1,0:T(8,128)(2,1)S(1)} %get-tuple-element.88), channel_id=1, source_target_pairs={{16,8},{20,12},{24,16},{28,20},{17,9},{21,13},{25,17},{29,21},{18,... | collective-permute-start | bytes 1572872 | tf_op jit(solution)/shard_map/ppermute | solution.py:344
  149.7 16.6 %copy-start.8 = (bf16[256,2048]{1,0:T(8,128)(2,1)}, bf16[256,2048]{1,0:T(8,128)(2,1)S(1)}, u32[]{:S(2)}) copy-start(bf16[256,2048]{1,0:T(8,128)(2,1)S(1)} %collective-permute-done.30.refs_2_) | copy-start | bytes 3145732
  149.7 26.0 %collective-permute-start.31 = (bf16[256,2048]{1,0:T(8,128)(2,1)S(1)}, bf16[256,2048]{1,0:T(8,128)(2,1)S(1)}, u32[]{:S(2)}, u32[]{:S(2)}) collective-permute-start(bf16[256,2048]{1,0:T(8,128)(2,1)S(1)} %collective-permute-done.30.refs_2_), channel_id=1, source_target_pairs={{8,0},{12,4},{9,1},{13,5},{10,2},{14,6},{11,3},{15,7}} | collective-permute-start | bytes 3145736 | tf_op jit(solution)/shard_map/ppermute | solution.py:348
  151.0 15.3 %copy-start.9 = (bf16[256,2048]{1,0:T(8,128)(2,1)}, bf16[256,2048]{1,0:T(8,128)(2,1)S(1)}, u32[]{:S(2)}) copy-start(bf16[256,2048]{1,0:T(8,128)(2,1)S(1)} %collective-permute-done.32.refs_5_) | copy-start | bytes 3145732
  151.0 24.7 %collective-permute-start.33 = (bf16[256,2048]{1,0:T(8,128)(2,1)S(1)}, bf16[256,2048]{1,0:T(8,128)(2,1)S(1)}, u32[]{:S(2)}, u32[]{:S(2)}) collective-permute-start(bf16[256,2048]{1,0:T(8,128)(2,1)S(1)} %collective-permute-done.32.refs_5_), channel_id=1, source_target_pairs={{16,24},{20,28},{17,25},{21,29},{18,26},{22,30},{19,27},{23,31}} | collective-permute-start | bytes 3145736 | tf_op jit(solution)/shard_map/ppermute | solution.py:348
  154.1 17.1 %copy-start.16 = (bf16[128,2048]{1,0:T(8,128)(2,1)S(1)}, bf16[128,2048]{1,0:T(8,128)(2,1)}, u32[]{:S(2)}) copy-start(bf16[128,2048]{1,0:T(8,128)(2,1)} %get-tuple-element.50) | copy-start | bytes 1572868
  155.3 30.7 %collective-permute-start.20 = (bf16[128,2048]{1,0:T(8,128)(2,1)}, bf16[128,2048]{1,0:T(8,128)(2,1)S(1)}, u32[]{:S(2)}, u32[]{:S(2)}) collective-permute-start(bf16[128,2048]{1,0:T(8,128)(2,1)} %get-tuple-element.87), channel_id=1, source_target_pairs={{0,8},{4,12},{8,16},{12,20},{1,9},{5,13},{9,17},{13,21},{2,10},{6,... | collective-permute-start | bytes 1572872 | tf_op jit(solution)/shard_map/ppermute | solution.py:340
  165.4 30.6 %collective-permute-start.26 = (bf16[128,2048]{1,0:T(8,128)(2,1)S(1)}, bf16[128,2048]{1,0:T(8,128)(2,1)S(1)}, u32[]{:S(2)}, u32[]{:S(2)}) collective-permute-start(bf16[128,2048]{1,0:T(8,128)(2,1)S(1)} %get-tuple-element.86), channel_id=1, source_target_pairs={{16,8},{20,12},{24,16},{28,20},{17,9},{21,13},{25,17},{29,21},{18,... | collective-permute-start | bytes 1572872 | tf_op jit(solution)/shard_map/ppermute | solution.py:344
  166.2 43.4 %collective-permute-start.18 = (bf16[128,2048]{1,0:T(8,128)(2,1)S(1)}, bf16[128,2048]{1,0:T(8,128)(2,1)S(1)}, u32[]{:S(2)}, u32[]{:S(2)}) collective-permute-start(bf16[128,2048]{1,0:T(8,128)(2,1)S(1)} %add_convert_fusion.5), channel_id=1, source_target_pairs={{0,8},{4,12},{8,16},{12,20},{16,24},{20,28},{1,9},{5,13},{9,17},{1... | collective-permute-start | bytes 1572872 | tf_op jit(solution)/shard_map/ppermute | solution.py:340
  175.7 1.0 copy-start.10
  175.7 1.3 copy-start.11
  177.0 10.4 %copy-start.15 = (bf16[128,2048]{1,0:T(8,128)(2,1)S(1)}, bf16[128,2048]{1,0:T(8,128)(2,1)}, u32[]{:S(2)}) copy-start(bf16[128,2048]{1,0:T(8,128)(2,1)} %get-tuple-element.51) | copy-start | bytes 1572868
  183.9 5.3 %collective-permute-start.36 = (f32[2,16,320]{2,1,0:T(8,128)}, f32[2,16,320]{2,1,0:T(8,128)S(1)}, u32[]{:S(2)}, u32[]{:S(2)}) collective-permute-start(f32[2,16,320]{2,1,0:T(8,128)} %get-tuple-element.59), channel_id=1, source_target_pairs={{0,3},{1,2},{2,1},{3,0},{4,7},{5,6},{6,5},{7,4},{8,11},{9,10},{10,... | collective-permute-start | bytes 122888 | tf_op jit(solution)/shard_map/ppermute | solution.py:354
  185.4 5.0 %collective-permute-start.35 = (f32[2,16,320]{2,1,0:T(8,128)}, f32[2,16,320]{2,1,0:T(8,128)S(1)}, u32[]{:S(2)}, u32[]{:S(2)}) collective-permute-start(f32[2,16,320]{2,1,0:T(8,128)} %get-tuple-element.59), channel_id=1, source_target_pairs={{0,2},{1,3},{2,0},{3,1},{4,6},{5,7},{6,4},{7,5},{8,10},{9,11},{10,... | collective-permute-start | bytes 122888 | tf_op jit(solution)/shard_map/ppermute | solution.py:354
  185.9 9.1 %collective-permute-start.34 = (f32[2,16,320]{2,1,0:T(8,128)}, f32[2,16,320]{2,1,0:T(8,128)S(1)}, u32[]{:S(2)}, u32[]{:S(2)}) collective-permute-start(f32[2,16,320]{2,1,0:T(8,128)} %get-tuple-element.59), channel_id=1, source_target_pairs={{0,1},{1,0},{2,3},{3,2},{4,5},{5,4},{6,7},{7,6},{8,9},{9,8},{10,11... | collective-permute-start | bytes 122888 | tf_op jit(solution)/shard_map/ppermute | solution.py:354
  189.1 20.5 %collective-permute-start.24 = (bf16[128,2048]{1,0:T(8,128)(2,1)S(1)}, bf16[128,2048]{1,0:T(8,128)(2,1)S(1)}, u32[]{:S(2)}, u32[]{:S(2)}) collective-permute-start(bf16[128,2048]{1,0:T(8,128)(2,1)S(1)} %add_convert_fusion.3), channel_id=1, source_target_pairs={{8,0},{12,4},{16,8},{20,12},{24,16},{28,20},{9,1},{13,5},{17,9},{2... | collective-permute-start | bytes 1572872 | tf_op jit(solution)/shard_map/ppermute | solution.py:344
  190.4 19.2 %collective-permute-start.21 = (bf16[128,2048]{1,0:T(8,128)(2,1)S(1)}, bf16[128,2048]{1,0:T(8,128)(2,1)S(1)}, u32[]{:S(2)}, u32[]{:S(2)}) collective-permute-start(bf16[128,2048]{1,0:T(8,128)(2,1)S(1)} %add_convert_fusion.4), channel_id=1, source_target_pairs={{0,8},{4,12},{8,16},{12,20},{16,24},{20,28},{1,9},{5,13},{9,17},{1... | collective-permute-start | bytes 1572872 | tf_op jit(solution)/shard_map/ppermute | solution.py:340
  195.0 5.1 %collective-permute-start.38 = (bf16[320,2048]{1,0:T(8,128)(2,1)}, bf16[320,2048]{1,0:T(8,128)(2,1)S(1)}, u32[]{:S(2)}, u32[]{:S(2)}) collective-permute-start(bf16[320,2048]{1,0:T(8,128)(2,1)} %get-tuple-element.61), channel_id=1, source_target_pairs={{0,4},{4,0},{8,12},{12,8},{16,20},{20,16},{24,28},{28,24},{1,5},{5... | collective-permute-start | bytes 3932168 | tf_op jit(solution)/shard_map/ppermute | solution.py:351
  196.0 2.2 collective-permute-start.37
  198.2 21.3 %collective-permute-start.27 = (bf16[128,2048]{1,0:T(8,128)(2,1)S(1)}, bf16[128,2048]{1,0:T(8,128)(2,1)S(1)}, u32[]{:S(2)}, u32[]{:S(2)}) collective-permute-start(bf16[128,2048]{1,0:T(8,128)(2,1)S(1)} %add_convert_fusion.2), channel_id=1, source_target_pairs={{8,0},{12,4},{16,8},{20,12},{24,16},{28,20},{9,1},{13,5},{17,9},{2... | collective-permute-start | bytes 1572872 | tf_op jit(solution)/shard_map/ppermute | solution.py:344
  200.1 1.1 copy-start.7
  201.2 18.2 %copy-start.13 = (f32[128,2048]{1,0:T(8,128)S(1)}, f32[128,2048]{1,0:T(8,128)}, u32[]{:S(2)}) copy-start(f32[128,2048]{1,0:T(8,128)} %get-tuple-element.65) | copy-start | bytes 3145732
  209.6 10.0 %copy-start.12 = (f32[128,2048]{1,0:T(8,128)S(1)}, f32[128,2048]{1,0:T(8,128)}, u32[]{:S(2)}) copy-start(f32[128,2048]{1,0:T(8,128)} %get-tuple-element.47) | copy-start | bytes 3145732
  (1 other events, 0.6 us)

commit v6 on v5

--- a/solution.py
+++ b/solution.py
@@ -204,7 +204,7 @@
     blocks, tensors = 2 * blocks, sum(len(ks) for _, ks in names) // 2
     rows = blocks * sub * tensors
     width, depth = weights[0].shape
-    tile = min(512, width)
+    tile = min(1024, width)
     return pl.pallas_call(
         functools.partial(frozen_kernel, names),
         grid=(width // tile,),

time: 222 us -> 223 us (level)
  transfers between devices with their start and end apart: 41 -> 41, of which waited for: 18 -> 17; matrix products, arithmetic and copies ran while one was open for 9% -> 8% of each run, Pallas kernels for 24% -> 24%
where the time goes in v6:
time: 223 us; the launch traced here: 222 us
  starting transfers between devices  74.9 us (34%)
  waiting for transfers between devices  65.6 us (29%)
  Pallas kernels  53 us (24%)
  other arithmetic  15.1 us (7%)
  local copies, waits for them, and re-layouts  12 us (5%)
    ppermute x13, waiting for transfers between devices, flip(): return lax.ppermute(x, 'tensor', [(t, t ^ k) for t in range(tensors)])  32 us
    ppermute x6, starting transfers between devices, up_line(): return lax.ppermute(x, 'adapter', pairs)  26.4 us
    ppermute x13, starting transfers between devices, flip(): return lax.ppermute(x, 'tensor', [(t, t ^ k) for t in range(tensors)])  16.8 us
    pallas_call x1, Pallas kernels, frozen_part(): pl.pallas_call(functools.partial(frozen_kernel, names), grid=(width // ti...  16 us
    pallas_call x2, Pallas kernels, add_term(): pl.pallas_call(functools.partial(term_kernel, per_owner), grid=(width //...  13 us
    ppermute x6, waiting for transfers between devices, up_line(): return lax.ppermute(x, 'adapter', pairs)  12 us
    ppermute x6, starting transfers between devices, attn_line(): lax.ppermute(x, 'adapter', [(2 * z + c, 2 * (z + way) + c) for z in plane...  11 us
    ppermute x6, waiting for transfers between devices, down_line(): return lax.ppermute(x, 'adapter', pairs)  10.9 us
  transfers between devices with their start and end apart: 41, of which 17 were waited for; matrix products, arithmetic and copies ran while one was open for 8% of the time, Pallas kernels for 24%

profile of v6, /device:TPU:0, one launch (start us, length us, event | category | flops | bytes accessed | tf_op | source)
XLA Modules:
  0.0 222.0 jit_solution(14649941223558303664)
XLA Ops:
  0.7 2.3 %constant_dynamic-slice_fusion.8 = (bf16[64,2048]{1,0:T(8,128)(2,1)}, bf16[64,2048]{1,0:T(8,128)(2,1)}, bf16[64,2048]{1,0:T(8,128)(2,1)}, bf16[64,2048]{1,0:T(8,128)(2,1)}) fusion(bf16[64,8192]{1,0:T(8,128)(2,1)} %param.7, s32[]{:T(128)S(6)} %select_n.162, s32[]{:T(128)S(6)} %select_n.161, s32[]{:T(128)S(6)} %select_n.160, s32[]{:T(128)S(6)} %select_n.159), kind=kLoop, calls=%fused_computation.74 | loop fusion | bytes 2097168 | tf_op jit(solution)/shard_map/dynamic_slice | solution.py:360
  2.9 3.0 %collective-permute-start = (bf16[64,2048]{1,0:T(8,128)(2,1)}, bf16[64,2048]{1,0:T(8,128)(2,1)}, u32[]{:S(2)}, u32[]{:S(2)}) collective-permute-start(bf16[64,2048]{1,0:T(8,128)(2,1)} %get-tuple-element.84), channel_id=1, source_target_pairs={{0,1},{1,0},{2,3},{3,2},{4,5},{5,4},{6,7},{7,6},{8,9},{9,8},{10,11... | collective-permute-start | bytes 786440 | tf_op jit(solution)/shard_map/ppermute | solution.py:354
  5.9 1.5 collective-permute-start.1
  7.5 2.1 collective-permute-start.4
  9.6 2.1 collective-permute-start.3
  12.7 2.4 %copy.11 = bf16[2048,512]{0,1:T(8,128)(2,1)} copy(bf16[2048,512]{1,0:T(8,128)(2,1)S(1)} %copy-done.4) | data formatting | bytes 4194304 | tf_op args[4]
  15.2 1.3 collective-permute-start.6
  16.5 3.1 %collective-permute-done.1.refs_2_ = bf16[64,2048]{1,0:T(8,128)(2,1)} collective-permute-done((bf16[64,2048]{1,0:T(8,128)(2,1)}, bf16[64,2048]{1,0:T(8,128)(2,1)}, u32[]{:S(2)}, u32[]{:S(2)}) %collective-permute-start.1) | collective-permute-done | bytes 262176 | tf_op jit(solution)/shard_map/ppermute | solution.py:354
  20.7 4.9 %all-to-all-start = ((s32[8,1,256]{2,1,0:T(1,128)}), s32[8,1,256]{2,1,0:T(1,128)S(1)}, u32[]{:S(2)}, u32[]{:S(2)}) async-start(s32[8,1,256]{2,1,0:T(1,128)} %broadcast_in_dim.59), calls=%async_computation | async-start | bytes 16384 | tf_op jit(solution)/shard_map/all_to_all | solution.py:381
  26.2 3.2 %pack_rows.1 = bf16[640,2048]{1,0:T(8,128)(2,1)} custom-call(s32[1,256]{1,0:T(1,128)} %bitcast.65, bf16[64,2048]{1,0:T(8,128)(2,1)} %get-tuple-element.41.refs_0_, bf16[64,2048]{1,0:T(8,128)(2,1)} %collective-permute-done.refs_1_, bf16[64,2048]{1,0:T(8,128)(2,1)} %collective-permute-done.1.refs_2_, bf16[64,2048]{1,0:T(8,128)(2,1)} %collective-permute-done.2.refs_3_), custom_call_target="tpu_custom_call" | custom-call | flops 10485760 | bytes 57344 | tf_op jit(solution)/shard_map/pack_rows/pallas_call | solution.py:43
  29.4 4.8 %all-to-all-done = s32[8,1,256]{2,1,0:T(1,128)S(1)} async-done(((s32[8,1,256]{2,1,0:T(1,128)}), s32[8,1,256]{2,1,0:T(1,128)S(1)}, u32[]{:S(2)}, u32[]{:S(2)}) %all-to-all-start) | async-done | bytes 8224 | tf_op jit(solution)/shard_map/all_to_all | solution.py:381
  34.2 3.6 %all-to-all-start.1 = ((bf16[8,80,2048]{2,1,0:T(8,128)(2,1)}), bf16[8,80,2048]{2,1,0:T(8,128)(2,1)S(1)}, u32[]{:S(2)}, u32[]{:S(2)}) async-start(bf16[8,80,2048]{2,1,0:T(8,128)(2,1)} %bitcast.57), calls=%async_computation.1 | async-start | bytes 5242880 | tf_op jit(solution)/shard_map/all_to_all | solution.py:400
  37.9 1.1 maximum_bitcast_fusion.refs_0_
  39.0 1.6 collective-permute-start.5
  40.6 1.6 collective-permute-start.7
  43.0 10.3 %collective-permute-done.5.refs_1_ = bf16[1,2,64,2048]{3,2,1,0:T(8,128)(2,1)S(1)} collective-permute-done((bf16[1,2,64,2048]{3,2,1,0:T(8,128)(2,1)S(1)}, bf16[1,2,64,2048]{3,2,1,0:T(8,128)(2,1)S(1)}, u32[]{:S(2)}, u32[]{:S(2)}) %collective-permute-start.5) | collective-permute-done | bytes 524320 | tf_op jit(solution)/shard_map/ppermute | solution.py:354
  53.3 1.3 collective-permute-done.7.refs_4_
  54.6 1.1 pad_maximum_fusion
  55.8 1.5 collective-permute-start.10
  57.3 1.1 pad_maximum_fusion.1
  61.4 1.3 collective-permute-start.28
  62.7 5.5 %collective-permute-start.29 = (bf16[256,2048]{1,0:T(8,128)(2,1)}, bf16[256,2048]{1,0:T(8,128)(2,1)}, u32[]{:S(2)}, u32[]{:S(2)}) collective-permute-start(bf16[256,2048]{1,0:T(8,128)(2,1)} %refs_0_.1), channel_id=1, source_target_pairs={{0,8},{4,12},{8,16},{12,20},{16,24},{20,28},{1,9},{5,13},{9,17},{1... | collective-permute-start | bytes 3145736 | tf_op jit(solution)/shard_map/ppermute | solution.py:348
  70.5 10.0 %collective-permute-done.10.refs_2_ = bf16[2,2,64,2048]{3,2,1,0:T(8,128)(2,1)} collective-permute-done((bf16[2,2,64,2048]{3,2,1,0:T(8,128)(2,1)}, bf16[2,2,64,2048]{3,2,1,0:T(8,128)(2,1)}, u32[]{:S(2)}, u32[]{:S(2)}) %collective-permute-start.10) | collective-permute-done | bytes 1048608 | tf_op jit(solution)/shard_map/ppermute | solution.py:354
  80.5 2.4 %collective-permute-done.11.refs_5_ = bf16[2,2,64,2048]{3,2,1,0:T(8,128)(2,1)} collective-permute-done((bf16[2,2,64,2048]{3,2,1,0:T(8,128)(2,1)}, bf16[2,2,64,2048]{3,2,1,0:T(8,128)(2,1)}, u32[]{:S(2)}, u32[]{:S(2)}) %collective-permute-start.11) | collective-permute-done | bytes 1048608 | tf_op jit(solution)/shard_map/ppermute | solution.py:354
  82.9 16.0 %frozen_part.1.frozen_ref = f32[1024,2048]{1,0:T(8,128)} custom-call(s32[1]{0:T(128)} %bitcast.place_ref, bf16[2048,1024]{1,0:T(8,128)(2,1)} %own_w_ref, bf16[2048,1024]{1,0:T(8,128)(2,1)} %collective-permute-done.9.other_w_ref, bf16[1,2,64,2048]{3,2,1,0:T(8,128)(2,1)} %copy-done.1, bf16[1,2,64,2048]{3,2,1,0:T(8,128)(2,1)} %copy-done.5, ...), custom_call_target="tpu_custom_call" | custom-call | flops 134217728 | bytes 262144 | tf_op jit(solution)/shard_map/frozen_part/pallas_call | solution.py:208
  98.9 1.5 copy-done
  100.4 5.6 %token_ranks.1 = f32[16,640]{1,0:T(8,128)} custom-call(s32[8]{0:T(128)} %pad_add_fusion.4.order_ref, s32[1,640]{1,0:T(1,128)} %pad_add_fusion.2.local_ref, bf16[512,2048]{1,0:T(8,128)(2,1)} %weight_ref.1, bf16[640,2048]{1,0:T(8,128)(2,1)} %bitcast.41, bf16[640,2048]{1,0:T(8,128)(2,1)} %bitcast.42, bf16[640,2048]{1,0:T(8,128)(2,1)} %bitcast.43, ...), custom_call_target="tpu_custom_call" | custom-call | flops 20971520 | bytes 73728 | tf_op jit(solution)/shard_map/token_ranks/pallas_call | solution.py:153
  106.0 2.1 collective-permute-start.14
  108.6 0.9 collective-permute-start.12
  109.5 1.8 collective-permute-done.14
  111.3 1.0 collective-permute-done.13
  112.8 0.8 multiply_convert_fusion.1.refs_0_.grad_ranks_ref
  113.7 1.2 collective-permute-done.15.refs_1_
  115.5 6.4 %add_term.3 = (bf16[128,2048]{1,0:T(8,128)(2,1)}, bf16[128,2048]{1,0:T(8,128)(2,1)}, bf16[128,2048]{1,0:T(8,128)(2,1)}, bf16[128,2048]{1,0:T(8,128)(2,1)}) custom-call(f32[1024,2048]{1,0:T(8,128)} %frozen_part.1.frozen_ref, s32[4,1024]{1,0:T(4,128)} %bitcast.62, bf16[16,640]{1,0:T(8,128)(2,1)} %copy-done.19, bf16[16,640]{1,0:T(8,128)(2,1)} %copy-done.22, ...), custom_call_target="tpu_custom_call" | custom-call | flops 33554432 | bytes 163840 | tf_op jit(solution)/shard_map/add_term/pallas_call | solution.py:253
  121.9 1.4 collective-permute-start.30
  124.8 6.7 %collective-permute-start.16 = (bf16[128,2048]{1,0:T(8,128)(2,1)}, bf16[128,2048]{1,0:T(8,128)(2,1)S(1)}, u32[]{:S(2)}, u32[]{:S(2)}) collective-permute-start(bf16[128,2048]{1,0:T(8,128)(2,1)} %get-tuple-element.50), channel_id=1, source_target_pairs={{0,8},{4,12},{1,9},{5,13},{2,10},{6,14},{3,11},{7,15}} | collective-permute-start | bytes 1572872 | tf_op jit(solution)/shard_map/ppermute | solution.py:340
  131.5 0.9 collective-permute-start.25
  132.3 6.6 %add_term.2 = (bf16[128,2048]{1,0:T(8,128)(2,1)}, bf16[128,2048]{1,0:T(8,128)(2,1)}, f32[128,2048]{1,0:T(8,128)}, f32[128,2048]{1,0:T(8,128)}) custom-call(f32[1024,2048]{1,0:T(8,128)} %frozen_part.1.frozen_ref, s32[4,1024]{1,0:T(4,128)} %bitcast.63, bf16[16,640]{1,0:T(8,128)(2,1)} %copy-done.19, bf16[16,640]{1,0:T(8,128)(2,1)} %copy-done.22, ...), custom_call_target="tpu_custom_call" | custom-call | flops 33554432 | bytes 163840 | tf_op jit(solution)/shard_map/add_term/pallas_call | solution.py:253
  138.9 1.5 collective-permute-start.19
  140.4 3.7 %collective-permute-done.16 = bf16[128,2048]{1,0:T(8,128)(2,1)S(1)} collective-permute-done((bf16[128,2048]{1,0:T(8,128)(2,1)}, bf16[128,2048]{1,0:T(8,128)(2,1)S(1)}, u32[]{:S(2)}, u32[]{:S(2)}) %collective-permute-start.16) | collective-permute-done | bytes 524320 | tf_op jit(solution)/shard_map/ppermute | solution.py:340
  144.1 1.4 fusion.1
  145.5 4.3 %collective-permute-start.17 = (bf16[128,2048]{1,0:T(8,128)(2,1)S(1)}, bf16[128,2048]{1,0:T(8,128)(2,1)S(1)}, u32[]{:S(2)}, u32[]{:S(2)}) collective-permute-start(bf16[128,2048]{1,0:T(8,128)(2,1)S(1)} %get-tuple-element.89), channel_id=1, source_target_pairs={{0,8},{4,12},{8,16},{12,20},{1,9},{5,13},{9,17},{13,21},{2,10},{6,... | collective-permute-start | bytes 1572872 | tf_op jit(solution)/shard_map/ppermute | solution.py:340
  150.6 1.3 collective-permute-start.31
  152.6 2.6 %collective-permute-done.19 = bf16[128,2048]{1,0:T(8,128)(2,1)S(1)} collective-permute-done((bf16[128,2048]{1,0:T(8,128)(2,1)S(1)}, bf16[128,2048]{1,0:T(8,128)(2,1)S(1)}, u32[]{:S(2)}, u32[]{:S(2)}) %collective-permute-start.19) | collective-permute-done | bytes 524320 | tf_op jit(solution)/shard_map/ppermute | solution.py:340
  155.2 1.1 fusion.3
  156.4 4.4 %collective-permute-start.20 = (bf16[128,2048]{1,0:T(8,128)(2,1)}, bf16[128,2048]{1,0:T(8,128)(2,1)S(1)}, u32[]{:S(2)}, u32[]{:S(2)}) collective-permute-start(bf16[128,2048]{1,0:T(8,128)(2,1)} %get-tuple-element.87), channel_id=1, source_target_pairs={{0,8},{4,12},{8,16},{12,20},{1,9},{5,13},{9,17},{13,21},{2,10},{6,... | collective-permute-start | bytes 1572872 | tf_op jit(solution)/shard_map/ppermute | solution.py:340
  160.8 5.7 %collective-permute-done.17 = bf16[128,2048]{1,0:T(8,128)(2,1)S(1)} collective-permute-done((bf16[128,2048]{1,0:T(8,128)(2,1)S(1)}, bf16[128,2048]{1,0:T(8,128)(2,1)S(1)}, u32[]{:S(2)}, u32[]{:S(2)}) %collective-permute-start.17) | collective-permute-done | bytes 524320 | tf_op jit(solution)/shard_map/ppermute | solution.py:340
  167.3 5.0 %collective-permute-start.18 = (bf16[128,2048]{1,0:T(8,128)(2,1)S(1)}, bf16[128,2048]{1,0:T(8,128)(2,1)S(1)}, u32[]{:S(2)}, u32[]{:S(2)}) collective-permute-start(bf16[128,2048]{1,0:T(8,128)(2,1)S(1)} %add_convert_fusion.5), channel_id=1, source_target_pairs={{0,8},{4,12},{8,16},{12,20},{16,24},{20,28},{1,9},{5,13},{9,17},{1... | collective-permute-start | bytes 1572872 | tf_op jit(solution)/shard_map/ppermute | solution.py:340
  172.5 3.2 %collective-permute-done.31.refs_3_ = bf16[256,2048]{1,0:T(8,128)(2,1)S(1)} collective-permute-done((bf16[256,2048]{1,0:T(8,128)(2,1)S(1)}, bf16[256,2048]{1,0:T(8,128)(2,1)S(1)}, u32[]{:S(2)}, u32[]{:S(2)}) %collective-permute-start.31) | collective-permute-done | bytes 1048608 | tf_op jit(solution)/shard_map/ppermute | solution.py:348
  175.7 1.0 copy-done.10
  177.0 6.8 %repack.1 = (bf16[320,2048]{1,0:T(8,128)(2,1)}, bf16[320,2048]{1,0:T(8,128)(2,1)}, f32[2,16,320]{2,1,0:T(8,128)}) custom-call(s32[1]{0:T(128)} %bitcast.18.plane_ref, s32[1,1024]{1,0:T(1,128)} %bitcast.64, s32[2,320]{1,0:T(2,128)} %pad_add_fusion.1.local_ref, bf16[512,2048]{1,0:T(8,128)(2,1)} %bitcast.14.refs_2_.own_d_ref, ...), custom_call_target="tpu_custom_call" | custom-call | flops 31457280 | bytes 106496 | tf_op jit(solution)/shard_map/repack/pallas_call | solution.py:107
  183.8 1.6 collective-permute-start.36
  185.4 0.9 collective-permute-start.35
  186.3 1.1 collective-permute-start.34
  187.5 1.6 collective-permute-done.36
  189.1 1.3 collective-permute-start.24
  190.4 4.6 %collective-permute-start.21 = (bf16[128,2048]{1,0:T(8,128)(2,1)S(1)}, bf16[128,2048]{1,0:T(8,128)(2,1)S(1)}, u32[]{:S(2)}, u32[]{:S(2)}) collective-permute-start(bf16[128,2048]{1,0:T(8,128)(2,1)S(1)} %add_convert_fusion.4), channel_id=1, source_target_pairs={{0,8},{4,12},{8,16},{12,20},{16,24},{20,28},{1,9},{5,13},{9,17},{1... | collective-permute-start | bytes 1572872 | tf_op jit(solution)/shard_map/ppermute | solution.py:340
  195.1 0.8 multiply_convert_fusion
  196.6 1.5 collective-permute-done.37
  198.1 1.3 collective-permute-start.27
  200.1 1.1 copy-done.7
  201.2 8.4 %adapter_gradients.1 = (f32[2048,512]{1,0:T(8,128)}, f32[512,2048]{1,0:T(8,128)}) custom-call(s32[8]{0:T(128)} %pad_add_fusion.4.order_ref, s32[1,640]{1,0:T(1,128)} %pad_add_fusion.2.local_ref, bf16[16,640]{1,0:T(8,128)(2,1)} %copy-done.19, bf16[16,640]{1,0:T(8,128)(2,1)} %pad_maximum_fusion.7.up_ranks_ref, bf16[320,2048]{1,0:T(8,128)(2,1)} %get-tuple-element.60.own_ref, ...), custom_call_target="tpu_custom_call" | custom-call | flops 41943040 | bytes 212992 | tf_op jit(solution)/shard_map/adapter_gradients/pallas_call | solution.py:294
  209.6 10.9 %collective-permute-done.27 = bf16[128,2048]{1,0:T(8,128)(2,1)S(1)} collective-permute-done((bf16[128,2048]{1,0:T(8,128)(2,1)S(1)}, bf16[128,2048]{1,0:T(8,128)(2,1)S(1)}, u32[]{:S(2)}, u32[]{:S(2)}) %collective-permute-start.27) | collective-permute-done | bytes 524320 | tf_op jit(solution)/shard_map/ppermute | solution.py:344
  220.9 1.1 pad_maximum_fusion.2
  (132 shorter events, 16.8 us)
Async XLA Ops:
  0.6 6.8 %copy-start.3 = (bf16[64,8192]{1,0:T(8,128)(2,1)S(1)}, bf16[64,8192]{1,0:T(8,128)(2,1)}, u32[]{:S(2)}) copy-start(bf16[64,8192]{1,0:T(8,128)(2,1)} %param.7) | copy-start | bytes 3145732
  2.9 8.8 %copy-start.23 = (s32[256]{0:T(256)S(1)}, s32[256]{0:T(256)}, u32[]{:S(2)}) copy-start(s32[256]{0:T(256)} %param.8) | copy-start | bytes 3076
  2.9 9.8 %copy-start.4 = (bf16[2048,512]{1,0:T(8,128)(2,1)S(1)}, bf16[2048,512]{1,0:T(8,128)(2,1)}, u32[]{:S(2)}) copy-start(bf16[2048,512]{1,0:T(8,128)(2,1)} %param.10) | copy-start | bytes 6291460
  2.9 12.2 %collective-permute-start = (bf16[64,2048]{1,0:T(8,128)(2,1)}, bf16[64,2048]{1,0:T(8,128)(2,1)}, u32[]{:S(2)}, u32[]{:S(2)}) collective-permute-start(bf16[64,2048]{1,0:T(8,128)(2,1)} %get-tuple-element.84), channel_id=1, source_target_pairs={{0,1},{1,0},{2,3},{3,2},{4,5},{5,4},{6,7},{7,6},{8,9},{9,8},{10,11... | collective-permute-start | bytes 786440 | tf_op jit(solution)/shard_map/ppermute | solution.py:354
  5.9 13.7 %collective-permute-start.1 = (bf16[64,2048]{1,0:T(8,128)(2,1)}, bf16[64,2048]{1,0:T(8,128)(2,1)}, u32[]{:S(2)}, u32[]{:S(2)}) collective-permute-start(bf16[64,2048]{1,0:T(8,128)(2,1)} %get-tuple-element.83), channel_id=1, source_target_pairs={{0,2},{1,3},{2,0},{3,1},{4,6},{5,7},{6,4},{7,5},{8,10},{9,11},{10,... | collective-permute-start | bytes 786440 | tf_op jit(solution)/shard_map/ppermute | solution.py:354
  7.4 12.2 %collective-permute-start.2 = (bf16[64,2048]{1,0:T(8,128)(2,1)}, bf16[64,2048]{1,0:T(8,128)(2,1)}, u32[]{:S(2)}, u32[]{:S(2)}) collective-permute-start(bf16[64,2048]{1,0:T(8,128)(2,1)} %get-tuple-element.82), channel_id=1, source_target_pairs={{0,3},{1,2},{2,1},{3,0},{4,7},{5,6},{6,5},{7,4},{8,11},{9,10},{10,... | collective-permute-start | bytes 786440 | tf_op jit(solution)/shard_map/ppermute | solution.py:354
  7.5 21.9 %collective-permute-start.4 = (bf16[64,2048]{1,0:T(8,128)(2,1)S(1)}, bf16[64,2048]{1,0:T(8,128)(2,1)S(1)}, u32[]{:S(2)}, u32[]{:S(2)}) collective-permute-start(bf16[64,2048]{1,0:T(8,128)(2,1)S(1)} %pad_maximum_fusion.4), channel_id=1, source_target_pairs={{0,8},{4,12},{8,16},{12,20},{16,24},{20,28},{24,0},{28,4},{1,9},{5... | collective-permute-start | bytes 786440 | tf_op jit(solution)/shard_map/ppermute | solution.py:336
  9.6 19.8 %collective-permute-start.3 = (bf16[64,2048]{1,0:T(8,128)(2,1)S(1)}, bf16[64,2048]{1,0:T(8,128)(2,1)S(1)}, u32[]{:S(2)}, u32[]{:S(2)}) collective-permute-start(bf16[64,2048]{1,0:T(8,128)(2,1)S(1)} %pad_maximum_fusion.6), channel_id=1, source_target_pairs={{0,24},{4,28},{8,0},{12,4},{16,8},{20,12},{24,16},{28,20},{1,25},{... | collective-permute-start | bytes 786440 | tf_op jit(solution)/shard_map/ppermute | solution.py:336
  15.2 25.4 %collective-permute-start.6 = (bf16[64,2048]{1,0:T(8,128)(2,1)}, bf16[64,2048]{1,0:T(8,128)(2,1)S(1)}, u32[]{:S(2)}, u32[]{:S(2)}) collective-permute-start(bf16[64,2048]{1,0:T(8,128)(2,1)} %pad_maximum_fusion.5), channel_id=1, source_target_pairs={{0,16},{4,20},{8,24},{12,28},{16,0},{20,4},{24,8},{28,12},{1,17},{... | collective-permute-start | bytes 786440 | tf_op jit(solution)/shard_map/ppermute | solution.py:336
  19.6 43.1 %collective-permute-start.8 = (bf16[512,2048]{1,0:T(8,128)(2,1)}, bf16[512,2048]{1,0:T(8,128)(2,1)}, u32[]{:S(2)}, u32[]{:S(2)}) collective-permute-start(bf16[512,2048]{1,0:T(8,128)(2,1)} %bitcast.14.refs_2_.own_d_ref), channel_id=1, source_target_pairs={{0,4},{4,0},{8,12},{12,8},{16,20},{20,16},{24,28},{28,24},{1,5},{5... | collective-permute-start | bytes 6291464 | tf_op jit(solution)/shard_map/ppermute | solution.py:351
  19.6 63.3 %collective-permute-start.9 = (bf16[2048,1024]{1,0:T(8,128)(2,1)}, bf16[2048,1024]{1,0:T(8,128)(2,1)}, u32[]{:S(2)}, u32[]{:S(2)}) collective-permute-start(bf16[2048,1024]{1,0:T(8,128)(2,1)} %own_w_ref), channel_id=1, source_target_pairs={{0,4},{4,0},{8,12},{12,8},{16,20},{20,16},{24,28},{28,24},{1,5},{5... | collective-permute-start | bytes 12582920 | tf_op jit(solution)/shard_map/ppermute | solution.py:351
  20.7 13.5 %all-to-all-start = ((s32[8,1,256]{2,1,0:T(1,128)}), s32[8,1,256]{2,1,0:T(1,128)S(1)}, u32[]{:S(2)}, u32[]{:S(2)}) async-start(s32[8,1,256]{2,1,0:T(1,128)} %broadcast_in_dim.59), calls=%async_computation | async-start | bytes 16384 | tf_op jit(solution)/shard_map/all_to_all | solution.py:381
  29.4 4.8 %copy-start.20 = (bf16[64,2048]{1,0:T(8,128)(2,1)}, bf16[64,2048]{1,0:T(8,128)(2,1)S(1)}, u32[]{:S(2)}) copy-start(bf16[64,2048]{1,0:T(8,128)(2,1)S(1)} %collective-permute-done.4) | copy-start | bytes 786436
  29.4 4.8 %copy-start.21 = (bf16[64,2048]{1,0:T(8,128)(2,1)}, bf16[64,2048]{1,0:T(8,128)(2,1)S(1)}, u32[]{:S(2)}) copy-start(bf16[64,2048]{1,0:T(8,128)(2,1)S(1)} %collective-permute-done.3) | copy-start | bytes 786436
  34.2 64.7 %all-to-all-start.1 = ((bf16[8,80,2048]{2,1,0:T(8,128)(2,1)}), bf16[8,80,2048]{2,1,0:T(8,128)(2,1)S(1)}, u32[]{:S(2)}, u32[]{:S(2)}) async-start(bf16[8,80,2048]{2,1,0:T(8,128)(2,1)} %bitcast.57), calls=%async_computation.1 | async-start | bytes 5242880 | tf_op jit(solution)/shard_map/all_to_all | solution.py:400
  39.0 19.4 %copy-start.1 = (bf16[1,2,64,2048]{3,2,1,0:T(8,128)(2,1)}, bf16[1,2,64,2048]{3,2,1,0:T(8,128)(2,1)S(1)}, u32[]{:S(2)}) copy-start(bf16[1,2,64,2048]{3,2,1,0:T(8,128)(2,1)S(1)} %maximum_bitcast_fusion.refs_0_) | copy-start | bytes 1572868
  39.0 14.3 %collective-permute-start.5 = (bf16[1,2,64,2048]{3,2,1,0:T(8,128)(2,1)S(1)}, bf16[1,2,64,2048]{3,2,1,0:T(8,128)(2,1)S(1)}, u32[]{:S(2)}, u32[]{:S(2)}) collective-permute-start(bf16[1,2,64,2048]{3,2,1,0:T(8,128)(2,1)S(1)} %maximum_bitcast_fusion.refs_0_), channel_id=1, source_target_pairs={{0,1},{1,0},{2,3},{3,2},{4,5},{5,4},{6,7},{7,6},{8,9},{9,8},{10,11... | collective-permute-start | bytes 1572872 | tf_op jit(solution)/shard_map/ppermute | solution.py:354
  40.6 17.8 %copy-start.2 = (bf16[1,2,64,2048]{3,2,1,0:T(8,128)(2,1)}, bf16[1,2,64,2048]{3,2,1,0:T(8,128)(2,1)S(1)}, u32[]{:S(2)}) copy-start(bf16[1,2,64,2048]{3,2,1,0:T(8,128)(2,1)S(1)} %maximum_bitcast_fusion.1.refs_3_) | copy-start | bytes 1572868
  40.6 14.0 %collective-permute-start.7 = (bf16[1,2,64,2048]{3,2,1,0:T(8,128)(2,1)S(1)}, bf16[1,2,64,2048]{3,2,1,0:T(8,128)(2,1)S(1)}, u32[]{:S(2)}, u32[]{:S(2)}) collective-permute-start(bf16[1,2,64,2048]{3,2,1,0:T(8,128)(2,1)S(1)} %maximum_bitcast_fusion.1.refs_3_), channel_id=1, source_target_pairs={{0,2},{1,3},{2,0},{3,1},{4,6},{5,7},{6,4},{7,5},{8,10},{9,11},{10,... | collective-permute-start | bytes 1572872 | tf_op jit(solution)/shard_map/ppermute | solution.py:354
  53.3 5.1 %copy-start.5 = (bf16[1,2,64,2048]{3,2,1,0:T(8,128)(2,1)}, bf16[1,2,64,2048]{3,2,1,0:T(8,128)(2,1)S(1)}, u32[]{:S(2)}) copy-start(bf16[1,2,64,2048]{3,2,1,0:T(8,128)(2,1)S(1)} %collective-permute-done.5.refs_1_) | copy-start | bytes 1572868
  54.6 3.8 %copy-start.6 = (bf16[1,2,64,2048]{3,2,1,0:T(8,128)(2,1)}, bf16[1,2,64,2048]{3,2,1,0:T(8,128)(2,1)S(1)}, u32[]{:S(2)}) copy-start(bf16[1,2,64,2048]{3,2,1,0:T(8,128)(2,1)S(1)} %collective-permute-done.7.refs_4_) | copy-start | bytes 1572868
  55.8 24.7 %collective-permute-start.10 = (bf16[2,2,64,2048]{3,2,1,0:T(8,128)(2,1)}, bf16[2,2,64,2048]{3,2,1,0:T(8,128)(2,1)}, u32[]{:S(2)}, u32[]{:S(2)}) collective-permute-start(bf16[2,2,64,2048]{3,2,1,0:T(8,128)(2,1)} %pad_maximum_fusion), channel_id=1, source_target_pairs={{0,2},{1,3},{2,0},{3,1},{4,6},{5,7},{6,4},{7,5},{8,10},{9,11},{10,... | collective-permute-start | bytes 3145736 | tf_op jit(solution)/shard_map/ppermute | solution.py:354
  58.4 24.5 %collective-permute-start.11 = (bf16[2,2,64,2048]{3,2,1,0:T(8,128)(2,1)}, bf16[2,2,64,2048]{3,2,1,0:T(8,128)(2,1)}, u32[]{:S(2)}, u32[]{:S(2)}) collective-permute-start(bf16[2,2,64,2048]{3,2,1,0:T(8,128)(2,1)} %pad_maximum_fusion.1), channel_id=1, source_target_pairs={{0,1},{1,0},{2,3},{3,2},{4,5},{5,4},{6,7},{7,6},{8,9},{9,8},{10,11... | collective-permute-start | bytes 3145736 | tf_op jit(solution)/shard_map/ppermute | solution.py:354
  61.4 60.5 %collective-permute-start.28 = (bf16[256,2048]{1,0:T(8,128)(2,1)}, bf16[256,2048]{1,0:T(8,128)(2,1)}, u32[]{:S(2)}, u32[]{:S(2)}) collective-permute-start(bf16[256,2048]{1,0:T(8,128)(2,1)} %refs_0_.1), channel_id=1, source_target_pairs={{8,0},{12,4},{16,8},{20,12},{24,16},{28,20},{9,1},{13,5},{17,9},{2... | collective-permute-start | bytes 3145736 | tf_op jit(solution)/shard_map/ppermute | solution.py:348
  62.7 59.2 %collective-permute-start.29 = (bf16[256,2048]{1,0:T(8,128)(2,1)}, bf16[256,2048]{1,0:T(8,128)(2,1)}, u32[]{:S(2)}, u32[]{:S(2)}) collective-permute-start(bf16[256,2048]{1,0:T(8,128)(2,1)} %refs_0_.1), channel_id=1, source_target_pairs={{0,8},{4,12},{8,16},{12,20},{16,24},{20,28},{1,9},{5,13},{9,17},{1... | collective-permute-start | bytes 3145736 | tf_op jit(solution)/shard_map/ppermute | solution.py:348
  98.9 1.5 copy-start
  106.0 5.3 %collective-permute-start.14 = (f32[16,640]{1,0:T(8,128)}, f32[16,640]{1,0:T(8,128)S(1)}, u32[]{:S(2)}, u32[]{:S(2)}) collective-permute-start(f32[16,640]{1,0:T(8,128)} %token_ranks.1), channel_id=1, source_target_pairs={{0,3},{1,2},{2,1},{3,0},{4,7},{5,6},{6,5},{7,4},{8,11},{9,10},{10,... | collective-permute-start | bytes 122888 | tf_op jit(solution)/shard_map/ppermute | solution.py:354
  108.1 4.2 %collective-permute-start.13 = (f32[16,640]{1,0:T(8,128)}, f32[16,640]{1,0:T(8,128)S(1)}, u32[]{:S(2)}, u32[]{:S(2)}) collective-permute-start(f32[16,640]{1,0:T(8,128)} %token_ranks.1), channel_id=1, source_target_pairs={{0,2},{1,3},{2,0},{3,1},{4,6},{5,7},{6,4},{7,5},{8,10},{9,11},{10,... | collective-permute-start | bytes 122888 | tf_op jit(solution)/shard_map/ppermute | solution.py:354
  108.6 4.2 %collective-permute-start.12 = (f32[16,640]{1,0:T(8,128)}, f32[16,640]{1,0:T(8,128)S(1)}, u32[]{:S(2)}, u32[]{:S(2)}) collective-permute-start(f32[16,640]{1,0:T(8,128)} %token_ranks.1), channel_id=1, source_target_pairs={{0,1},{1,0},{2,3},{3,2},{4,5},{5,4},{6,7},{7,6},{8,9},{9,8},{10,11... | collective-permute-start | bytes 122888 | tf_op jit(solution)/shard_map/ppermute | solution.py:354
  113.6 1.3 copy-start.19
  113.6 1.3 collective-permute-start.15
  121.9 17.0 %copy-start.14 = (bf16[128,2048]{1,0:T(8,128)(2,1)S(1)}, bf16[128,2048]{1,0:T(8,128)(2,1)}, u32[]{:S(2)}) copy-start(bf16[128,2048]{1,0:T(8,128)(2,1)} %get-tuple-element.53) | copy-start | bytes 1572868
  121.9 28.6 %collective-permute-start.30 = (bf16[256,2048]{1,0:T(8,128)(2,1)}, bf16[256,2048]{1,0:T(8,128)(2,1)S(1)}, u32[]{:S(2)}, u32[]{:S(2)}) collective-permute-start(bf16[256,2048]{1,0:T(8,128)(2,1)} %collective-permute-done.28.refs_1_), channel_id=1, source_target_pairs={{8,0},{12,4},{16,8},{20,12},{9,1},{13,5},{17,9},{21,13},{10,2},{14... | collective-permute-start | bytes 3145736 | tf_op jit(solution)/shard_map/ppermute | solution.py:348
  123.3 28.5 %collective-permute-start.32 = (bf16[256,2048]{1,0:T(8,128)(2,1)}, bf16[256,2048]{1,0:T(8,128)(2,1)S(1)}, u32[]{:S(2)}, u32[]{:S(2)}) collective-permute-start(bf16[256,2048]{1,0:T(8,128)(2,1)} %collective-permute-done.29.refs_4_), channel_id=1, source_target_pairs={{8,16},{12,20},{16,24},{20,28},{9,17},{13,21},{17,25},{21,29},{10,... | collective-permute-start | bytes 3145736 | tf_op jit(solution)/shard_map/ppermute | solution.py:348
  124.1 14.8 %collective-permute-start.22 = (bf16[128,2048]{1,0:T(8,128)(2,1)}, bf16[128,2048]{1,0:T(8,128)(2,1)S(1)}, u32[]{:S(2)}, u32[]{:S(2)}) collective-permute-start(bf16[128,2048]{1,0:T(8,128)(2,1)} %get-tuple-element.48), channel_id=1, source_target_pairs={{24,16},{28,20},{25,17},{29,21},{26,18},{30,22},{27,19},{31,23}} | collective-permute-start | bytes 1572872 | tf_op jit(solution)/shard_map/ppermute | solution.py:344
  124.8 19.3 %collective-permute-start.16 = (bf16[128,2048]{1,0:T(8,128)(2,1)}, bf16[128,2048]{1,0:T(8,128)(2,1)S(1)}, u32[]{:S(2)}, u32[]{:S(2)}) collective-permute-start(bf16[128,2048]{1,0:T(8,128)(2,1)} %get-tuple-element.50), channel_id=1, source_target_pairs={{0,8},{4,12},{1,9},{5,13},{2,10},{6,14},{3,11},{7,15}} | collective-permute-start | bytes 1572872 | tf_op jit(solution)/shard_map/ppermute | solution.py:340
  131.5 18.4 %collective-permute-start.25 = (bf16[128,2048]{1,0:T(8,128)(2,1)}, bf16[128,2048]{1,0:T(8,128)(2,1)S(1)}, u32[]{:S(2)}, u32[]{:S(2)}) collective-permute-start(bf16[128,2048]{1,0:T(8,128)(2,1)} %get-tuple-element.51), channel_id=1, source_target_pairs={{24,16},{28,20},{25,17},{29,21},{26,18},{30,22},{27,19},{31,23}} | collective-permute-start | bytes 1572872 | tf_op jit(solution)/shard_map/ppermute | solution.py:344
  138.9 16.3 %copy-start.18 = (bf16[128,2048]{1,0:T(8,128)(2,1)S(1)}, bf16[128,2048]{1,0:T(8,128)(2,1)}, u32[]{:S(2)}) copy-start(bf16[128,2048]{1,0:T(8,128)(2,1)} %get-tuple-element.52) | copy-start | bytes 1572868
  138.9 16.3 %collective-permute-start.19 = (bf16[128,2048]{1,0:T(8,128)(2,1)S(1)}, bf16[128,2048]{1,0:T(8,128)(2,1)S(1)}, u32[]{:S(2)}, u32[]{:S(2)}) collective-permute-start(bf16[128,2048]{1,0:T(8,128)(2,1)S(1)} %copy-done.14), channel_id=1, source_target_pairs={{0,8},{4,12},{1,9},{5,13},{2,10},{6,14},{3,11},{7,15}} | collective-permute-start | bytes 1572872 | tf_op jit(solution)/shard_map/ppermute | solution.py:340
  144.1 23.1 %copy-start.17 = (bf16[128,2048]{1,0:T(8,128)(2,1)S(1)}, bf16[128,2048]{1,0:T(8,128)(2,1)}, u32[]{:S(2)}) copy-start(bf16[128,2048]{1,0:T(8,128)(2,1)} %get-tuple-element.48) | copy-start | bytes 1572868
  145.5 21.0 %collective-permute-start.17 = (bf16[128,2048]{1,0:T(8,128)(2,1)S(1)}, bf16[128,2048]{1,0:T(8,128)(2,1)S(1)}, u32[]{:S(2)}, u32[]{:S(2)}) collective-permute-start(bf16[128,2048]{1,0:T(8,128)(2,1)S(1)} %get-tuple-element.89), channel_id=1, source_target_pairs={{0,8},{4,12},{8,16},{12,20},{1,9},{5,13},{9,17},{13,21},{2,10},{6,... | collective-permute-start | bytes 1572872 | tf_op jit(solution)/shard_map/ppermute | solution.py:340
  149.8 17.5 %collective-permute-start.23 = (bf16[128,2048]{1,0:T(8,128)(2,1)S(1)}, bf16[128,2048]{1,0:T(8,128)(2,1)S(1)}, u32[]{:S(2)}, u32[]{:S(2)}) collective-permute-start(bf16[128,2048]{1,0:T(8,128)(2,1)S(1)} %get-tuple-element.88), channel_id=1, source_target_pairs={{16,8},{20,12},{24,16},{28,20},{17,9},{21,13},{25,17},{29,21},{18,... | collective-permute-start | bytes 1572872 | tf_op jit(solution)/shard_map/ppermute | solution.py:344
  150.5 16.7 %copy-start.8 = (bf16[256,2048]{1,0:T(8,128)(2,1)}, bf16[256,2048]{1,0:T(8,128)(2,1)S(1)}, u32[]{:S(2)}) copy-start(bf16[256,2048]{1,0:T(8,128)(2,1)S(1)} %collective-permute-done.30.refs_2_) | copy-start | bytes 3145732
  150.6 25.1 %collective-permute-start.31 = (bf16[256,2048]{1,0:T(8,128)(2,1)S(1)}, bf16[256,2048]{1,0:T(8,128)(2,1)S(1)}, u32[]{:S(2)}, u32[]{:S(2)}) collective-permute-start(bf16[256,2048]{1,0:T(8,128)(2,1)S(1)} %collective-permute-done.30.refs_2_), channel_id=1, source_target_pairs={{8,0},{12,4},{9,1},{13,5},{10,2},{14,6},{11,3},{15,7}} | collective-permute-start | bytes 3145736 | tf_op jit(solution)/shard_map/ppermute | solution.py:348
  151.9 15.4 %copy-start.9 = (bf16[256,2048]{1,0:T(8,128)(2,1)}, bf16[256,2048]{1,0:T(8,128)(2,1)S(1)}, u32[]{:S(2)}) copy-start(bf16[256,2048]{1,0:T(8,128)(2,1)S(1)} %collective-permute-done.32.refs_5_) | copy-start | bytes 3145732
  151.9 23.8 %collective-permute-start.33 = (bf16[256,2048]{1,0:T(8,128)(2,1)S(1)}, bf16[256,2048]{1,0:T(8,128)(2,1)S(1)}, u32[]{:S(2)}, u32[]{:S(2)}) collective-permute-start(bf16[256,2048]{1,0:T(8,128)(2,1)S(1)} %collective-permute-done.32.refs_5_), channel_id=1, source_target_pairs={{16,24},{20,28},{17,25},{21,29},{18,26},{22,30},{19,27},{23,31}} | collective-permute-start | bytes 3145736 | tf_op jit(solution)/shard_map/ppermute | solution.py:348
  155.2 17.1 %copy-start.16 = (bf16[128,2048]{1,0:T(8,128)(2,1)S(1)}, bf16[128,2048]{1,0:T(8,128)(2,1)}, u32[]{:S(2)}) copy-start(bf16[128,2048]{1,0:T(8,128)(2,1)} %get-tuple-element.50) | copy-start | bytes 1572868
  156.4 29.9 %collective-permute-start.20 = (bf16[128,2048]{1,0:T(8,128)(2,1)}, bf16[128,2048]{1,0:T(8,128)(2,1)S(1)}, u32[]{:S(2)}, u32[]{:S(2)}) collective-permute-start(bf16[128,2048]{1,0:T(8,128)(2,1)} %get-tuple-element.87), channel_id=1, source_target_pairs={{0,8},{4,12},{8,16},{12,20},{1,9},{5,13},{9,17},{13,21},{2,10},{6,... | collective-permute-start | bytes 1572872 | tf_op jit(solution)/shard_map/ppermute | solution.py:340
  166.5 29.5 %collective-permute-start.26 = (bf16[128,2048]{1,0:T(8,128)(2,1)S(1)}, bf16[128,2048]{1,0:T(8,128)(2,1)S(1)}, u32[]{:S(2)}, u32[]{:S(2)}) collective-permute-start(bf16[128,2048]{1,0:T(8,128)(2,1)S(1)} %get-tuple-element.86), channel_id=1, source_target_pairs={{16,8},{20,12},{24,16},{28,20},{17,9},{21,13},{25,17},{29,21},{18,... | collective-permute-start | bytes 1572872 | tf_op jit(solution)/shard_map/ppermute | solution.py:344
  167.3 42.3 %collective-permute-start.18 = (bf16[128,2048]{1,0:T(8,128)(2,1)S(1)}, bf16[128,2048]{1,0:T(8,128)(2,1)S(1)}, u32[]{:S(2)}, u32[]{:S(2)}) collective-permute-start(bf16[128,2048]{1,0:T(8,128)(2,1)S(1)} %add_convert_fusion.5), channel_id=1, source_target_pairs={{0,8},{4,12},{8,16},{12,20},{16,24},{20,28},{1,9},{5,13},{9,17},{1... | collective-permute-start | bytes 1572872 | tf_op jit(solution)/shard_map/ppermute | solution.py:340
  175.7 1.0 copy-start.10
  175.7 1.3 copy-start.11
  177.0 10.4 %copy-start.15 = (bf16[128,2048]{1,0:T(8,128)(2,1)S(1)}, bf16[128,2048]{1,0:T(8,128)(2,1)}, u32[]{:S(2)}) copy-start(bf16[128,2048]{1,0:T(8,128)(2,1)} %get-tuple-element.51) | copy-start | bytes 1572868
  183.8 5.3 %collective-permute-start.36 = (f32[2,16,320]{2,1,0:T(8,128)}, f32[2,16,320]{2,1,0:T(8,128)S(1)}, u32[]{:S(2)}, u32[]{:S(2)}) collective-permute-start(f32[2,16,320]{2,1,0:T(8,128)} %get-tuple-element.59), channel_id=1, source_target_pairs={{0,3},{1,2},{2,1},{3,0},{4,7},{5,6},{6,5},{7,4},{8,11},{9,10},{10,... | collective-permute-start | bytes 122888 | tf_op jit(solution)/shard_map/ppermute | solution.py:354
  185.4 5.0 %collective-permute-start.35 = (f32[2,16,320]{2,1,0:T(8,128)}, f32[2,16,320]{2,1,0:T(8,128)S(1)}, u32[]{:S(2)}, u32[]{:S(2)}) collective-permute-start(f32[2,16,320]{2,1,0:T(8,128)} %get-tuple-element.59), channel_id=1, source_target_pairs={{0,2},{1,3},{2,0},{3,1},{4,6},{5,7},{6,4},{7,5},{8,10},{9,11},{10,... | collective-permute-start | bytes 122888 | tf_op jit(solution)/shard_map/ppermute | solution.py:354
  186.3 8.7 %collective-permute-start.34 = (f32[2,16,320]{2,1,0:T(8,128)}, f32[2,16,320]{2,1,0:T(8,128)S(1)}, u32[]{:S(2)}, u32[]{:S(2)}) collective-permute-start(f32[2,16,320]{2,1,0:T(8,128)} %get-tuple-element.59), channel_id=1, source_target_pairs={{0,1},{1,0},{2,3},{3,2},{4,5},{5,4},{6,7},{7,6},{8,9},{9,8},{10,11... | collective-permute-start | bytes 122888 | tf_op jit(solution)/shard_map/ppermute | solution.py:354
  189.1 20.5 %collective-permute-start.24 = (bf16[128,2048]{1,0:T(8,128)(2,1)S(1)}, bf16[128,2048]{1,0:T(8,128)(2,1)S(1)}, u32[]{:S(2)}, u32[]{:S(2)}) collective-permute-start(bf16[128,2048]{1,0:T(8,128)(2,1)S(1)} %add_convert_fusion.3), channel_id=1, source_target_pairs={{8,0},{12,4},{16,8},{20,12},{24,16},{28,20},{9,1},{13,5},{17,9},{2... | collective-permute-start | bytes 1572872 | tf_op jit(solution)/shard_map/ppermute | solution.py:344
  190.4 19.2 %collective-permute-start.21 = (bf16[128,2048]{1,0:T(8,128)(2,1)S(1)}, bf16[128,2048]{1,0:T(8,128)(2,1)S(1)}, u32[]{:S(2)}, u32[]{:S(2)}) collective-permute-start(bf16[128,2048]{1,0:T(8,128)(2,1)S(1)} %add_convert_fusion.4), channel_id=1, source_target_pairs={{0,8},{4,12},{8,16},{12,20},{16,24},{20,28},{1,9},{5,13},{9,17},{1... | collective-permute-start | bytes 1572872 | tf_op jit(solution)/shard_map/ppermute | solution.py:340
  195.0 5.1 %collective-permute-start.38 = (bf16[320,2048]{1,0:T(8,128)(2,1)}, bf16[320,2048]{1,0:T(8,128)(2,1)S(1)}, u32[]{:S(2)}, u32[]{:S(2)}) collective-permute-start(bf16[320,2048]{1,0:T(8,128)(2,1)} %get-tuple-element.61), channel_id=1, source_target_pairs={{0,4},{4,0},{8,12},{12,8},{16,20},{20,16},{24,28},{28,24},{1,5},{5... | collective-permute-start | bytes 3932168 | tf_op jit(solution)/shard_map/ppermute | solution.py:351
  195.9 2.2 collective-permute-start.37
  198.1 22.4 %collective-permute-start.27 = (bf16[128,2048]{1,0:T(8,128)(2,1)S(1)}, bf16[128,2048]{1,0:T(8,128)(2,1)S(1)}, u32[]{:S(2)}, u32[]{:S(2)}) collective-permute-start(bf16[128,2048]{1,0:T(8,128)(2,1)S(1)} %add_convert_fusion.2), channel_id=1, source_target_pairs={{8,0},{12,4},{16,8},{20,12},{24,16},{28,20},{9,1},{13,5},{17,9},{2... | collective-permute-start | bytes 1572872 | tf_op jit(solution)/shard_map/ppermute | solution.py:344
  200.1 1.1 copy-start.7
  201.2 19.3 %copy-start.13 = (f32[128,2048]{1,0:T(8,128)S(1)}, f32[128,2048]{1,0:T(8,128)}, u32[]{:S(2)}) copy-start(f32[128,2048]{1,0:T(8,128)} %get-tuple-element.65) | copy-start | bytes 3145732
  209.6 11.1 %copy-start.12 = (f32[128,2048]{1,0:T(8,128)S(1)}, f32[128,2048]{1,0:T(8,128)}, u32[]{:S(2)}) copy-start(f32[128,2048]{1,0:T(8,128)} %get-tuple-element.47) | copy-start | bytes 3145732
  (1 other events, 0.6 us)
